TPU v7x, 256 devices: a whole 4x4x8 slice. The times are simulated.
256 devices in a mesh: tm: 128 (over x, y, z), chan: 2 (over core).
Axes of the slice: x: 4, y: 4, z: 8, core: 2. Of those that a mesh axis runs over, the one named last changes fastest.
Arguments:
- record: float32 [2048, 32768], P('chan', 'tm'), may hold values from -90 to 90
- gauge_table: float32 [6, 8], replicated, may hold values from 0.7 to 1.4
- gauge_index: int32 [6, 32], replicated, may hold values from 0 to 7
Outputs:
- denoised: float32 [2048, 32768], P('chan', 'tm')
Inputs may be any that keep to these rules, and one draw needn't show every extreme that they name: gauge_index[l, b] picks the entry of gauge_table[l] for channel block b at level l.
All inputs are finite; a program needn't handle non-finite values.
Results may differ from a plain program's by a relative error of at most 0.0001.
Values sent between devices are 32-bit elements; how exact they have to be, the bound alone decides.
No kernel may reach another device: no remote copies, remote signals or barrier semaphores. Data moves between devices by JAX's collectives and lax.ppermute only.
A program may use at most 64 MiB of HBM per device.

v0:
```python
import jax
import jax.numpy as jnp
from jax import lax
from jax.sharding import PartitionSpec as P

LEVELS = 6
COARSE = 6
GTAB = 8


lift_predict_one = -1.586134342059924
lift_update_one = -0.052980118572961
lift_predict_two = 0.882911075530934
lift_update_two = 0.443506852043971
lift_scale = 1.149604398860241
noise_floor = 1e-06


def with_halo(block, sides, width):
    for axis, dim in sides:
        count = lax.axis_size(axis)
        forward = [(i, i + 1) for i in range(count - 1)]
        backward = [(target, source) for source, target in forward]
        low = lax.ppermute(
            lax.slice_in_dim(block, block.shape[dim] - width, None, axis=dim), axis, forward
        )
        high = lax.ppermute(lax.slice_in_dim(block, 0, width, axis=dim), axis, backward)
        block = jnp.concatenate([low, block, high], axis=dim)
    return block


def shifted(values, direction, forward, keep_mask):
    length = values.shape[direction]
    if forward:
        moved_values = jnp.concatenate(
            (
                lax.slice_in_dim(values, 1, length, axis=direction),
                lax.slice_in_dim(values, length - 1, length, axis=direction),
            ),
            axis=direction,
        )
    else:
        moved_values = jnp.concatenate(
            (
                lax.slice_in_dim(values, 0, 1, axis=direction),
                lax.slice_in_dim(values, 0, length - 1, axis=direction),
            ),
            axis=direction,
        )
    return jnp.where(keep_mask, values, moved_values)


def edge_masks(length, direction, low_edge, high_edge):
    extent_shape = (length, 1) if direction == 0 else (1, length)
    positions = lax.broadcasted_iota(jnp.int32, extent_shape, direction)
    return (
        jnp.logical_and(low_edge, positions == 2),
        jnp.logical_and(high_edge, positions == length - 3),
    )


def center(values, direction):
    length = values.shape[direction]
    return lax.slice_in_dim(values, 2, length - 2, axis=direction)


def lift_forward(even_part, odd_part, weights, direction, low_edge, high_edge):
    low_mask, high_mask = edge_masks(even_part.shape[direction], direction, low_edge, high_edge)
    odd_part = odd_part + lift_predict_one * weights * (
        even_part + shifted(even_part, direction, True, high_mask)
    )
    even_part = even_part + lift_update_one * weights * (
        shifted(odd_part, direction, False, low_mask) + odd_part
    )
    odd_part = odd_part + lift_predict_two * weights * (
        even_part + shifted(even_part, direction, True, high_mask)
    )
    even_part = even_part + lift_update_two * weights * (
        shifted(odd_part, direction, False, low_mask) + odd_part
    )
    return (lift_scale * center(even_part, direction), center(odd_part, direction) / lift_scale)


def lift_inverse(low_band, high_band, weights, direction, low_edge, high_edge):
    low_mask, high_mask = edge_masks(low_band.shape[direction], direction, low_edge, high_edge)
    even_part = low_band / lift_scale
    odd_part = high_band * lift_scale
    even_part = even_part - lift_update_two * weights * (
        shifted(odd_part, direction, False, low_mask) + odd_part
    )
    odd_part = odd_part - lift_predict_two * weights * (
        even_part + shifted(even_part, direction, True, high_mask)
    )
    even_part = even_part - lift_update_one * weights * (
        shifted(odd_part, direction, False, low_mask) + odd_part
    )
    odd_part = odd_part - lift_predict_one * weights * (
        even_part + shifted(even_part, direction, True, high_mask)
    )
    return (center(even_part, direction), center(odd_part, direction))


def alternate(even_part, odd_part, direction):
    if direction == 0:
        return jnp.stack((even_part, odd_part), axis=1).reshape(
            2 * even_part.shape[0], even_part.shape[1]
        )
    return jnp.stack((even_part, odd_part), axis=2).reshape(
        even_part.shape[0], 2 * even_part.shape[1]
    )


def pad_pairs(values, direction):
    widths = ((2, 2), (0, 0)) if direction == 0 else ((0, 0), (2, 2))
    return jnp.pad(values, widths)


def split_pairs(values, direction):
    if direction == 0:
        return (values[0::2, :], values[1::2, :])
    return (values[:, 0::2], values[:, 1::2])


def full_forward(values, weights, direction):
    even_part, odd_part = split_pairs(values, direction)
    return lift_forward(
        pad_pairs(even_part, direction),
        pad_pairs(odd_part, direction),
        weights,
        direction,
        True,
        True,
    )


def full_inverse(low_band, high_band, weights, direction):
    even_part, odd_part = lift_inverse(
        pad_pairs(low_band, direction),
        pad_pairs(high_band, direction),
        weights,
        direction,
        True,
        True,
    )
    return alternate(even_part, odd_part, direction)


def level_weights(block_weights, level_index):
    pair_weights = jnp.repeat(block_weights[level_index], 2 ** (LEVELS - 1 - level_index))
    return jnp.pad(pair_weights, 2, mode="edge")


def shrink(band_values, limit_value):
    return band_values - jnp.clip(band_values, -limit_value, limit_value)


def squares(band_values):
    return jnp.sum(band_values * band_values)


def rim_edges(values, direction, width):
    length = values.shape[direction]
    return jnp.concatenate(
        (
            lax.slice_in_dim(values, 0, width, axis=direction),
            lax.slice_in_dim(values, length - width, length, axis=direction),
        ),
        axis=direction,
    )


def attach_rims(extended, values, direction, width):
    length = extended.shape[direction]
    lower_part = lax.slice_in_dim(extended, 0, width, axis=direction)
    upper_part = lax.slice_in_dim(extended, length - width, length, axis=direction)
    return jnp.concatenate((lower_part, values, upper_part), axis=direction)


def channel_forward(combined, weights):
    gathered = lax.all_to_all(combined, "chan", split_axis=1, concat_axis=0, tiled=True)
    chan_low, chan_high = full_forward(gathered, weights[:, None], 0)
    return (
        lax.all_to_all(chan_low, "chan", split_axis=0, concat_axis=1, tiled=True),
        lax.all_to_all(chan_high, "chan", split_axis=0, concat_axis=1, tiled=True),
    )


def channel_inverse(chan_low, chan_high, weights):
    low_full, high_full = (
        lax.all_to_all(chan_low, "chan", split_axis=1, concat_axis=0, tiled=True),
        lax.all_to_all(chan_high, "chan", split_axis=1, concat_axis=0, tiled=True),
    )
    combined = full_inverse(low_full, high_full, weights[:, None], 0)
    return lax.all_to_all(combined, "chan", split_axis=0, concat_axis=1, tiled=True)


def shards(record, gauge_table, gauge_index):
    matches = (gauge_index[:, :, None] == jnp.arange(GTAB, dtype=jnp.int32)[None, None, :]).astype(
        jnp.float32
    )
    block_weights = jnp.sum(matches * gauge_table[:, None, :], axis=2)
    time_place = lax.axis_index("tm")
    time_count = lax.axis_size("tm")
    chan_count = lax.axis_size("chan")
    time_low_edge = time_place == 0
    time_high_edge = time_place == time_count - 1
    current = record
    details = []
    level_sums = []
    for level_index in range(LEVELS):
        extended = with_halo(rim_edges(current, 1, 4), (("tm", 1),), 4)
        widened = attach_rims(extended, current, 1, 4)
        time_low, time_high = lift_forward(
            widened[:, 0::2], widened[:, 1::2], 1.0, 1, time_low_edge, time_high_edge
        )
        half_width = time_low.shape[1]
        combined = jnp.concatenate((time_low, time_high), axis=1)
        weights = level_weights(block_weights, level_index)
        chan_low, chan_high = channel_forward(combined, weights)
        level_bands = (
            chan_low[:, half_width:],
            chan_high[:, :half_width],
            chan_high[:, half_width:],
        )
        details.append(level_bands)
        local_sum = squares(level_bands[0]) + squares(level_bands[1]) + squares(level_bands[2])
        level_sums.append(lax.psum(local_sum, ("tm", "chan")))
        current = chan_low[:, :half_width]
    own_width = current.shape[1]
    current = lax.all_gather(current, "tm", axis=1, tiled=True)
    coarse_highs = []
    coarse_local = jnp.zeros((), jnp.float32)
    coarse_count = 0
    for coarse_step in range(COARSE):
        current, high_band = full_forward(current, 1.0, 1)
        coarse_highs.append(high_band)
        coarse_local = coarse_local + squares(high_band)
        coarse_count = coarse_count + high_band.size * chan_count
    coarse_total = lax.psum(coarse_local, "chan")
    coarse_limit = jnp.sqrt(coarse_total / coarse_count + noise_floor)
    for coarse_step in reversed(range(COARSE)):
        current = full_inverse(current, shrink(coarse_highs[coarse_step], coarse_limit), 1.0, 1)
    current = lax.dynamic_slice_in_dim(current, time_place * own_width, own_width, 1)
    for level_index in reversed(range(LEVELS)):
        level_bands = details[level_index]
        global_count = 3 * level_bands[0].size * time_count * chan_count
        level_limit = jnp.sqrt(level_sums[level_index] / global_count + noise_floor)
        time_detail = shrink(level_bands[0], level_limit)
        channel_detail = shrink(level_bands[1], level_limit)
        both_detail = shrink(level_bands[2], level_limit)
        half_width = current.shape[1]
        chan_low = jnp.concatenate((current, time_detail), axis=1)
        chan_high = jnp.concatenate((channel_detail, both_detail), axis=1)
        weights = level_weights(block_weights, level_index)
        combined = channel_inverse(chan_low, chan_high, weights)
        row_count = combined.shape[0]
        stacked = jnp.concatenate((combined[:, :half_width], combined[:, half_width:]), axis=0)
        extended = with_halo(rim_edges(stacked, 1, 2), (("tm", 1),), 2)
        widened = attach_rims(extended, stacked, 1, 2)
        even_part, odd_part = lift_inverse(
            widened[:row_count], widened[row_count:], 1.0, 1, time_low_edge, time_high_edge
        )
        current = alternate(even_part, odd_part, 1)
    return current


def solution(mesh):
    return jax.shard_map(
        shards,
        mesh=mesh,
        in_specs=(P("chan", "tm"), P(), P()),
        out_specs=P("chan", "tm"),
        check_vma=False,
    )
```

profile of v0, /device:TPU:1, one launch (start us, length us, event | category | flops | bytes accessed | tf_op | source)
XLA Modules:
  0.0 828.3 jit_solution(6529678220151501434)
XLA Ops:
  1.5 4.4 collective-permute-start
  24.4 20.5 %slice.1504 = f32[1024,132]{1,0:T(8,128)S(1)} slice(f32[1024,264]{1,0:T(8,128)S(1)} %pad_maximum_fusion.1), slice={[0:1024:1], [0:264:2]} | slice | bytes 1081344 | tf_op jit(solution)/shard_map/slice | solution.py:214
  46.5 21.0 %slice.1505 = f32[1024,132]{1,0:T(8,128)} slice(f32[1024,264]{1,0:T(8,128)S(1)} %pad_maximum_fusion.1), slice={[0:1024:1], [1:264:2]} | slice | bytes 1081344 | tf_op jit(solution)/shard_map/slice | solution.py:214
  71.4 5.2 all_to_all.669
  79.5 4.2 all_to_all.670
  84.5 4.3 collective-permute-start.2
  90.1 4.4 all_to_all.671
  98.4 4.4 all_to_all.672
  102.8 4.5 slice.1546
  107.3 4.5 slice.1552
  112.8 3.8 all_to_all.673
  117.3 4.3 collective-permute-start.4
  122.8 4.1 all_to_all.674
  130.0 3.8 all_to_all.675
  136.8 3.7 all_to_all.676
  141.2 5.2 collective-permute-start.6
  147.6 4.0 all_to_all.677
  154.7 3.7 all_to_all.678
  159.8 3.7 all_to_all.679
  165.4 5.5 collective-permute-start.8
  172.4 4.0 all_to_all.680
  180.2 3.7 all_to_all.681
  185.8 3.7 all_to_all.682
  190.9 5.5 collective-permute-start.10
  197.8 3.9 all_to_all.683
  205.6 3.7 all_to_all.684
  215.5 3.7 all_to_all.686
  221.8 98.5 %all-reduce.60 = (f32[]{:T(128)}, f32[]{:T(128)}, f32[]{:T(128)}, f32[]{:T(128)}, f32[]{:T(128)}, /*index=5*/f32[]{:T(128)}) all-reduce(f32[]{:T(128)S(6)} %add.1088, f32[]{:T(128)S(6)} %add.1077, f32[]{:T(128)S(6)} %add.1066, f32[]{:T(128)S(6)} %add.1055, f32[]{:T(128)S(6)} %add.1044, ...), channel_id=1, replica_groups=mesh['tm'=128,'chan'=2] {'tm','chan'}, use_global_device_ids=true, to_apply=%region_31.32 | all-reduce | flops 6 | bytes 48 | tf_op jit(solution)/shard_map/psum | solution.py:227
  320.9 287.4 %all-gather = f32[128,4,16]{2,1,0:T(4,128)S(1)} all-gather(f32[1,4,16]{2,1,0:T(4,128)S(1)} %get-tuple-element.145), channel_id=1, replica_groups=mesh['tm'=128,'chan'=2] {'tm'}, dimensions={0}, use_global_device_ids=true | all-gather | bytes 33024 | tf_op jit(solution)/shard_map/all_gather | solution.py:230
  622.3 58.1 %psum.49 = f32[]{:T(128)} all-reduce(f32[]{:T(128)S(6)} %add.1005), channel_id=1, replica_groups=mesh['tm'=128,'chan'=2] {'chan'}, use_global_device_ids=true, to_apply=%region_7.8 | all-reduce | flops 1 | bytes 8 | tf_op jit(solution)/shard_map/psum | solution.py:239
  687.0 3.7 all_to_all.687
  690.8 3.7 all_to_all.688
  698.5 3.7 all_to_all.689
  710.3 3.7 all_to_all.691
  716.3 3.8 all-to-all-start.34
  727.0 3.7 all_to_all.692
  732.5 3.7 all_to_all.693
  737.0 4.3 collective-permute-start.14
  746.2 5.1 all_to_all.694
  753.0 3.7 all_to_all.695
  759.8 4.1 all_to_all.696
  764.4 4.0 all_to_all.697
  769.3 3.8 all_to_all.698
  773.1 4.1 collective-permute-start.18
  782.1 5.3 all_to_all.699
  788.8 3.9 all_to_all.700
  799.9 5.8 all_to_all.701
  808.3 4.6 all_to_all.702
  (767 shorter events, 140.2 us)
Async XLA Ops:
  0.0 22.8 %copy-start = (f32[1024,256]{1,0:T(8,128)S(1)}, f32[1024,256]{1,0:T(8,128)}, u32[]{:S(2)}) copy-start(f32[1024,256]{1,0:T(8,128)} %param.3) | copy-start | bytes 3145732
  0.0 7.5 copy-start.1
  0.0 7.5 copy-start.2
  1.5 21.3 %collective-permute-start = (f32[1024,4]{1,0:T(8,128)S(1)}, f32[1024,4]{1,0:T(8,128)S(1)}, u32[]{:S(2)}, u32[]{:S(2)}) collective-permute-start(f32[1024,4]{1,0:T(8,128)S(1)} %get-tuple-element.35), channel_id=1, source_target_pairs={{0,2},{2,4},{4,6},{6,8},{8,10},{10,12},{12,14},{14,16},{16,18},{18... | collective-permute-start | bytes 49160 | tf_op jit(solution)/shard_map/ppermute | solution.py:24
  5.9 16.9 %collective-permute-start.1 = (f32[1024,4]{1,0:T(8,128)S(1)}, f32[1024,4]{1,0:T(8,128)}, u32[]{:S(2)}, u32[]{:S(2)}) collective-permute-start(f32[1024,4]{1,0:T(8,128)S(1)} %get-tuple-element.36), channel_id=1, source_target_pairs={{2,0},{4,2},{6,4},{8,6},{10,8},{12,10},{14,12},{16,14},{18,16},{20... | collective-permute-start | bytes 49160 | tf_op jit(solution)/shard_map/ppermute | solution.py:27
  84.5 12.9 %collective-permute-start.2 = (f32[512,4]{0,1:T(4,128)S(1)}, f32[512,4]{0,1:T(4,128)S(1)}, u32[]{:S(2)}, u32[]{:S(2)}) collective-permute-start(f32[512,4]{0,1:T(4,128)S(1)} %get-tuple-element.43), channel_id=1, source_target_pairs={{0,2},{2,4},{4,6},{6,8},{8,10},{10,12},{12,14},{14,16},{16,18},{18... | collective-permute-start | bytes 24584 | tf_op jit(solution)/shard_map/ppermute | solution.py:24
  88.8 8.6 %collective-permute-start.3 = (f32[512,4]{0,1:T(4,128)S(1)}, f32[512,4]{0,1:T(4,128)S(1)}, u32[]{:S(2)}, u32[]{:S(2)}) collective-permute-start(f32[512,4]{0,1:T(4,128)S(1)} %get-tuple-element.44), channel_id=1, source_target_pairs={{2,0},{4,2},{6,4},{8,6},{10,8},{12,10},{14,12},{16,14},{18,16},{20... | collective-permute-start | bytes 24584 | tf_op jit(solution)/shard_map/ppermute | solution.py:27
  117.3 12.3 %collective-permute-start.4 = (f32[256,4]{0,1:T(4,128)S(1)}, f32[256,4]{0,1:T(4,128)S(1)}, u32[]{:S(2)}, u32[]{:S(2)}) collective-permute-start(f32[256,4]{0,1:T(4,128)S(1)} %get-tuple-element.61), channel_id=1, source_target_pairs={{0,2},{2,4},{4,6},{6,8},{8,10},{10,12},{12,14},{14,16},{16,18},{18... | collective-permute-start | bytes 12296 | tf_op jit(solution)/shard_map/ppermute | solution.py:24
  121.5 8.0 collective-permute-start.5
  141.2 13.1 %collective-permute-start.6 = (f32[128,4]{0,1:T(4,128)S(1)}, f32[128,4]{0,1:T(4,128)S(1)}, u32[]{:S(2)}, u32[]{:S(2)}) collective-permute-start(f32[128,4]{0,1:T(4,128)S(1)} %get-tuple-element.79), channel_id=1, source_target_pairs={{0,2},{2,4},{4,6},{6,8},{8,10},{10,12},{12,14},{14,16},{16,18},{18... | collective-permute-start | bytes 6152 | tf_op jit(solution)/shard_map/ppermute | solution.py:24
  146.3 7.9 collective-permute-start.7
  165.4 14.3 %collective-permute-start.8 = (f32[64,4]{0,1:T(4,128)S(1)}, f32[64,4]{0,1:T(4,128)S(1)}, u32[]{:S(2)}, u32[]{:S(2)}) collective-permute-start(f32[64,4]{0,1:T(4,128)S(1)} %get-tuple-element.99), channel_id=1, source_target_pairs={{0,2},{2,4},{4,6},{6,8},{8,10},{10,12},{12,14},{14,16},{16,18},{18... | collective-permute-start | bytes 3080 | tf_op jit(solution)/shard_map/ppermute | solution.py:24
  170.9 8.8 %collective-permute-start.9 = (f32[64,4]{0,1:T(4,128)S(1)}, f32[64,4]{0,1:T(4,128)S(1)}, u32[]{:S(2)}, u32[]{:S(2)}) collective-permute-start(f32[64,4]{0,1:T(4,128)S(1)} %get-tuple-element.100), channel_id=1, source_target_pairs={{2,0},{4,2},{6,4},{8,6},{10,8},{12,10},{14,12},{16,14},{18,16},{20... | collective-permute-start | bytes 3080 | tf_op jit(solution)/shard_map/ppermute | solution.py:27
  190.9 14.2 %collective-permute-start.10 = (f32[32,4]{0,1:T(4,128)S(1)}, f32[32,4]{0,1:T(4,128)S(1)}, u32[]{:S(2)}, u32[]{:S(2)}) collective-permute-start(f32[32,4]{0,1:T(4,128)S(1)} %get-tuple-element.131), channel_id=1, source_target_pairs={{0,2},{2,4},{4,6},{6,8},{8,10},{10,12},{12,14},{14,16},{16,18},{18... | collective-permute-start | bytes 1544 | tf_op jit(solution)/shard_map/ppermute | solution.py:24
  196.4 8.7 %collective-permute-start.11 = (f32[32,4]{0,1:T(4,128)S(1)}, f32[32,4]{0,1:T(4,128)S(1)}, u32[]{:S(2)}, u32[]{:S(2)}) collective-permute-start(f32[32,4]{0,1:T(4,128)S(1)} %get-tuple-element.132), channel_id=1, source_target_pairs={{2,0},{4,2},{6,4},{8,6},{10,8},{12,10},{14,12},{16,14},{18,16},{20... | collective-permute-start | bytes 1544 | tf_op jit(solution)/shard_map/ppermute | solution.py:27
  703.0 23.3 %collective-permute-start.12 = (f32[64,2]{0,1:T(2,128)S(1)}, f32[64,2]{0,1:T(2,128)S(1)}, u32[]{:S(2)}, u32[]{:S(2)}) collective-permute-start(f32[64,2]{0,1:T(2,128)S(1)} %get-tuple-element.163), channel_id=1, source_target_pairs={{0,2},{2,4},{4,6},{6,8},{8,10},{10,12},{12,14},{14,16},{16,18},{18... | collective-permute-start | bytes 1544 | tf_op jit(solution)/shard_map/ppermute | solution.py:24
  704.3 22.0 %collective-permute-start.13 = (f32[64,2]{0,1:T(2,128)S(1)}, f32[64,2]{0,1:T(2,128)S(1)}, u32[]{:S(2)}, u32[]{:S(2)}) collective-permute-start(f32[64,2]{0,1:T(2,128)S(1)} %get-tuple-element.164), channel_id=1, source_target_pairs={{2,0},{4,2},{6,4},{8,6},{10,8},{12,10},{14,12},{16,14},{18,16},{20... | collective-permute-start | bytes 1544 | tf_op jit(solution)/shard_map/ppermute | solution.py:27
  716.3 5.2 all-to-all-start.34
  721.5 4.7 all-to-all-start.26
  737.0 5.6 collective-permute-start.14
  741.3 4.3 collective-permute-start.15
  756.8 7.2 collective-permute-start.16
  758.4 5.5 collective-permute-start.17
  773.1 5.5 collective-permute-start.18
  777.2 4.4 collective-permute-start.19
  792.8 3.0 collective-permute-start.20
  794.5 4.4 collective-permute-start.21
  814.4 3.4 collective-permute-start.22
  816.4 4.6 collective-permute-start.23
where the time goes:
time: 839 us; the launch traced here: 828 us
  blocking collectives  581 us (69%)
  local copies, waits for them, and re-layouts  98.1 us (12%)
  starting transfers between devices  66.5 us (8%)
  other arithmetic  46.7 us (6%)
  between operations  22.3 us (3%)
  waiting for transfers between devices  13.3 us (2%)
    all_gather x1, blocking collectives, shards(): current = lax.all_gather(current, 'tm', axis=1, tiled=True)  287 us
    psum x1, blocking collectives, shards(): level_sums.append(lax.psum(local_sum, ('tm', 'chan')))  98.5 us
    psum x1, blocking collectives, shards(): coarse_total = lax.psum(coarse_local, 'chan')  58.1 us
    ppermute x12, starting transfers between devices, with_halo(): lax.ppermute(lax.slice_in_dim(block, block.shape[dim] - width, None, axis...  43.5 us
    all_to_all x6, blocking collectives, channel_inverse(): lax.all_to_all(chan_low, 'chan', split_axis=1, concat_axis=0, tiled=True)  27.5 us
    all_to_all x6, blocking collectives, channel_forward(): lax.all_to_all(combined, 'chan', split_axis=1, concat_axis=0, tiled=True)  24.4 us
    all_to_all x6, blocking collectives, channel_forward(): lax.all_to_all(chan_high, 'chan', split_axis=0, concat_axis=1, tiled=True)  24.2 us
    all_to_all x6, blocking collectives, channel_inverse(): lax.all_to_all(combined, 'chan', split_axis=0, concat_axis=1, tiled=True)  23.4 us
  transfers between devices with their start and end apart: 26, of which 6 were waited for; matrix products, arithmetic and copies ran while one was open for 3% of the time, Pallas kernels for 0%

commit v1 on v0

v1 whole, which is shorter than its diff:
```python
import functools

import jax
import jax.numpy as jnp
import ml_dtypes
import numpy as np
from jax import lax
from jax.experimental import pallas as pl
from jax.experimental.pallas import tpu as pltpu
from jax.sharding import PartitionSpec as P

LEVELS = 6
COARSE = 6
GTAB = 8
NBLK = 32
C = 2048
S = 32768
NT = 128
OWN = 1024
HALO = 512
SEG = 192
A1 = -1.586134342059924
B1 = -0.052980118572961
A2 = 0.882911075530934
B2 = 0.443506852043971
KS = 1.149604398860241
FLOOR = 1e-06
F32 = jnp.float32
BF16 = jnp.bfloat16


def _next(e):
    return np.concatenate((e[1:], e[-1:]))


def _prev(o):
    return np.concatenate((o[:1], o[:-1]))


def _lift(x):
    e, o = x[0::2], x[1::2]
    o = o + A1 * (e + _next(e))
    e = e + B1 * (_prev(o) + o)
    o = o + A2 * (e + _next(e))
    e = e + B2 * (_prev(o) + o)
    return KS * e, o / KS


def _unlift(low, high):
    e, o = low / KS, high * KS
    e = e - B2 * (_prev(o) + o)
    o = o - A2 * (e + _next(e))
    e = e - B1 * (_prev(o) + o)
    o = o - A1 * (e + _next(e))
    return np.stack((e, o), axis=1).reshape((2 * e.shape[0],) + e.shape[1:])


def _forward(inputs, lows, highs, rows, cols, start, stop, scale):
    pairs = list(lows) + list(highs)
    a = max(2 * min(pairs) - 16, start)
    b = min(2 * max(pairs) + 16, stop)
    low, high = _lift(np.eye(b - a))
    out = np.zeros((rows, cols))
    for band, places in ((low, lows), (high, highs)):
        for pair, col in places.items():
            if a <= 2 * pair < b:
                line = band[pair - a // 2]
                for i in np.nonzero(line)[0]:
                    out[inputs[a + int(i)], col] += scale * line[i]
    return out


def _inverse(lows, highs, outputs, rows, cols, start, stop, scale):
    a = max(2 * (min(outputs) // 2) - 16, start) // 2
    b = min(2 * (max(outputs) // 2) + 18, stop) // 2
    n = b - a
    eye, zero = np.eye(n), np.zeros((n, n))
    from_low, from_high = _unlift(eye, zero), _unlift(zero, eye)
    out = np.zeros((rows, cols))
    for sample, col in outputs.items():
        if 2 * a <= sample < 2 * b:
            for lines, places in ((from_low, lows), (from_high, highs)):
                line = lines[sample - 2 * a]
                for i in np.nonzero(line)[0]:
                    out[places[a + int(i)], col] += scale * line[i]
    return out


def _pair(m):
    hi = m.astype(ml_dtypes.bfloat16)
    lo = (m - hi.astype(np.float64)).astype(ml_dtypes.bfloat16)
    return np.stack((hi, lo))


def _run(first, last, at):
    return {k: at + k - first for k in range(first, last)}


OWN_LOW0 = _run(2, 126, 2)
OWN_HIGH0 = _run(2, 126, 130)
RIM_LOW0 = {**_run(-8, 2, 0), **_run(126, 137, 10)}
RIM_HIGH0 = {**_run(-2, 2, 32), **_run(126, 130, 36)}
RIM_IN0 = {**_run(0, 32, 0), **_run(-32, 0, 32), **_run(256, 288, 64), **_run(224, 256, 96)}
IN1 = {**OWN_LOW0, **{k: 128 + v for k, v in RIM_LOW0.items()}}
LOW1 = {**_run(0, 64, 0), **_run(-2, 0, 134), **_run(64, 67, 136)}
HIGH1 = {**_run(0, 64, 64), **_run(-3, 0, 128), **_run(64, 67, 131)}
IN2 = {**_run(0, 128, 0), **_run(-64, 0, 128), **_run(128, 192, 192), **_run(-128, -64, 256)}
LOW2 = _run(-52, 85, 0)
HIGH2 = _run(-3, 36, 140)
LOW3 = _run(-24, 41, 0)
HIGH3 = _run(-3, 20, 70)
LOW4 = _run(-10, 19, 0)
HIGH4 = _run(-3, 12, 40)
LOW5 = _run(-2, 8, 0)
HIGH5 = _run(-3, 8, 16)


def _edges(variants, width):
    far = 1 << 20
    if variants == 3:
        return ((0, far), (-far, far), (-far, width))
    return ((0, far), (-width, far), (-far, far), (-far, 2 * width), (-far, width))


def _table(build, variants, width):
    return np.stack([_pair(build(*edge)) for edge in _edges(variants, width)])


@functools.cache
def _tables():
    fw, inv = _forward, _inverse
    out = {}
    out["t0"] = _pair(fw(_run(0, 256, 0), OWN_LOW0, OWN_HIGH0, 256, 256, -(1 << 20), 1 << 20, 1.0))
    out["t0r"] = _table(lambda a, b: fw(RIM_IN0, RIM_LOW0, RIM_HIGH0, 128, 128, a, b, 1.0), 3, 256)
    out["t1"] = _table(lambda a, b: fw(IN1, LOW1, HIGH1, 256, 256, a, b, KS), 3, 128)
    out["t2"] = _table(lambda a, b: fw(IN2, LOW2, HIGH2, 384, 256, a, b, KS), 5, 64)
    out["t3"] = _table(lambda a, b: fw(LOW2, LOW3, HIGH3, 256, 128, a, b, KS), 5, 32)
    out["t4"] = _table(lambda a, b: fw(LOW3, LOW4, HIGH4, 128, 128, a, b, KS), 5, 16)

    def level5(a, b):
        m = fw(LOW4, LOW5, HIGH5, 128, 256, a, b, KS)
        for i in range(128):
            m[:, 128 + i] = m[:, LOW5[i % 4]]
        return m

    out["t5"] = _table(level5, 5, 8)

    def low_part(places, first, last):
        return {k: places[k] for k in range(first, last)}

    full0 = {**OWN_LOW0, **{k: 256 + v for k, v in RIM_LOW0.items() if -2 <= k < 2 or 126 <= k < 130}}
    high0 = {**OWN_HIGH0, **{k: 256 + v for k, v in RIM_HIGH0.items()}}
    out["s0"] = _table(lambda a, b: inv(full0, high0, _run(0, 256, 0), 384, 256, a, b, 1.0), 3, 256)
    out["s1"] = _table(
        lambda a, b: inv(LOW1, HIGH1, low_part(IN1, -1, 130), 256, 256, a, b, 1.0 / KS), 3, 128
    )
    out["s2"] = _table(
        lambda a, b: inv(low_part(LOW2, -2, 36), HIGH2, low_part(LOW1, -2, 67), 256, 256, a, b, 1.0 / KS),
        3,
        64,
    )
    out["s3"] = _table(
        lambda a, b: inv(low_part(LOW3, -2, 20), HIGH3, low_part(LOW2, -2, 36), 128, 128, a, b, 1.0 / KS),
        3,
        32,
    )
    out["s4"] = _table(
        lambda a, b: inv(low_part(LOW4, -2, 12), HIGH4, low_part(LOW3, -2, 20), 128, 128, a, b, 1.0 / KS),
        3,
        16,
    )
    out["s5"] = _table(
        lambda a, b: inv(low_part(LOW5, -2, 8), HIGH5, low_part(LOW4, -2, 12), 128, 128, a, b, 1.0 / KS),
        3,
        8,
    )
    n = S >> LEVELS
    bands = []
    current = np.eye(n)
    for _ in range(COARSE):
        current, high = _lift(current)
        bands.append(high)
    coarse = np.concatenate([current] + bands[::-1])
    order = (np.arange(n) % NT) * 4 + np.arange(n) // NT
    out["w"] = _pair((KS * coarse.T)[order])
    last = n >> COARSE
    current = np.eye(n)[:last]
    for step in range(COARSE):
        size = last << step
        current = _unlift(current, np.eye(n)[size : 2 * size])
    rebuilt = np.zeros((n + 32, n))
    rebuilt[2 : n + 2] = current / KS
    rebuilt = np.moveaxis(_pair(rebuilt), 0, 0)
    pieces = np.zeros((NT, 2, 16, n), ml_dtypes.bfloat16)
    for t in range(NT):
        pieces[t, :, :10] = rebuilt[:, 4 * t : 4 * t + 10]
    out["v"] = pieces
    return out


def _lane_mask(*places):
    row = np.zeros(128, np.float32)
    for lanes in places:
        row[list(lanes)] = 1.0
    return row


@functools.cache
def _lane_masks():
    def own(places, first, last, base):
        return [v - base for k, v in places.items() if first <= k < last and 0 <= v - base < 128]

    rows = []
    rows.append(_lane_mask(own(RIM_HIGH0, 0, 128, 0)))
    rows.append(_lane_mask(own(RIM_HIGH0, 0, 128, 0), own(RIM_LOW0, 0, 128, 0)))
    for low, high, n in ((LOW1, HIGH1, 64), (LOW2, HIGH2, 32), (LOW3, HIGH3, 16), (LOW4, HIGH4, 8), (LOW5, HIGH5, 4)):
        rows.append(_lane_mask(own(high, 0, n, 0)))
        rows.append(_lane_mask(own(high, 0, n, 0), own(low, 0, n, 0)))
    rows.append(_lane_mask(own(HIGH2, 0, 32, 128)))
    rows.append(_lane_mask(own(HIGH2, 0, 32, 128)))
    out = np.zeros((16, 128), np.float32)
    out[: len(rows)] = np.stack(rows)
    return out


def _dot3(x, t):
    hi = x.astype(BF16)
    lo = (x - hi.astype(F32)).astype(BF16)
    d = functools.partial(jnp.dot, preferred_element_type=F32)
    return d(hi, t[0]) + d(lo, t[0]) + d(hi, t[1])


def _time(load, count, t, store, step):
    for j in range(0, count, step):
        x = load(j, step)
        y = _dot3(x.reshape(step * 8, x.shape[2]), t)
        store(j, step, y.reshape(step, 8, y.shape[1]))


def _sublane(lanes):
    return lax.broadcasted_iota(jnp.int32, (8, lanes), 0)


def _lane(rows=8):
    return lax.broadcasted_iota(jnp.int32, (rows, 128), 1)


def _wide(v, lanes):
    return v if lanes == 128 else jnp.concatenate([v] * (lanes // 128), axis=1)


class _Wrap:
    def __init__(self, lanes):
        sub = _sublane(lanes)
        self.last, self.first = sub == 7, sub == 0

    def after(self, first, last):
        return jnp.where(self.last, last, pltpu.roll(first, 7, 0))

    def before(self, last, first):
        return jnp.where(self.first, first, pltpu.roll(last, 1, 0))


def _coefs(w_ref, level, lanes):
    return [[_wide(c * w_ref[level, q], lanes) for q in range(3)] for c in (A1, B1, A2, B2)]


def _chan_forward(get, n, w_ref, level, lanes, put_low, put_high):
    wrap = _Wrap(lanes)
    ca, cb, cc, cd = _coefs(w_ref, level, lanes)
    per = n // 3
    first = get(0)
    e, o1, e1, o2 = {0: first}, {}, {}, {}

    def high(k, v):
        o2[k] = v
        put_high(k, k // per, v)

    def low(k):
        put_low(k, k // per, e1[k] + cd[k // per] * (o2[k - 1] + o2[k]))

    for k in range(n):
        q = k // per
        e[k + 1] = get(2 * k + 2) if k + 1 < n else wrap.after(first, e[k])
        o1[k] = get(2 * k + 1) + ca[q] * (e[k] + e[k + 1])
        if k >= 1:
            e1[k] = e[k] + cb[q] * (o1[k - 1] + o1[k])
        if k >= 2:
            high(k - 1, o1[k - 1] + cc[(k - 1) // per] * (e1[k - 1] + e1[k]))
        if k >= 3:
            low(k - 1)
    e1[0] = first + cb[0] * (wrap.before(o1[n - 1], o1[0]) + o1[0])
    high(0, o1[0] + cc[0] * (e1[0] + e1[1]))
    high(n - 1, o1[n - 1] + cc[2] * (e1[n - 1] + wrap.after(e1[0], e1[n - 1])))
    o2[-1] = wrap.before(o2[n - 1], o2[0])
    for k in (0, 1, n - 1):
        low(k)


def _chan_inverse(get_low, get_high, n, w_ref, level, lanes, put):
    wrap = _Wrap(lanes)
    ca, cb, cc, cd = _coefs(w_ref, level, lanes)
    per = n // 3
    o = {0: get_high(0)}
    o[-1] = wrap.before(get_high(n - 1), o[0])
    e1, o1, e2 = {}, {}, {}

    def even(k):
        e2[k] = e1[k] - cb[k // per] * (o1[k - 1] + o1[k])
        put(2 * k, e2[k])

    def odd(k):
        put(2 * k + 1, o1[k] - ca[k // per] * (e2[k] + e2[k + 1]))

    for k in range(n):
        q = k // per
        if k:
            o[k] = get_high(k)
        e1[k] = get_low(k) - cd[q] * (o[k - 1] + o[k])
        if k >= 1:
            o1[k - 1] = o[k - 1] - cc[(k - 1) // per] * (e1[k - 1] + e1[k])
        if k >= 2:
            even(k - 1)
        if k >= 3:
            odd(k - 2)
    o1[n - 1] = o[n - 1] - cc[2] * (e1[n - 1] + wrap.after(e1[0], e1[n - 1]))
    o1[-1] = wrap.before(o1[n - 1], o1[0])
    even(n - 1)
    if n > 2:
        odd(n - 2)
    even(0)
    odd(0)
    e2[n] = wrap.after(e2[0], e2[n - 1])
    odd(n - 1)


class _Squares:
    def __init__(self):
        self.acc = {}

    def add(self, key, v):
        self.acc[key] = v * v if key not in self.acc else self.acc[key] + v * v

    def total(self, rows_ref, tiles):
        out = None
        for q in range(3):
            part = None
            for (band, tile), lanes in tiles.items():
                v = self.acc[(band, tile, q)] * (KS * KS if band == "low" else 1.0 / (KS * KS))
                v = v if lanes is None else v * lanes
                part = v if part is None else part + v
            part = part * rows_ref[q]
            out = part if out is None else out + part
        return out


def _tile(v, i):
    return v[:, 128 * i : 128 * (i + 1)]


def _pack_kernel(sc, x, recv, xs, right, left, xa, xb, sems):
    core = sc[0]
    at_own = pl.multiple_of(core * HALO, 8)
    at_recv = pl.multiple_of((1 - core) * OWN, 8)
    copies = []
    for i, buf in enumerate((xa, xb)):
        lanes = pl.ds(128 * i, 128)
        copies.append(pltpu.make_async_copy(x.at[:, lanes], buf.at[pl.ds(at_own, OWN)], sems.at[2 * i]))
        copies.append(pltpu.make_async_copy(recv.at[:, lanes], buf.at[pl.ds(at_recv, HALO)], sems.at[2 * i + 1]))
    for c in copies:
        c.start()
    for c in copies:
        c.wait()
    group = _lane() // 32
    for i in range(48):
        to_right, to_left = None, None
        for g in range(4):
            j = 48 * g + i
            a = xa[pl.ds(j, 8, stride=SEG), :]
            b = xb[pl.ds(j, 8, stride=SEG), :]
            xs[j, :, 0:128] = a
            xs[j, :, 128:256] = b
            a = pltpu.roll(a, 32 * g, 1) if g else a
            b = pltpu.roll(b, (32 * g + 32) % 128, 1) if g != 3 else b
            to_left = a if to_left is None else jnp.where(group == g, a, to_left)
            to_right = b if to_right is None else jnp.where(group == g, b, to_right)
        right[i] = to_right
        left[i] = to_left


def _own_kernel(xs, t, w, rows, low, dlow, dhigh, sums, y):
    def store(j, step, v):
        y[pl.ds(j, step)] = v

    _time(lambda j, step: xs[pl.ds(j, step)], SEG, t, store, 24)
    sq = _Squares()

    def put_low(k, q, v):
        low[k] = _tile(v, 0)
        dlow[k] = _tile(v, 1)
        sq.add(("low", 1, q), _tile(v, 1))

    def put_high(k, q, v):
        dhigh[k] = v
        sq.add(("high", 0, q), v[:, :128])
        sq.add(("high", 1, q), v[:, 128:])

    _chan_forward(lambda j: y[j], 96, w, 0, 256, put_low, put_high)
    sums[...] = sq.total(rows, {("low", 1): None, ("high", 0): None, ("high", 1): None})


def _rim_kernel(
    sc, xs, from_left, from_right, low0, t0r_all, t1_all, w, rows, lanes,
    dlow_r, dhigh_r, low1, high1, message, sums, t0r, t1, rim, y, y1, sems,
):
    variant = sc[1]
    c0 = pltpu.make_async_copy(t0r_all.at[variant], t0r, sems.at[0])
    c1 = pltpu.make_async_copy(t1_all.at[variant], t1, sems.at[1])
    c0.start()
    c1.start()
    lane = _lane()
    for j in range(SEG):
        g, i = j // 48, j % 48
        a = from_left[i]
        b = from_right[i]
        a = pltpu.roll(a, (32 - 32 * g) % 128, 1) if g != 1 else a
        b = pltpu.roll(b, (64 - 32 * g) % 128, 1) if g != 2 else b
        halo = jnp.where(lane < 64, a, b)
        own = jnp.where(lane < 32, xs[j, :, 0:128], xs[j, :, 128:256])
        rim[j] = jnp.where((lane < 32) | (lane >= 96), own, halo)
    c0.wait()

    def store(j, step, v):
        y[pl.ds(j, step)] = v

    _time(lambda j, step: rim[pl.ds(j, step)], SEG, t0r, store, 24)
    sq = _Squares()

    def put_low(k, q, v):
        dlow_r[k] = v
        sq.add(("low", 0, q), v)

    def put_high(k, q, v):
        dhigh_r[k] = v
        sq.add(("high", 0, q), v)

    _chan_forward(lambda j: y[j], 96, w, 0, 128, put_low, put_high)
    sums[0] = sq.total(rows, {("low", 0): lanes[0:1], ("high", 0): lanes[1:2]})
    c1.wait()

    def load1(j, step):
        return jnp.concatenate([low0[pl.ds(j, step)], dlow_r[pl.ds(j, step)]], axis=2)

    def store1(j, step, v):
        y1[pl.ds(j, step)] = v

    _time(load1, 96, t1, store1, 24)
    sq1 = _Squares()

    def put_low1(k, q, v):
        low1[k] = v
        sq1.add(("low", 0, q), _tile(v, 0))

    def put_high1(k, q, v):
        high1[k] = v
        sq1.add(("high", 0, q), _tile(v, 0))

    _chan_forward(lambda j: y1[j], 48, w, 1, 256, put_low1, put_high1)
    sums[1] = sq1.total(rows, {("low", 0): lanes[2:3], ("high", 0): lanes[3:4]})
    for i in range(24):
        message[i] = jnp.where(lane < 64, low1[i, :, 0:128], pltpu.roll(low1[i + 24, :, 0:128], 64, 1))


def _middle_kernel(
    sc, own, m2, m1, p1, p2, s0, s01, t2_all, t3_all, t4_all, t5_all, w, rows, lanes, place,
    a2l, a2h, a3l, a3h, a4l, a4h, a5l, a5h, payload,
    t2, t3, t4, t5, x2, y2, y3, y4, y5, l5, sems,
):
    variant = sc[2]
    copies = []
    for i, (src, dst) in enumerate(((t2_all, t2), (t3_all, t3), (t4_all, t4), (t5_all, t5))):
        c = pltpu.make_async_copy(src.at[variant], dst, sems.at[i])
        c.start()
        copies.append(c)
    lane = _lane()
    for j in range(48):
        h, i = j // 24, j % 24

        def low_half(ref):
            return ref[i] if h == 0 else pltpu.roll(ref[i], 64, 1)

        def high_half(ref):
            return ref[i] if h == 1 else pltpu.roll(ref[i], 64, 1)

        x2[j, :, 0:128] = jnp.where(lane < 64, low_half(own), high_half(p1))
        x2[j, :, 128:256] = jnp.where(lane < 64, low_half(m1), high_half(p2))
        x2[j, :, 256:384] = low_half(m2)

    totals = [s0[...] + s01[0], s01[1]]

    def level(l, load, count, t, y, step, lanes_n, low, high, tiles):
        def store(j, n, v):
            y[pl.ds(j, n)] = v

        _time(load, count, t, store, step)
        sq = _Squares()

        def put_low(k, q, v):
            low[k] = v
            for i in range(tiles):
                sq.add(("low", i, q), _tile(v, i))

        def put_high(k, q, v):
            if high.shape[2] == v.shape[1]:
                high[k] = v
            else:
                high[k] = _tile(v, 0)
            for i in range(tiles):
                sq.add(("high", i, q), _tile(v, i))

        _chan_forward(lambda j: y[j], count // 2, w, l, lanes_n, put_low, put_high)
        masks = {("low", 0): lanes[2 * l : 2 * l + 1], ("high", 0): lanes[2 * l + 1 : 2 * l + 2]}
        if tiles == 2:
            masks[("low", 1)] = lanes[12:13]
            masks[("high", 1)] = lanes[13:14]
        totals.append(sq.total(rows, masks))

    copies[0].wait()
    level(2, lambda j, n: x2[pl.ds(j, n)], 48, t2, y2, 24, 256, a2l, a2h, 2)
    copies[1].wait()
    level(3, lambda j, n: a2l[pl.ds(j, n)], 24, t3, y3, 24, 128, a3l, a3h, 1)
    copies[2].wait()
    level(4, lambda j, n: a3l[pl.ds(j, n)], 12, t4, y4, 12, 128, a4l, a4h, 1)
    copies[3].wait()
    level(5, lambda j, n: a4l[pl.ds(j, n)], 6, t5, y5, 6, 256, l5, a5h, 1)
    sub = _sublane(128)
    line = jnp.zeros((8, 128), F32)
    for j in range(3):
        a5l[j] = l5[j, :, 0:128]
        line = line + place[j] * l5[j, :, 128:256]
    sums = jnp.zeros((8, 128), F32)
    for l in range(LEVELS):
        sums = jnp.where(sub == l, jnp.sum(totals[l], axis=0, keepdims=True), sums)
    sums = jnp.sum(sums, axis=1, keepdims=True)
    line = line + jnp.where(lane == 96 + sub, sums, 0.0) * jnp.where(sub < LEVELS, 1.0, 0.0)
    line = jnp.sum(line, axis=0, keepdims=True)
    payload[...] = jnp.broadcast_to(line, payload.shape)


def _shrink(v, limit):
    return v - jnp.minimum(jnp.maximum(v, -limit), limit)


def _back_kernel(
    sc, g, w_all, v_all, s0_all, s1_all, s2_all, s3_all, s4_all, s5_all, w, cmask,
    dlow0, dhigh0, rlow0, rhigh0, a1l, a1h, a2l, a2h, a3l, a3h, a4l, a4h, a5l, a5h,
    out,
    v, s0, s1, s2, s3, s4, s5, gt, y5, y4, y3, y2, y1, y0, c4, c3, c2, c1, c0, fa, fb, sems,
):
    variant = sc[1]
    core = sc[0]
    v[...] = jnp.zeros(v.shape, BF16)
    copies = [pltpu.make_async_copy(v_all.at[sc[3]], v.at[:, pl.ds(0, 16), :], sems.at[0])]
    for i, (src, dst) in enumerate(
        ((s5_all, s5), (s4_all, s4), (s3_all, s3), (s2_all, s2), (s1_all, s1), (s0_all, s0))
    ):
        copies.append(pltpu.make_async_copy(src.at[variant], dst, sems.at[i + 1]))
    for c in copies:
        c.start()
    lane1 = _lane(1)
    total = jnp.sum(g[...], axis=0, keepdims=True)
    limits = []
    for l in range(LEVELS):
        entries = 3 * (C >> (l + 1)) * (S >> (l + 1))
        s = jnp.sum(jnp.where(lane1 == 96 + l, total, 0.0), axis=1, keepdims=True)
        limits.append(jnp.sqrt(s * (1.0 / entries) + FLOOR))
    gt[0] = jnp.transpose(g[0:128])
    gt[1] = jnp.transpose(g[128:256])
    rows = [
        jnp.concatenate([gt[c, pl.ds(m, 24, stride=4), :] for m in range(4)], axis=1) for c in range(2)
    ]
    coarse = _dot3(jnp.concatenate(rows, axis=0), w_all)
    position = lax.broadcasted_iota(jnp.int32, (48, 512), 1)
    highs = position >= (S >> (LEVELS + COARSE))
    square = jnp.where(highs, coarse * coarse, 0.0)
    square = square[:, 0:128] + square[:, 128:256] + square[:, 256:384] + square[:, 384:512]
    square = jnp.sum(square * cmask[...], axis=0, keepdims=True)
    square = jnp.sum(square, axis=1, keepdims=True)
    entries = (C >> LEVELS) * ((S >> LEVELS) - (S >> (LEVELS + COARSE)))
    limit = jnp.sqrt(square * (1.0 / entries) + FLOOR)
    coarse = jnp.where(highs, _shrink(coarse, limit), coarse)
    mine = jnp.where(core == 0, coarse[0:24], coarse[24:48])
    mine = jnp.concatenate([mine, jnp.zeros((8, 512), F32)], axis=0)
    hi = mine.astype(BF16)
    lo = (mine - hi.astype(F32)).astype(BF16)
    copies[0].wait()

    def nt(a, b):
        return lax.dot_general(a, b, (((1,), (1,)), ((), ())), preferred_element_type=F32)

    current = nt(hi, v[0]) + nt(lo, v[0]) + nt(hi, v[1])

    lane = _lane()

    def level(l, get_current, low, high, n, y, s, nxt, step, lanes, needed):
        width = y.shape[2]
        tl = jnp.broadcast_to(limits[l] * (1.0 / KS), (8, width))
        th = jnp.broadcast_to(limits[l] * KS, (8, width))
        is_low = lax.broadcasted_iota(jnp.int32, (8, width), 1)
        is_low = needed(is_low)

        def get_low(k):
            return jnp.where(is_low, get_current(k), _shrink(low[k], tl))

        def put(j, value):
            y[j] = value

        _chan_inverse(get_low, lambda k: _shrink(high[k], th), n, w, l, width, put)

        def store(j, m, value):
            nxt[pl.ds(j, m)] = value

        _time(lambda j, m: y[pl.ds(j, m)], 2 * n, s, store, step)

    copies[1].wait()
    level(5, lambda k: current[8 * k : 8 * k + 8], a5l, a5h, 3, y5, s5, c4, 6, 128, lambda i: i < 10)
    copies[2].wait()
    level(4, lambda k: c4[k], a4l, a4h, 6, y4, s4, c3, 12, 128, lambda i: i < 29)
    copies[3].wait()
    level(3, lambda k: c3[k], a3l, a3h, 12, y3, s3, c2, 24, 128, lambda i: i < 65)
    copies[4].wait()
    pad = jnp.zeros((8, 128), F32)
    level(
        2, lambda k: jnp.concatenate([c2[k], pad], axis=1), a2l, a2h, 24, y2, s2, c1, 24, 256, lambda i: i < 128
    )
    copies[5].wait()
    level(
        1, lambda k: c1[k], a1l, a1h, 48, y1, s1, c0, 24, 256, lambda i: (i < 64) | (i >= 134),
    )
    copies[6].wait()
    tl = jnp.broadcast_to(limits[0] * (1.0 / KS), (8, 128))
    th = jnp.broadcast_to(limits[0] * KS, (8, 128))
    th2 = jnp.broadcast_to(limits[0] * KS, (8, 256))
    rim_low = lane < 32

    def get_low0(k):
        now = c0[k]
        rim = jnp.where(rim_low, _tile(now, 1), _shrink(rlow0[k], tl))
        return jnp.concatenate([_tile(now, 0), _shrink(dlow0[k], tl), rim], axis=1)

    def get_high0(k):
        return jnp.concatenate([_shrink(dhigh0[k], th2), _shrink(rhigh0[k], th)], axis=1)

    def put0(j, value):
        y0[j] = value

    _chan_inverse(get_low0, get_high0, 96, w, 0, 384, put0)

    def store0(j, m, value):
        for i in range(m):
            fa[pl.ds(j + i, 8, stride=SEG), :] = value[i, :, 0:128]
            fb[pl.ds(j + i, 8, stride=SEG), :] = value[i, :, 128:256]

    _time(lambda j, m: y0[pl.ds(j, m)], SEG, s0, store0, 24)
    at_own = pl.multiple_of(core * HALO, 8)
    last = [
        pltpu.make_async_copy(buf.at[pl.ds(at_own, OWN)], out.at[:, pl.ds(128 * i, 128)], sems.at[7 + i])
        for i, buf in enumerate((fa, fb))
    ]
    for c in last:
        c.start()
    for c in last:
        c.wait()


VM = pl.BlockSpec(memory_space=pltpu.VMEM)
SM = pl.BlockSpec(memory_space=pltpu.SMEM)
ANY = pl.BlockSpec(memory_space=pl.ANY)


def _call(kernel, name, args, specs, outs, out_specs, scratch):
    return pl.pallas_call(
        kernel,
        out_shape=[jax.ShapeDtypeStruct(s, F32) for s in outs],
        in_specs=specs,
        out_specs=out_specs,
        scratch_shapes=scratch,
        compiler_params=pltpu.CompilerParams(vmem_limit_bytes=40 * 1024 * 1024),
        name=name,
    )(*args)


def _shift(v, by):
    return lax.ppermute(v, "tm", [(i, i + by) for i in range(NT) if 0 <= i + by < NT])


def shards(record, gauge_table, gauge_index):
    tables = _tables()
    core = lax.axis_index("chan")
    place = lax.axis_index("tm")
    v3 = jnp.where(place == 0, 0, jnp.where(place == NT - 1, 2, 1))
    v5 = jnp.minimum(place, 2) + jnp.maximum(place - (NT - 3), 0)
    sc = jnp.stack([core, v3, v5, place]).astype(jnp.int32)

    matches = (gauge_index[:, :, None] == jnp.arange(GTAB, dtype=jnp.int32)[None, None, :]).astype(F32)
    block_weights = jnp.sum(matches * gauge_table[:, None, :], axis=2)
    kept = jnp.where(core == 0, block_weights[:, 0:24], block_weights[:, 8:32])
    weights = jnp.broadcast_to(kept.reshape(LEVELS, 8, 3).transpose(0, 2, 1)[..., None], (LEVELS, 3, 8, 128))

    block = 3 * np.arange(8)[None, :] + np.arange(3)[:, None]
    row_masks = np.stack([block < 16, block >= 8]).astype(np.float32)
    row_mask = jnp.where(core == 0, row_masks[0], row_masks[1])
    row_mask = jnp.broadcast_to(row_mask[..., None], (3, 8, 128))
    lane_masks = jnp.asarray(_lane_masks())
    spots = np.zeros((3, 8, 128), np.float32)
    cmask = np.zeros((48, 128), np.float32)
    for j in range(3):
        for s in range(8):
            spots[j, s, 4 * (8 * j + s) : 4 * (8 * j + s) + 4] = 1.0
            cmask[8 * j + s] = 1.0 if 3 * s + j < 16 else 0.0
            cmask[24 + 8 * j + s] = 1.0 if 3 * s + j >= 8 else 0.0

    sent = jnp.where(core == 0, record[OWN - HALO :], record[:HALO])
    recv = lax.ppermute(sent, "chan", [(0, 1), (1, 0)])
    dma = pltpu.SemaphoreType.DMA
    xs, right, left = _call(
        _pack_kernel, "pack", (sc, record, recv), [SM, ANY, ANY],
        [(SEG, 8, 256), (48, 8, 128), (48, 8, 128)], [VM] * 3,
        [pltpu.VMEM((8 * SEG, 128), F32)] * 2 + [dma((4,))],
    )
    from_left, from_right = _shift(right, 1), _shift(left, -1)
    low0, dlow0, dhigh0, sum0 = _call(
        _own_kernel, "own", (xs, tables["t0"], weights, row_mask), [VM] * 4,
        [(96, 8, 128), (96, 8, 128), (96, 8, 256), (8, 128)], [VM] * 4,
        [pltpu.VMEM((SEG, 8, 256), F32)],
    )
    rlow0, rhigh0, a1l, a1h, message, sum01 = _call(
        _rim_kernel, "rim",
        (sc, xs, from_left, from_right, low0, tables["t0r"], tables["t1"], weights, row_mask, lane_masks),
        [SM, VM, VM, VM, VM, ANY, ANY, VM, VM, VM],
        [(96, 8, 128), (96, 8, 128), (48, 8, 256), (48, 8, 256), (24, 8, 128), (2, 8, 128)], [VM] * 6,
        [
            pltpu.VMEM((2, 128, 128), BF16), pltpu.VMEM((2, 256, 256), BF16),
            pltpu.VMEM((SEG, 8, 128), F32), pltpu.VMEM((SEG, 8, 128), F32), pltpu.VMEM((96, 8, 256), F32),
            dma((2,)),
        ],
    )
    near = [_shift(message, by) for by in (2, 1, -1, -2)]
    a2l, a2h, a3l, a3h, a4l, a4h, a5l, a5h, payload = _call(
        _middle_kernel, "middle",
        (sc, message, *near, sum0, sum01, tables["t2"], tables["t3"], tables["t4"], tables["t5"],
         weights, row_mask, lane_masks, jnp.asarray(spots)),
        [SM] + [VM] * 7 + [ANY] * 4 + [VM] * 4,
        [(24, 8, 256)] * 2 + [(12, 8, 128)] * 2 + [(6, 8, 128)] * 2 + [(3, 8, 128)] * 2 + [(256, 128)], [VM] * 9,
        [
            pltpu.VMEM((2, 384, 256), BF16), pltpu.VMEM((2, 256, 128), BF16),
            pltpu.VMEM((2, 128, 128), BF16), pltpu.VMEM((2, 128, 256), BF16),
            pltpu.VMEM((48, 8, 384), F32), pltpu.VMEM((48, 8, 256), F32), pltpu.VMEM((24, 8, 128), F32),
            pltpu.VMEM((12, 8, 128), F32), pltpu.VMEM((6, 8, 256), F32), pltpu.VMEM((3, 8, 256), F32),
            dma((4,)),
        ],
    )
    everyone = lax.all_to_all(payload, ("chan", "tm"), split_axis=0, concat_axis=0, tiled=True)
    (out,) = _call(
        _back_kernel, "back",
        (sc, everyone, tables["w"], tables["v"], *(tables["s%d" % l] for l in range(6)), weights, jnp.asarray(cmask),
         dlow0, dhigh0, rlow0, rhigh0, a1l, a1h, a2l, a2h, a3l, a3h, a4l, a4h, a5l, a5h),
        [SM, VM, VM] + [ANY] * 7 + [VM] * 16,
        [(OWN, 256)], [ANY],
        [
            pltpu.VMEM((2, 128, 512), BF16),
            pltpu.VMEM((2, 384, 256), BF16), pltpu.VMEM((2, 256, 256), BF16), pltpu.VMEM((2, 256, 256), BF16),
            pltpu.VMEM((2, 128, 128), BF16), pltpu.VMEM((2, 128, 128), BF16), pltpu.VMEM((2, 128, 128), BF16),
            pltpu.VMEM((2, 128, 128), F32),
            pltpu.VMEM((6, 8, 128), F32), pltpu.VMEM((12, 8, 128), F32), pltpu.VMEM((24, 8, 128), F32),
            pltpu.VMEM((48, 8, 256), F32), pltpu.VMEM((96, 8, 256), F32), pltpu.VMEM((SEG, 8, 384), F32),
            pltpu.VMEM((6, 8, 128), F32), pltpu.VMEM((12, 8, 128), F32), pltpu.VMEM((24, 8, 128), F32),
            pltpu.VMEM((48, 8, 256), F32), pltpu.VMEM((96, 8, 256), F32),
            pltpu.VMEM((8 * SEG, 128), F32), pltpu.VMEM((8 * SEG, 128), F32),
            dma((9,)),
        ],
    )
    return out


def solution(mesh):
    return jax.shard_map(
        shards,
        mesh=mesh,
        in_specs=(P("chan", "tm"), P(), P()),
        out_specs=P("chan", "tm"),
        check_vma=False,
    )
```

time: 839 us -> 88.4 us (0.11); the launches traced: 828 us -> 87.8 us
  blocking collectives: 581 us -> 34.8 us
  local copies, waits for them, and re-layouts: 98.1 us -> 8.67 us
  starting transfers between devices: 66.5 us -> 20.8 us
  other arithmetic: 46.7 us -> 2.35 us
  between operations: 22.3 us -> 0.23 us
  Pallas kernels: 0 us -> 15.1 us
    all_gather x1 -> x0, blocking collectives: 287 us -> none  [shards(): current = lax.all_gather(current, 'tm', axis=1, tiled=True)]
    psum x2 -> x0, blocking collectives: 157 us -> none  [the longest x1 98.5 us: shards(): level_sums.append(lax.psum(local_sum, ('tm', 'chan')))]
    all_to_all x34 -> x1, blocking collectives: 137 us -> 34.8 us  [shards(): lax.all_to_all(payload, ('chan', 'tm'), split_axis=0, concat_axis=0, tile...]
    slice x274 -> x0, local copies, waits for them, and re-layouts: 77.2 us -> none  [the longest x6 21.3 us: shards(): widened[:, 1::2]]
    ppermute x24 -> x7, starting transfers between devices: 59 us -> 20.8 us  [the longest x6 17.5 us: _shift(): lax.ppermute(v, 'tm', [(i, i + by) for i in range(NT) if 0 <= i + by < NT])]
    pallas_call x0 -> x5, Pallas kernels: none -> 15.1 us  [_call(): pl.pallas_call(kernel, out_shape=[jax.ShapeDtypeStruct(s, F32) for s in o...]
    reshape x24 -> x1, local copies, waits for them, and re-layouts: 10.3 us -> 0.69 us  [shards(): kept.reshape(LEVELS, 8, 3).transpose(0, 2, 1)[..., None]]
  transfers between devices with their start and end apart: 26 -> 7, of which waited for: 6 -> 3; matrix products, arithmetic and copies ran while one was open for 3% -> 4% of each run, Pallas kernels for 0% -> 1%
where the time goes in v1:
time: 88.4 us; the launch traced here: 87.8 us
  blocking collectives  34.8 us (39%)
  starting transfers between devices  20.8 us (24%)
  Pallas kernels  15.1 us (17%)
  local copies, waits for them, and re-layouts  8.67 us (10%)
  waiting for transfers between devices  5.84 us (7%)
  other arithmetic  2.35 us (3%)
    all_to_all x1, blocking collectives, shards(): lax.all_to_all(payload, ('chan', 'tm'), split_axis=0, concat_axis=0, tile...  34.8 us
    ppermute x6, starting transfers between devices, _shift(): lax.ppermute(v, 'tm', [(i, i + by) for i in range(NT) if 0 <= i + by < NT])  17.5 us
    pallas_call x5, Pallas kernels, _call(): pl.pallas_call(kernel, out_shape=[jax.ShapeDtypeStruct(s, F32) for s in o...  15.1 us
    ppermute x6, waiting for transfers between devices, _shift(): lax.ppermute(v, 'tm', [(i, i + by) for i in range(NT) if 0 <= i + by < NT])  5.83 us
    unnamed x40, local copies, waits for them, and re-layouts  5.68 us
    ppermute x1, starting transfers between devices, shards(): recv = lax.ppermute(sent, 'chan', [(0, 1), (1, 0)])  3.32 us
  transfers between devices with their start and end apart: 7, of which 3 were waited for; matrix products, arithmetic and copies ran while one was open for 4% of the time, Pallas kernels for 1%

profile of v1, /device:TPU:1, one launch (start us, length us, event | category | flops | bytes accessed | tf_op | source)
XLA Modules:
  0.0 87.8 jit_solution(13144349545618843452)
XLA Ops:
  0.0 1.4 %slice_select_fusion = f32[512,256]{1,0:T(8,128)S(1)} fusion(f32[1024,256]{1,0:T(8,128)} %x.1, pred[]{:T(512)S(6)} %eq.26), kind=kLoop, calls=%fused_computation | loop fusion | flops 131072 | bytes 1572865 | tf_op jit(solution)/shard_map/jit(_where)/select_n | solution.py:723
  1.4 0.0 copy-start.7
  1.4 0.0 copy-start.16
  1.4 3.3 %collective-permute-start = (f32[512,256]{1,0:T(8,128)S(1)}, f32[512,256]{1,0:T(8,128)S(1)}, u32[]{:S(2)}, u32[]{:S(2)}) collective-permute-start(f32[512,256]{1,0:T(8,128)S(1)} %slice_select_fusion), channel_id=1, source_target_pairs={{0,1},{1,0},{2,3},{3,2},{4,5},{5,4},{6,7},{7,6},{8,9},{9,8},{10,11... | collective-permute-start | bytes 1572872 | tf_op jit(solution)/shard_map/ppermute | solution.py:724
  4.8 0.8 select_reduce_fusion
  5.5 0.1 slice_select_fusion.1
  5.6 0.7 reshape.9
  6.3 1.4 %copy.27 = f32[6,3,8]{2,1,0:T(4,128)} copy(f32[6,3,8]{1,2,0:T(8,128)} %bitcast.11) | data formatting | bytes 1152 | tf_op jit(solution)/shard_map/transpose | solution.py:708
  7.7 0.1 pad_add_fusion.sc
  7.8 0.0 collective-permute-done.recv
  7.8 0.0 copy-done.1
  7.8 1.6 %pack.1 = (f32[192,8,256]{2,1,0:T(8,128)S(1)}, f32[48,8,128]{2,1,0:T(8,128)S(1)}, f32[48,8,128]{2,1,0:T(8,128)S(1)}) custom-call(s32[4]{0:T(128)S(1)} %pad_add_fusion.sc, f32[1024,256]{1,0:T(8,128)S(1)} %copy-done.1, f32[512,256]{1,0:T(8,128)S(1)} %collective-permute-done.recv), custom_call_target="tpu_custom_call" | custom-call | tf_op jit(solution)/shard_map/pack/pallas_call | solution.py:682
  9.5 1.8 %collective-permute-start.1 = (f32[48,8,128]{2,1,0:T(8,128)S(1)}, f32[48,8,128]{2,1,0:T(8,128)S(1)}, u32[]{:S(2)}, u32[]{:S(2)}) collective-permute-start(f32[48,8,128]{2,1,0:T(8,128)S(1)} %get-tuple-element.28), channel_id=1, source_target_pairs={{0,2},{2,4},{4,6},{6,8},{8,10},{10,12},{12,14},{14,16},{16,18},{18... | collective-permute-start | bytes 589832 | tf_op jit(solution)/shard_map/ppermute | solution.py:694
  11.3 1.3 %collective-permute-start.2 = (f32[48,8,128]{2,1,0:T(8,128)S(1)}, f32[48,8,128]{2,1,0:T(8,128)S(1)}, u32[]{:S(2)}, u32[]{:S(2)}) collective-permute-start(f32[48,8,128]{2,1,0:T(8,128)S(1)} %get-tuple-element.29), channel_id=1, source_target_pairs={{2,0},{4,2},{6,4},{8,6},{10,8},{12,10},{14,12},{16,14},{18,16},{20... | collective-permute-start | bytes 589832 | tf_op jit(solution)/shard_map/ppermute | solution.py:694
  12.6 0.0 copy-done.19
  12.7 0.1 broadcast_in_dim.5.rows
  12.7 0.8 broadcast_in_dim.4.w
  13.5 0.0 copy-start.11
  13.5 0.9 %copy-done.11 = bf16[2,256,256]{2,1,0:T(8,128)(2,1)S(1)} copy-done((bf16[2,256,256]{2,1,0:T(8,128)(2,1)S(1)}, bf16[2,256,256]{2,1,0:T(8,128)(2,1)}, u32[]{:S(2)}) %copy-start.11) | copy-done | bytes 262168
  14.5 1.0 %own.1 = (f32[96,8,128]{2,1,0:T(8,128)S(1)}, f32[96,8,128]{2,1,0:T(8,128)S(1)}, f32[96,8,256]{2,1,0:T(8,128)S(1)}, f32[8,128]{1,0:T(8,128)S(1)}) custom-call(f32[192,8,256]{2,1,0:T(8,128)S(1)} %get-tuple-element.27.xs, bf16[2,256,256]{2,1,0:T(8,128)(2,1)S(1)} %copy-done.11, f32[6,3,8,128]{3,2,1,0:T(8,128)S(1)} %broadcast_in_dim.4.w, ...), custom_call_target="tpu_custom_call" | custom-call | tf_op jit(solution)/shard_map/own/pallas_call | solution.py:682
  15.5 0.0 copy-start.2
  15.5 0.1 collective-permute-done.1.from_left
  15.5 4.2 %collective-permute-done.2.from_right = f32[48,8,128]{2,1,0:T(8,128)S(1)} collective-permute-done((f32[48,8,128]{2,1,0:T(8,128)S(1)}, f32[48,8,128]{2,1,0:T(8,128)S(1)}, u32[]{:S(2)}, u32[]{:S(2)}) %collective-permute-start.2) | collective-permute-done | bytes 196640 | tf_op jit(solution)/shard_map/ppermute | solution.py:694
  19.7 0.0 copy-done.7
  19.7 0.0 copy-done.16
  19.7 0.9 %copy-done.12 = bf16[3,2,128,128]{3,2,1,0:T(8,128)(2,1)S(1)} copy-done((bf16[3,2,128,128]{3,2,1,0:T(8,128)(2,1)S(1)}, bf16[3,2,128,128]{3,2,1,0:T(8,128)(2,1)}, u32[]{:S(2)}) %copy-start.12) | copy-done | bytes 196632
  20.7 2.2 %rim.1 = (f32[96,8,128]{2,1,0:T(8,128)S(1)}, f32[96,8,128]{2,1,0:T(8,128)S(1)}, f32[48,8,256]{2,1,0:T(8,128)S(1)}, f32[48,8,256]{2,1,0:T(8,128)S(1)}, f32[24,8,1...) custom-call(s32[4]{0:T(128)S(1)} %pad_add_fusion.sc, f32[192,8,256]{2,1,0:T(8,128)S(1)} %get-tuple-element.27.xs, ...), custom_call_target="tpu_custom_call" | custom-call | tf_op jit(solution)/shard_map/rim/pallas_call | solution.py:682
  22.9 1.3 %collective-permute-start.6 = (f32[24,8,128]{2,1,0:T(8,128)S(1)}, f32[24,8,128]{2,1,0:T(8,128)S(1)}, u32[]{:S(2)}, u32[]{:S(2)}) collective-permute-start(f32[24,8,128]{2,1,0:T(8,128)S(1)} %get-tuple-element.31.own), channel_id=1, source_target_pairs={{4,0},{6,2},{8,4},{10,6},{12,8},{14,10},{16,12},{18,14},{20,16},{2... | collective-permute-start | bytes 294920 | tf_op jit(solution)/shard_map/ppermute | solution.py:694
  24.2 1.3 %collective-permute-start.5 = (f32[24,8,128]{2,1,0:T(8,128)S(1)}, f32[24,8,128]{2,1,0:T(8,128)S(1)}, u32[]{:S(2)}, u32[]{:S(2)}) collective-permute-start(f32[24,8,128]{2,1,0:T(8,128)S(1)} %get-tuple-element.31.own), channel_id=1, source_target_pairs={{2,0},{4,2},{6,4},{8,6},{10,8},{12,10},{14,12},{16,14},{18,16},{20... | collective-permute-start | bytes 294920 | tf_op jit(solution)/shard_map/ppermute | solution.py:694
  25.5 4.2 %collective-permute-start.4 = (f32[24,8,128]{2,1,0:T(8,128)S(1)}, f32[24,8,128]{2,1,0:T(8,128)S(1)}, u32[]{:S(2)}, u32[]{:S(2)}) collective-permute-start(f32[24,8,128]{2,1,0:T(8,128)S(1)} %get-tuple-element.31.own), channel_id=1, source_target_pairs={{0,2},{2,4},{4,6},{6,8},{8,10},{10,12},{12,14},{14,16},{16,18},{18... | collective-permute-start | bytes 294920 | tf_op jit(solution)/shard_map/ppermute | solution.py:694
  29.7 7.6 %collective-permute-start.3 = (f32[24,8,128]{2,1,0:T(8,128)S(1)}, f32[24,8,128]{2,1,0:T(8,128)S(1)}, u32[]{:S(2)}, u32[]{:S(2)}) collective-permute-start(f32[24,8,128]{2,1,0:T(8,128)S(1)} %get-tuple-element.31.own), channel_id=1, source_target_pairs={{0,4},{2,6},{4,8},{6,10},{8,12},{10,14},{12,16},{14,18},{16,20},{1... | collective-permute-start | bytes 294920 | tf_op jit(solution)/shard_map/ppermute | solution.py:694
  37.3 0.0 collective-permute-done.6.p2
  37.3 0.0 collective-permute-done.5.p1
  37.3 0.0 collective-permute-done.4.m1
  37.3 1.6 %collective-permute-done.3.m2 = f32[24,8,128]{2,1,0:T(8,128)S(1)} collective-permute-done((f32[24,8,128]{2,1,0:T(8,128)S(1)}, f32[24,8,128]{2,1,0:T(8,128)S(1)}, u32[]{:S(2)}, u32[]{:S(2)}) %collective-permute-start.3) | collective-permute-done | bytes 98336 | tf_op jit(solution)/shard_map/ppermute | solution.py:694
  38.9 0.0 copy-done.9
  38.9 0.0 copy-done.18
  38.9 0.0 copy-done.8
  38.9 0.0 copy-start.10
  38.9 1.0 %copy-done.10 = bf16[5,2,128,128]{3,2,1,0:T(8,128)(2,1)S(1)} copy-done((bf16[5,2,128,128]{3,2,1,0:T(8,128)(2,1)S(1)}, bf16[5,2,128,128]{3,2,1,0:T(8,128)(2,1)}, u32[]{:S(2)}) %copy-start.10) | copy-done | bytes 327704
  39.9 2.7 %middle.1 = (f32[24,8,256]{2,1,0:T(8,128)S(1)}, f32[24,8,256]{2,1,0:T(8,128)S(1)}, f32[12,8,128]{2,1,0:T(8,128)S(1)}, f32[12,8,128]{2,1,0:T(8,128)S(1)}, f32[6,8...) custom-call(s32[4]{0:T(128)S(1)} %pad_add_fusion.sc, ...), custom_call_target="tpu_custom_call" | custom-call | tf_op jit(solution)/shard_map/middle/pallas_call | solution.py:682
  42.6 34.8 %all_to_all.11 = f32[256,1,128]{2,1,0:T(1,128)S(1)} all-to-all(f32[256,1,128]{2,1,0:T(1,128)S(1)} %bitcast.10), channel_id=1, replica_groups=mesh['tm'=128,'chan'=2] {'chan','tm'}, dimensions={0} | all-to-all | bytes 262144 | tf_op jit(solution)/shard_map/all_to_all | solution.py:763
  77.4 0.0 copy-done.4
  77.5 0.0 copy-start.13
  77.5 0.9 %copy-done.13 = bf16[3,2,128,128]{3,2,1,0:T(8,128)(2,1)S(1)} copy-done((bf16[3,2,128,128]{3,2,1,0:T(8,128)(2,1)S(1)}, bf16[3,2,128,128]{3,2,1,0:T(8,128)(2,1)}, u32[]{:S(2)}) %copy-start.13) | copy-done | bytes 196632
  78.4 0.9 %copy-done.14 = bf16[3,2,128,128]{3,2,1,0:T(8,128)(2,1)S(1)} copy-done((bf16[3,2,128,128]{3,2,1,0:T(8,128)(2,1)S(1)}, bf16[3,2,128,128]{3,2,1,0:T(8,128)(2,1)}, u32[]{:S(2)}) %copy-start.14) | copy-done | bytes 196632
  79.3 0.9 %copy-done.15 = bf16[3,2,128,128]{3,2,1,0:T(8,128)(2,1)S(1)} copy-done((bf16[3,2,128,128]{3,2,1,0:T(8,128)(2,1)S(1)}, bf16[3,2,128,128]{3,2,1,0:T(8,128)(2,1)}, u32[]{:S(2)}) %copy-start.15) | copy-done | bytes 196632
  80.3 7.6 %back.1 = f32[1024,256]{1,0:T(8,128)} custom-call(s32[4]{0:T(128)S(1)} %pad_add_fusion.sc, f32[256,128]{1,0:T(8,128)S(1)} %bitcast.9, bf16[2,512,512]{2,1,0:T(8,128)(2,1)S(1)} %copy-done.4, bf16[128,2,16,512]{3,2,1,0:T(8,128)(2,1)S(1)} %copy-done, bf16[3,2,384,256]{3,2,1,0:T(8,128)(2,1)S(1)} %copy-done.3, bf16[3,2,256,256]{3,2,1,0:T(8,128)(2,1)S(1)} %copy-done.6, ...), custom_call_target="tpu_custom_call" | custom-call | tf_op jit(solution)/shard_map/back/pallas_call | solution.py:682
  (21 shorter events, 0.0 us)
Async XLA Ops:
  0.0 12.6 %copy-start.19 = (f32[3,8]{1,0:T(4,128)S(1)}, f32[3,8]{1,0:T(4,128)}, u32[]{:S(2)}) copy-start(f32[3,8]{1,0:T(4,128)} %constant.63.clone) | copy-start | bytes 292
  0.0 7.8 %copy-start.1 = (f32[1024,256]{1,0:T(8,128)S(1)}, f32[1024,256]{1,0:T(8,128)}, u32[]{:S(2)}) copy-start(f32[1024,256]{1,0:T(8,128)} %x.1) | copy-start | bytes 3145732
  0.0 38.9 %copy-start.9 = (bf16[5,2,256,128]{3,2,1,0:T(8,128)(2,1)S(1)}, bf16[5,2,256,128]{3,2,1,0:T(8,128)(2,1)}, u32[]{:S(2)}) copy-start(bf16[5,2,256,128]{3,2,1,0:T(8,128)(2,1)} %constant.70.clone.t3_all) | copy-start | bytes 1966084
  1.4 18.3 %copy-start.7 = (bf16[3,2,256,256]{3,2,1,0:T(8,128)(2,1)S(1)}, bf16[3,2,256,256]{3,2,1,0:T(8,128)(2,1)}, u32[]{:S(2)}) copy-start(bf16[3,2,256,256]{3,2,1,0:T(8,128)(2,1)} %constant.67.clone.t1_all) | copy-start | bytes 2359300
  1.4 18.3 %copy-start.16 = (f32[16,128]{1,0:T(8,128)S(1)}, f32[16,128]{1,0:T(8,128)}, u32[]{:S(2)}) copy-start(f32[16,128]{1,0:T(8,128)} %constant.64.clone.lanes) | copy-start | bytes 24580
  1.4 6.4 %collective-permute-start = (f32[512,256]{1,0:T(8,128)S(1)}, f32[512,256]{1,0:T(8,128)S(1)}, u32[]{:S(2)}, u32[]{:S(2)}) collective-permute-start(f32[512,256]{1,0:T(8,128)S(1)} %slice_select_fusion), channel_id=1, source_target_pairs={{0,1},{1,0},{2,3},{3,2},{4,5},{5,4},{6,7},{7,6},{8,9},{9,8},{10,11... | collective-permute-start | bytes 1572872 | tf_op jit(solution)/shard_map/ppermute | solution.py:724
  7.8 69.6 %copy-start.6 = (bf16[3,2,256,256]{3,2,1,0:T(8,128)(2,1)S(1)}, bf16[3,2,256,256]{3,2,1,0:T(8,128)(2,1)}, u32[]{:S(2)}) copy-start(bf16[3,2,256,256]{3,2,1,0:T(8,128)(2,1)} %constant.77.clone.s1_all) | copy-start | bytes 2359300
  9.5 6.1 %collective-permute-start.1 = (f32[48,8,128]{2,1,0:T(8,128)S(1)}, f32[48,8,128]{2,1,0:T(8,128)S(1)}, u32[]{:S(2)}, u32[]{:S(2)}) collective-permute-start(f32[48,8,128]{2,1,0:T(8,128)S(1)} %get-tuple-element.28), channel_id=1, source_target_pairs={{0,2},{2,4},{4,6},{6,8},{8,10},{10,12},{12,14},{14,16},{16,18},{18... | collective-permute-start | bytes 589832 | tf_op jit(solution)/shard_map/ppermute | solution.py:694
  11.3 8.4 %collective-permute-start.2 = (f32[48,8,128]{2,1,0:T(8,128)S(1)}, f32[48,8,128]{2,1,0:T(8,128)S(1)}, u32[]{:S(2)}, u32[]{:S(2)}) collective-permute-start(f32[48,8,128]{2,1,0:T(8,128)S(1)} %get-tuple-element.29), channel_id=1, source_target_pairs={{2,0},{4,2},{6,4},{8,6},{10,8},{12,10},{14,12},{16,14},{18,16},{20... | collective-permute-start | bytes 589832 | tf_op jit(solution)/shard_map/ppermute | solution.py:694
  12.7 26.1 %copy-start.18 = (f32[3,8,128]{2,1,0:T(8,128)S(1)}, f32[3,8,128]{2,1,0:T(8,128)}, u32[]{:S(2)}) copy-start(f32[3,8,128]{2,1,0:T(8,128)} %constant.68.clone.place) | copy-start | bytes 36868
  13.5 1.0 %copy-start.11 = (bf16[2,256,256]{2,1,0:T(8,128)(2,1)S(1)}, bf16[2,256,256]{2,1,0:T(8,128)(2,1)}, u32[]{:S(2)}) copy-start(bf16[2,256,256]{2,1,0:T(8,128)(2,1)} %constant.65.clone.t) | copy-start | bytes 786436
  14.5 24.4 %copy-start.8 = (bf16[5,2,128,256]{3,2,1,0:T(8,128)(2,1)S(1)}, bf16[5,2,128,256]{3,2,1,0:T(8,128)(2,1)}, u32[]{:S(2)}) copy-start(bf16[5,2,128,256]{3,2,1,0:T(8,128)(2,1)} %constant.72.clone.t5_all) | copy-start | bytes 1966084
  14.5 63.0 %copy-start.4 = (bf16[2,512,512]{2,1,0:T(8,128)(2,1)S(1)}, bf16[2,512,512]{2,1,0:T(8,128)(2,1)}, u32[]{:S(2)}) copy-start(bf16[2,512,512]{2,1,0:T(8,128)(2,1)} %constant.74.clone.w_all) | copy-start | bytes 3145732
  14.5 63.0 %copy-start.5 = (bf16[3,2,256,256]{3,2,1,0:T(8,128)(2,1)S(1)}, bf16[3,2,256,256]{3,2,1,0:T(8,128)(2,1)}, u32[]{:S(2)}) copy-start(bf16[3,2,256,256]{3,2,1,0:T(8,128)(2,1)} %constant.78.clone.s2_all) | copy-start | bytes 2359300
  15.5 23.4 %copy-start.2 = (bf16[5,2,384,256]{3,2,1,0:T(8,128)(2,1)S(1)}, bf16[5,2,384,256]{3,2,1,0:T(8,128)(2,1)}, u32[]{:S(2)}) copy-start(bf16[5,2,384,256]{3,2,1,0:T(8,128)(2,1)} %constant.69.clone.t2_all) | copy-start | bytes 5898244
  19.7 0.9 %copy-start.12 = (bf16[3,2,128,128]{3,2,1,0:T(8,128)(2,1)S(1)}, bf16[3,2,128,128]{3,2,1,0:T(8,128)(2,1)}, u32[]{:S(2)}) copy-start(bf16[3,2,128,128]{3,2,1,0:T(8,128)(2,1)} %constant.66.clone.t0r_all) | copy-start | bytes 589828
  20.7 56.8 %copy-start.3 = (bf16[3,2,384,256]{3,2,1,0:T(8,128)(2,1)S(1)}, bf16[3,2,384,256]{3,2,1,0:T(8,128)(2,1)}, u32[]{:S(2)}) copy-start(bf16[3,2,384,256]{3,2,1,0:T(8,128)(2,1)} %constant.76.clone.s0_all) | copy-start | bytes 3538948
  22.9 14.4 %collective-permute-start.6 = (f32[24,8,128]{2,1,0:T(8,128)S(1)}, f32[24,8,128]{2,1,0:T(8,128)S(1)}, u32[]{:S(2)}, u32[]{:S(2)}) collective-permute-start(f32[24,8,128]{2,1,0:T(8,128)S(1)} %get-tuple-element.31.own), channel_id=1, source_target_pairs={{4,0},{6,2},{8,4},{10,6},{12,8},{14,10},{16,12},{18,14},{20,16},{2... | collective-permute-start | bytes 294920 | tf_op jit(solution)/shard_map/ppermute | solution.py:694
  24.2 13.1 %collective-permute-start.5 = (f32[24,8,128]{2,1,0:T(8,128)S(1)}, f32[24,8,128]{2,1,0:T(8,128)S(1)}, u32[]{:S(2)}, u32[]{:S(2)}) collective-permute-start(f32[24,8,128]{2,1,0:T(8,128)S(1)} %get-tuple-element.31.own), channel_id=1, source_target_pairs={{2,0},{4,2},{6,4},{8,6},{10,8},{12,10},{14,12},{16,14},{18,16},{20... | collective-permute-start | bytes 294920 | tf_op jit(solution)/shard_map/ppermute | solution.py:694
  25.5 11.8 %collective-permute-start.4 = (f32[24,8,128]{2,1,0:T(8,128)S(1)}, f32[24,8,128]{2,1,0:T(8,128)S(1)}, u32[]{:S(2)}, u32[]{:S(2)}) collective-permute-start(f32[24,8,128]{2,1,0:T(8,128)S(1)} %get-tuple-element.31.own), channel_id=1, source_target_pairs={{0,2},{2,4},{4,6},{6,8},{8,10},{10,12},{12,14},{14,16},{16,18},{18... | collective-permute-start | bytes 294920 | tf_op jit(solution)/shard_map/ppermute | solution.py:694
  29.7 9.2 %collective-permute-start.3 = (f32[24,8,128]{2,1,0:T(8,128)S(1)}, f32[24,8,128]{2,1,0:T(8,128)S(1)}, u32[]{:S(2)}, u32[]{:S(2)}) collective-permute-start(f32[24,8,128]{2,1,0:T(8,128)S(1)} %get-tuple-element.31.own), channel_id=1, source_target_pairs={{0,4},{2,6},{4,8},{6,10},{8,12},{10,14},{12,16},{14,18},{16,20},{1... | collective-permute-start | bytes 294920 | tf_op jit(solution)/shard_map/ppermute | solution.py:694
  38.9 1.0 %copy-start.10 = (bf16[5,2,128,128]{3,2,1,0:T(8,128)(2,1)S(1)}, bf16[5,2,128,128]{3,2,1,0:T(8,128)(2,1)}, u32[]{:S(2)}) copy-start(bf16[5,2,128,128]{3,2,1,0:T(8,128)(2,1)} %constant.71.clone.t4_all) | copy-start | bytes 983044
  39.9 37.6 %copy-start = (bf16[128,2,16,512]{3,2,1,0:T(8,128)(2,1)S(1)}, bf16[128,2,16,512]{3,2,1,0:T(8,128)(2,1)}, u32[]{:S(2)}) copy-start(bf16[128,2,16,512]{3,2,1,0:T(8,128)(2,1)} %constant.75.clone.v_all) | copy-start | bytes 12582916
  39.9 37.6 %copy-start.17 = (f32[48,128]{1,0:T(8,128)S(1)}, f32[48,128]{1,0:T(8,128)}, u32[]{:S(2)}) copy-start(f32[48,128]{1,0:T(8,128)} %constant.73.clone.cmask) | copy-start | bytes 73732
  77.5 0.9 %copy-start.13 = (bf16[3,2,128,128]{3,2,1,0:T(8,128)(2,1)S(1)}, bf16[3,2,128,128]{3,2,1,0:T(8,128)(2,1)}, u32[]{:S(2)}) copy-start(bf16[3,2,128,128]{3,2,1,0:T(8,128)(2,1)} %constant.81.clone.s5_all) | copy-start | bytes 589828
  78.4 0.9 %copy-start.14 = (bf16[3,2,128,128]{3,2,1,0:T(8,128)(2,1)S(1)}, bf16[3,2,128,128]{3,2,1,0:T(8,128)(2,1)}, u32[]{:S(2)}) copy-start(bf16[3,2,128,128]{3,2,1,0:T(8,128)(2,1)} %constant.80.clone.s4_all) | copy-start | bytes 589828
  79.3 0.9 %copy-start.15 = (bf16[3,2,128,128]{3,2,1,0:T(8,128)(2,1)S(1)}, bf16[3,2,128,128]{3,2,1,0:T(8,128)(2,1)}, u32[]{:S(2)}) copy-start(bf16[3,2,128,128]{3,2,1,0:T(8,128)(2,1)} %constant.79.clone.s3_all) | copy-start | bytes 589828

commit v2 on v1

v2 whole, which is shorter than its diff:
```python
import functools

import jax
import jax.numpy as jnp
import ml_dtypes
import numpy as np
from jax import lax
from jax.experimental import pallas as pl
from jax.experimental.pallas import tpu as pltpu
from jax.sharding import PartitionSpec as P

LEVELS = 6
COARSE = 6
GTAB = 8
NBLK = 32
C = 2048
S = 32768
NT = 128
OWN = 1024
HALO = 512
SEG = 192
A1 = -1.586134342059924
B1 = -0.052980118572961
A2 = 0.882911075530934
B2 = 0.443506852043971
KS = 1.149604398860241
FLOOR = 1e-06
F32 = jnp.float32
BF16 = jnp.bfloat16


def _next(e):
    return np.concatenate((e[1:], e[-1:]))


def _prev(o):
    return np.concatenate((o[:1], o[:-1]))


def _lift(x):
    e, o = x[0::2], x[1::2]
    o = o + A1 * (e + _next(e))
    e = e + B1 * (_prev(o) + o)
    o = o + A2 * (e + _next(e))
    e = e + B2 * (_prev(o) + o)
    return KS * e, o / KS


def _unlift(low, high):
    e, o = low / KS, high * KS
    e = e - B2 * (_prev(o) + o)
    o = o - A2 * (e + _next(e))
    e = e - B1 * (_prev(o) + o)
    o = o - A1 * (e + _next(e))
    return np.stack((e, o), axis=1).reshape((2 * e.shape[0],) + e.shape[1:])


def _forward(inputs, lows, highs, rows, cols, start, stop, scale):
    pairs = list(lows) + list(highs)
    a = max(2 * min(pairs) - 16, start)
    b = min(2 * max(pairs) + 16, stop)
    low, high = _lift(np.eye(b - a))
    out = np.zeros((rows, cols))
    for band, places in ((low, lows), (high, highs)):
        for pair, col in places.items():
            if a <= 2 * pair < b:
                line = band[pair - a // 2]
                for i in np.nonzero(line)[0]:
                    out[inputs[a + int(i)], col] += scale * line[i]
    return out


def _inverse(lows, highs, outputs, rows, cols, start, stop, scale):
    a = max(2 * (min(outputs) // 2) - 16, start) // 2
    b = min(2 * (max(outputs) // 2) + 18, stop) // 2
    n = b - a
    eye, zero = np.eye(n), np.zeros((n, n))
    from_low, from_high = _unlift(eye, zero), _unlift(zero, eye)
    out = np.zeros((rows, cols))
    for sample, col in outputs.items():
        if 2 * a <= sample < 2 * b:
            for lines, places in ((from_low, lows), (from_high, highs)):
                line = lines[sample - 2 * a]
                for i in np.nonzero(line)[0]:
                    out[places[a + int(i)], col] += scale * line[i]
    return out


def _pair(m):
    hi = m.astype(ml_dtypes.bfloat16)
    lo = (m - hi.astype(np.float64)).astype(ml_dtypes.bfloat16)
    return np.stack((hi, lo))


def _run(first, last, at):
    return {k: at + k - first for k in range(first, last)}


OWN_LOW0 = _run(2, 126, 2)
OWN_HIGH0 = _run(2, 126, 130)
RIM_LOW0 = {**_run(-10, 2, 0), **_run(126, 137, 12)}
RIM_HIGH0 = {**_run(-2, 2, 32), **_run(126, 130, 36)}
RIM_IN0 = {**_run(0, 32, 0), **_run(-32, 0, 32), **_run(256, 288, 64), **_run(224, 256, 96)}
OWN_LOW1 = _run(3, 61, 3)
OWN_HIGH1 = _run(2, 61, 66)
RIM_LOW1 = {**_run(-3, 3, 64), **_run(61, 67, 70)}
RIM_HIGH1 = {**_run(-3, 2, 80), **_run(61, 67, 85)}
IN1 = {**OWN_LOW0, **{k: 128 + v for k, v in RIM_LOW0.items()}}
IN2 = {
    **OWN_LOW1, **_run(67, 125, 67), **_run(-61, -3, 131), **{k: 128 + v for k, v in RIM_LOW1.items()}
}
LOW2 = _run(-28, 57, 0)
HIGH2 = _run(-3, 36, 85)
LOW3 = _run(-12, 27, 0)
HIGH3 = _run(-3, 20, 64)
LOW4 = _run(-4, 12, 0)
HIGH4 = _run(-3, 12, 32)
LOW5 = {4 * (d - 1) + i: 4 * i + d for i in range(4) for d in range(3)}
HIGH5 = {k: 32 + v for k, v in LOW5.items()}


def _part(places, first, last):
    return {k: places[k] for k in range(first, last)}


def _edges(width):
    far = 1 << 20
    return ((0, far), (-far, far), (-far, width))


def _bundle(parts, rows):
    out = np.zeros((rows, 256))
    for r, c, m in parts:
        out[r : r + m.shape[0], c : c + m.shape[1]] = m
    return _pair(out)


@functools.cache
def _tables():
    fw, inv = _forward, _inverse
    far = 1 << 20
    out = {}
    out["own"] = _bundle(
        (
            (0, 0, fw(_run(0, 256, 0), OWN_LOW0, OWN_HIGH0, 256, 256, -far, far, 1.0)),
            (256, 0, fw(OWN_LOW0, OWN_LOW1, OWN_HIGH1, 128, 128, -far, far, KS)),
        ),
        384,
    )
    rim, back = [], []
    for v in range(3):
        a, b = zip(*(_edges(256 >> l)[v] for l in range(LEVELS)))
        t5 = fw(LOW4, _part(LOW5, 0, 4), _part(HIGH5, 0, 4), 128, 256, a[5], b[5], KS)
        for i in range(128):
            t5[:, 128 + i] = t5[:, LOW5[i % 4]]
        rim.append(
            _bundle(
                (
                    (0, 0, fw(IN1, RIM_LOW1, RIM_HIGH1, 256, 128, a[1], b[1], KS)),
                    (0, 128, fw(IN2, LOW2, HIGH2, 256, 128, a[2], b[2], KS)),
                    (256, 0, fw(RIM_IN0, RIM_LOW0, RIM_HIGH0, 128, 128, a[0], b[0], 1.0)),
                    (256, 128, fw(LOW2, LOW3, HIGH3, 128, 128, a[3], b[3], KS)),
                    (384, 0, t5),
                    (512, 0, fw(LOW3, LOW4, HIGH4, 128, 128, a[4], b[4], KS)),
                ),
                640,
            )
        )
        low0 = {**OWN_LOW0, **{k: 256 + v for k, v in RIM_LOW0.items() if -2 <= k < 130}}
        high0 = {**OWN_HIGH0, **{k: 256 + v for k, v in RIM_HIGH0.items()}}
        low1 = {**OWN_LOW1, **{k: 128 + v for k, v in RIM_LOW1.items()}}
        high1 = {**OWN_HIGH1, **{k: 128 + v for k, v in RIM_HIGH1.items()}}
        back.append(
            _bundle(
                (
                    (0, 0, inv(low0, high0, _run(0, 256, 0), 384, 256, a[0], b[0], 1.0)),
                    (384, 0, inv(low1, high1, _part(IN1, -1, 130), 256, 256, a[1], b[1], 1.0 / KS)),
                    (640, 0, inv(LOW2, HIGH2, _part(low1, -2, 67), 128, 256, a[2], b[2], 1.0 / KS)),
                    (768, 0, inv(LOW3, HIGH3, _part(LOW2, -2, 36), 128, 128, a[3], b[3], 1.0 / KS)),
                    (768, 128, inv(LOW4, HIGH4, _part(LOW3, -2, 20), 128, 128, a[4], b[4], 1.0 / KS)),
                    (896, 0, inv(LOW5, HIGH5, _part(LOW4, -2, 12), 128, 128, a[5], b[5], 1.0 / KS)),
                ),
                1024,
            )
        )
    out["rim"], out["back"] = np.stack(rim), np.stack(back)
    n = S >> LEVELS
    bands = []
    current = np.eye(n)
    for _ in range(COARSE):
        current, high = _lift(current)
        bands.append(high)
    coarse = np.concatenate([current] + bands[::-1])
    order = (np.arange(n) % NT) * 4 + np.arange(n) // NT
    out["w"] = _pair((KS * coarse.T)[order])
    last = n >> COARSE
    current = np.eye(n)[:last]
    for step in range(COARSE):
        size = last << step
        current = _unlift(current, np.eye(n)[size : 2 * size])
    rebuilt = np.zeros((n + 8, n))
    rebuilt[4 : n + 4] = current / KS
    rebuilt = _pair(rebuilt)
    pieces = np.zeros((NT, 2, 16, n), ml_dtypes.bfloat16)
    for k, lane in LOW5.items():
        pieces[:, :, lane] = np.moveaxis(rebuilt[:, 4 + k : 4 + k + n : 4], 0, 1)
    out["v"] = pieces
    return out


def _mask(lane, places, first, last, base=0):
    lanes = sorted(v - base for k, v in places.items() if first <= k < last)
    out, i = None, 0
    while i < len(lanes):
        j = i
        while j + 1 < len(lanes) and lanes[j + 1] == lanes[j] + 1:
            j += 1
        hit = (lane >= lanes[i]) & (lane <= lanes[j])
        out = hit if out is None else out | hit
        i = j + 1
    return out


def _ones(hit):
    return jnp.where(hit, 1.0, 0.0)


def _dot3(x, t):
    hi = x.astype(BF16)
    lo = (x - hi.astype(F32)).astype(BF16)
    d = functools.partial(jnp.dot, preferred_element_type=F32)
    return d(hi, t(0)) + d(lo, t(0)) + d(hi, t(1))


def _time(load, t, y, step, j):
    x = load(j, step)
    y[pl.ds(j, step)] = _dot3(x.reshape(step * 8, x.shape[2]), t).reshape(step, 8, y.shape[2])


class _Forward:
    def __init__(self, load, t, y, step):
        self.load, self.t, self.y, self.step, self.done = load, t, y, step, 0

    def __call__(self, j):
        ahead = min(j + self.step, self.y.shape[0] - 1)
        while self.done <= ahead:
            _time(self.load, self.t, self.y, self.step, self.done)
            self.done += self.step
        return self.y[j]


class _Backward:
    def __init__(self, y, t, store, step):
        self.y, self.t, self.store, self.step, self.left = y, t, store, step, {}

    def __call__(self, j, value):
        self.y[j] = value
        chunk = j // self.step
        self.left[chunk] = self.left.get(chunk, self.step) - 1
        if not self.left[chunk]:
            x = self.y[pl.ds(chunk * self.step, self.step)]
            out = _dot3(x.reshape(self.step * 8, x.shape[2]), self.t)
            self.store(chunk * self.step, self.step, out.reshape(self.step, 8, out.shape[1]))


def _table(ref, rows, cols, *lead):
    r, c = pl.ds(*rows), pl.ds(*cols)
    return lambda i: ref[(*lead, i, r, c)]


def _sublane(lanes):
    return lax.broadcasted_iota(jnp.int32, (8, lanes), 0)


def _lane(rows=8):
    return lax.broadcasted_iota(jnp.int32, (rows, 128), 1)


def _wide(v, lanes):
    return v if lanes == 128 else jnp.concatenate([v] * (lanes // 128), axis=1)


class _Wrap:
    def __init__(self, lanes):
        sub = _sublane(lanes)
        self.last, self.first = sub == 7, sub == 0

    def after(self, first, last):
        return jnp.where(self.last, last, pltpu.roll(first, 7, 0))

    def before(self, last, first):
        return jnp.where(self.first, first, pltpu.roll(last, 1, 0))


def _coefs(w_ref, level, lanes):
    return [[_wide(c * w_ref[level, q], lanes) for q in range(3)] for c in (A1, B1, A2, B2)]


def _chan_forward(get, n, w_ref, level, lanes, put_low, put_high):
    wrap = _Wrap(lanes)
    ca, cb, cc, cd = _coefs(w_ref, level, lanes)
    per = n // 3
    first = get(0)
    e, o1, e1, o2 = {0: first}, {}, {}, {}

    def high(k, v):
        o2[k] = v
        put_high(k, k // per, v)

    def low(k):
        put_low(k, k // per, e1[k] + cd[k // per] * (o2[k - 1] + o2[k]))

    for k in range(n):
        q = k // per
        e[k + 1] = get(2 * k + 2) if k + 1 < n else wrap.after(first, e[k])
        o1[k] = get(2 * k + 1) + ca[q] * (e[k] + e[k + 1])
        if k >= 1:
            e1[k] = e[k] + cb[q] * (o1[k - 1] + o1[k])
        if k >= 2:
            high(k - 1, o1[k - 1] + cc[(k - 1) // per] * (e1[k - 1] + e1[k]))
        if k >= 3:
            low(k - 1)
    e1[0] = first + cb[0] * (wrap.before(o1[n - 1], o1[0]) + o1[0])
    high(0, o1[0] + cc[0] * (e1[0] + e1[1]))
    high(n - 1, o1[n - 1] + cc[2] * (e1[n - 1] + wrap.after(e1[0], e1[n - 1])))
    o2[-1] = wrap.before(o2[n - 1], o2[0])
    for k in (0, 1, n - 1):
        low(k)


def _chan_inverse(get_low, get_high, n, w_ref, level, lanes, put):
    wrap = _Wrap(lanes)
    ca, cb, cc, cd = _coefs(w_ref, level, lanes)
    per = n // 3
    o = {0: get_high(0)}
    o[-1] = wrap.before(get_high(n - 1), o[0])
    e1, o1, e2 = {}, {}, {}

    def even(k):
        e2[k] = e1[k] - cb[k // per] * (o1[k - 1] + o1[k])
        put(2 * k, e2[k])

    def odd(k):
        put(2 * k + 1, o1[k] - ca[k // per] * (e2[k] + e2[k + 1]))

    for k in range(n):
        q = k // per
        if k:
            o[k] = get_high(k)
        e1[k] = get_low(k) - cd[q] * (o[k - 1] + o[k])
        if k >= 1:
            o1[k - 1] = o[k - 1] - cc[(k - 1) // per] * (e1[k - 1] + e1[k])
        if k >= 2:
            even(k - 1)
        if k >= 3:
            odd(k - 2)
    o1[n - 1] = o[n - 1] - cc[2] * (e1[n - 1] + wrap.after(e1[0], e1[n - 1]))
    o1[-1] = wrap.before(o1[n - 1], o1[0])
    even(n - 1)
    if n > 2:
        odd(n - 2)
    even(0)
    odd(0)
    e2[n] = wrap.after(e2[0], e2[n - 1])
    odd(n - 1)


class _Squares:
    def __init__(self):
        self.acc = {}

    def add(self, key, v):
        self.acc[key] = v * v if key not in self.acc else self.acc[key] + v * v

    def total(self, rows, tiles):
        out = None
        for q in range(3):
            part = None
            for (band, tile), lanes in tiles.items():
                v = self.acc[(band, tile, q)] * (KS * KS if band == "low" else 1.0 / (KS * KS))
                v = v if lanes is None else v * lanes
                part = v if part is None else part + v
            part = part * rows[q]
            out = part if out is None else out + part
        return out


def _tile(v, i):
    return v[:, 128 * i : 128 * (i + 1)]


def _own_rows(core):
    block = 3 * _sublane(128)
    return [
        jnp.where(core == 0, _ones(block + q < 16), _ones(block + q >= 8)) for q in range(3)
    ]


def _half_kernel(sc, x, out, sems):
    at = pl.multiple_of((1 - sc[0]) * HALO, 8)
    copies = [
        pltpu.make_async_copy(x.at[pl.ds(at + 128 * i, 128)], out.at[pl.ds(128 * i, 128)], sems.at[i])
        for i in range(4)
    ]
    for c in copies:
        c.start()
    for c in copies:
        c.wait()


def _own_kernel(
    sc, x, recv, gauge_table_all, gauge_index_all, table_all, rim_all,
    right, left, rim_in, low0, a1l, sums, w, rim_table, kept,
    gauge_table, gauge_index, table, details, xa, xb, xs, y0, y1, sems,
):
    core = sc[0]
    gauges = [
        pltpu.make_async_copy(gauge_index_all, gauge_index, sems.at[4]),
        pltpu.make_async_copy(gauge_table_all, gauge_table, sems.at[5]),
    ]
    for c in gauges:
        c.start()
    at_own = pl.multiple_of(core * HALO, 8)
    at_recv = pl.multiple_of((1 - core) * OWN, 8)
    copies = []
    for i, buf in enumerate((xa, xb)):
        lanes = pl.ds(128 * i, 128)
        copies.append(pltpu.make_async_copy(x.at[:, lanes], buf.at[pl.ds(at_own, OWN)], sems.at[2 * i]))
        copies.append(pltpu.make_async_copy(recv.at[:, lanes], buf.at[pl.ds(at_recv, HALO)], sems.at[2 * i + 1]))
    for c in copies:
        c.start()
    own_table = pltpu.make_async_copy(table_all, table, sems.at[6])
    own_table.start()
    next_table = pltpu.make_async_copy(rim_all.at[sc[1]], rim_table, sems.at[7])
    next_table.start()
    for c in gauges:
        c.wait()
    index = gauge_index[...]
    table_rows = gauge_table[...]
    weights = jnp.zeros(index.shape, F32)
    for g in range(GTAB):
        weights = weights + jnp.where(index == g, table_rows[:, g : g + 1], 0.0)
    block = lax.broadcasted_iota(jnp.int32, (8, NBLK), 1) - 3 * lax.broadcasted_iota(jnp.int32, (8, NBLK), 0)
    block = block - 8 * core
    for l in range(LEVELS):
        for q in range(3):
            hit = jnp.where(block == q, weights[l : l + 1], 0.0)
            w[l, q] = jnp.broadcast_to(jnp.sum(hit, axis=1, keepdims=True), (8, 128))
    for c in copies:
        c.wait()
    lane = _lane()
    group = lane // 32
    for i in range(48):
        to_right, to_left = None, None
        for g in range(4):
            j = 48 * g + i
            a = xa[pl.ds(j, 8, stride=SEG), :]
            b = xb[pl.ds(j, 8, stride=SEG), :]
            xs[j, :, 0:128] = a
            xs[j, :, 128:256] = b
            rim_in[j] = jnp.where(lane < 32, a, b)
            a = pltpu.roll(a, 32 * g, 1) if g else a
            b = pltpu.roll(b, (32 * g + 32) % 128, 1) if g != 3 else b
            to_left = a if to_left is None else jnp.where(group == g, a, to_left)
            to_right = b if to_right is None else jnp.where(group == g, b, to_right)
        right[i] = to_right
        left[i] = to_left
    own_table.wait()
    rows = _own_rows(core)
    sq = _Squares()

    def put_low(k, q, v):
        low0[k] = _tile(v, 0)
        details[k] = _tile(v, 1)
        sq.add(("low", 1, q), _tile(v, 1))

    def put_high(k, q, v):
        details[96 + k] = _tile(v, 0)
        details[192 + k] = _tile(v, 1)
        sq.add(("high", 0, q), _tile(v, 0))
        sq.add(("high", 1, q), _tile(v, 1))

    get = _Forward(lambda j, n: xs[pl.ds(j, n)], _table(table, (0, 256), (0, 256)), y0, 24)
    _chan_forward(get, 96, w, 0, 256, put_low, put_high)
    sums[0] = sq.total(rows, {("low", 1): None, ("high", 0): None, ("high", 1): None})
    keep0 = pltpu.make_async_copy(details.at[pl.ds(0, 288)], kept.at[pl.ds(0, 288)], sems.at[8])
    keep0.start()
    sq1 = _Squares()

    def put_low1(k, q, v):
        a1l[k] = v
        details[288 + k] = v
        sq1.add(("low", 0, q), v)
        if k >= 26:
            packed = jnp.where(lane < 64, a1l[k - 24], pltpu.roll(v, 64, 1))
            right[24 + k] = packed
            left[24 + k] = packed

    def put_high1(k, q, v):
        details[336 + k] = v
        sq1.add(("high", 0, q), v)

    get = _Forward(lambda j, n: low0[pl.ds(j, n)], _table(table, (256, 128), (0, 128)), y1, 24)
    _chan_forward(get, 48, w, 1, 128, put_low1, put_high1)
    keep1 = pltpu.make_async_copy(details.at[pl.ds(288, 96)], kept.at[pl.ds(288, 96)], sems.at[9])
    keep1.start()
    for k in (24, 25):
        packed = jnp.where(lane < 64, a1l[k - 24], pltpu.roll(a1l[k], 64, 1))
        right[24 + k] = packed
        left[24 + k] = packed
    sums[1] = sq1.total(rows, {("low", 0): _ones(_mask(lane, OWN_HIGH1, 0, 64)), ("high", 0): None})
    next_table.wait()
    keep0.wait()
    keep1.wait()


def _bands(details):
    out, at = [], 0
    for n in (96, 48, 24, 12, 6, 3):
        out += [details.at[pl.ds(at, n)], details.at[pl.ds(at + n, n)]]
        at += 2 * n
    return out


def _rim_kernel(
    sc, rim_in, from_left, from_right, low0, a1l, own_sums, table, w,
    kept, message_out, payload_out,
    details, message, payload, rim, y0, y1, x2, y2, y3, y4, y5, l5, sems,
):
    core = sc[0]
    rlow0, rhigh0, r1l, r1h, a2l, a2h, a3l, a3h, a4l, a4h, a5l, a5h = _bands(details)
    copies = []

    def keep(first, last):
        rows = pl.ds(first, last - first)
        c = pltpu.make_async_copy(details.at[rows], kept.at[rows], sems.at[len(copies)])
        c.start()
        copies.append(c)

    lane = _lane()
    for j in range(SEG):
        g, i = j // 48, j % 48
        a = from_left[i]
        b = from_right[i]
        a = pltpu.roll(a, (32 - 32 * g) % 128, 1) if g != 1 else a
        b = pltpu.roll(b, (64 - 32 * g) % 128, 1) if g != 2 else b
        halo = jnp.where(lane < 64, a, b)
        rim[j] = jnp.where((lane < 32) | (lane >= 96), rim_in[j], halo)
    rows = _own_rows(core)
    totals = []

    def level(l, load, n, t, y, step, lanes, low, high, own_low, own_high, pairs):
        sq = _Squares()

        def put_low(k, q, value):
            low[k] = value
            sq.add(("low", 0, q), _tile(value, 0))

        def put_high(k, q, value):
            high[k] = _tile(value, 0)
            sq.add(("high", 0, q), _tile(value, 0))

        _chan_forward(_Forward(load, t, y, step), n, w, l, lanes, put_low, put_high)
        is_high = _mask(lane, own_high, 0, pairs)
        is_low = _mask(lane, own_low, 0, pairs)
        total = sq.total(rows, {("low", 0): _ones(is_high), ("high", 0): _ones(is_high | is_low)})
        totals.append(total + own_sums[l] if l < 2 else total)

    def pick(r, k, c, n):
        return _table(table, (r, k), (c, n))

    level(0, lambda j, n: rim[pl.ds(j, n)], 96, pick(256, 128, 0, 128), y0, 24, 128, rlow0, rhigh0, RIM_LOW0, RIM_HIGH0, 128)
    keep(0, 192)

    def load1(j, n):
        return jnp.concatenate([low0[pl.ds(j, n)], rlow0[pl.ds(j, n)]], axis=2)

    level(1, load1, 48, pick(0, 256, 0, 128), y1, 24, 128, r1l, r1h, RIM_LOW1, RIM_HIGH1, 64)
    keep(192, 288)
    for j in range(48):
        h, i = j // 24, 48 + j % 24
        b, a = from_left[i], from_right[i]
        if h == 0:
            a = pltpu.roll(a, 64, 1)
        else:
            b = pltpu.roll(b, 64, 1)
        x2[j, :, 0:128] = jnp.where(lane < 64, a1l[j], a)
        x2[j, :, 128:256] = jnp.where(lane < 64, b, r1l[j])
    level(2, lambda j, n: x2[pl.ds(j, n)], 24, pick(0, 256, 128, 128), y2, 24, 128, a2l, a2h, LOW2, HIGH2, 32)
    level(3, lambda j, n: a2l[pl.ds(j, n)], 12, pick(256, 128, 128, 128), y3, 24, 128, a3l, a3h, LOW3, HIGH3, 16)
    keep(288, 360)
    level(4, lambda j, n: a3l[pl.ds(j, n)], 6, pick(512, 128, 0, 128), y4, 12, 128, a4l, a4h, LOW4, HIGH4, 8)
    level(5, lambda j, n: a4l[pl.ds(j, n)], 3, pick(384, 128, 0, 256), y5, 6, 256, l5, a5h, LOW5, HIGH5, 4)
    sub = _sublane(128)
    line = jnp.zeros((8, 128), F32)
    for j in range(3):
        a = l5[j, :, 0:128]
        a5l[j] = a
        message[j] = jnp.where(lane < 64, a5h[j], pltpu.roll(a, 64, 1))
        line = line + jnp.where(lane // 4 == 8 * j + sub, l5[j, :, 128:256], 0.0)
    keep(360, 378)
    copies.append(pltpu.make_async_copy(message, message_out, sems.at[4]))
    copies[-1].start()
    sums = jnp.zeros((8, 128), F32)
    for l in range(LEVELS):
        sums = jnp.where(sub == l, jnp.sum(totals[l], axis=0, keepdims=True), sums)
    sums = jnp.sum(sums, axis=1, keepdims=True)
    line = line + jnp.where((lane == 96 + sub) & (sub < LEVELS), sums, 0.0)
    line = jnp.sum(line, axis=0, keepdims=True)
    payload[...] = jnp.broadcast_to(line, payload.shape)
    copies.append(pltpu.make_async_copy(payload, payload_out, sems.at[5]))
    copies[-1].start()
    for c in copies:
        c.wait()


def _shrink(v, limit):
    return v - jnp.minimum(jnp.maximum(v, -limit), limit)


def _back_kernel(
    sc, g, near_left_all, near_right_all, coarse_all, v_all, back_all, own_kept, rim_kept, w,
    out,
    near_left, near_right, w_all, table, own_details, rim_details, v, gt, x5l, x5h, y5, y4, y3, y2, y1, y0, c4, c3, c2, c1, c0, fa, fb, sems,
):
    core, variant = sc[0], sc[1]
    rlow0, rhigh0, r1l, r1h, a2l, a2h, a3l, a3h, a4l, a4h, a5l, a5h = _bands(rim_details)
    dlow0, dhigh0, dhigh1 = (own_details.at[pl.ds(96 * i, 96)] for i in range(3))
    a1l, a1h = (own_details.at[pl.ds(288 + 48 * i, 48)] for i in range(2))
    v[...] = jnp.zeros(v.shape, BF16)
    small = pl.ds(288, 90)
    large = pl.ds(0, 288)
    copies = [
        pltpu.make_async_copy(src, dst, sems.at[3 + i])
        for i, (src, dst) in enumerate(
            (
                (coarse_all, w_all),
                (v_all.at[sc[2]], v.at[:, pl.ds(0, 16), :]),
                (near_left_all, near_left),
                (near_right_all, near_right),
                (rim_kept.at[small], rim_details.at[small]),
                (back_all.at[variant], table),
                (own_kept, own_details),
                (rim_kept.at[large], rim_details.at[large]),
            )
        )
    ]
    for c in copies:
        c.start()
    lane = _lane()
    lane1 = _lane(1)
    total = jnp.sum(g[...], axis=0, keepdims=True)
    limits = []
    for l in range(LEVELS):
        entries = 3 * (C >> (l + 1)) * (S >> (l + 1))
        s = jnp.sum(jnp.where(lane1 == 96 + l, total, 0.0), axis=1, keepdims=True)
        limits.append(jnp.sqrt(s * (1.0 / entries) + FLOOR))
    gt[0] = jnp.transpose(g[0:128])
    gt[1] = jnp.transpose(g[128:256])
    rows = [
        jnp.concatenate([gt[c, pl.ds(m, 24, stride=4), :] for m in range(4)], axis=1) for c in range(2)
    ]
    copies[0].wait()
    coarse = _dot3(jnp.concatenate(rows, axis=0), lambda i: w_all[i])
    position = lax.broadcasted_iota(jnp.int32, (48, 512), 1)
    highs = position >= (S >> (LEVELS + COARSE))
    square = jnp.where(highs, coarse * coarse, 0.0)
    square = square[:, 0:128] + square[:, 128:256] + square[:, 256:384] + square[:, 384:512]
    kept = jnp.zeros((8, 128), F32)
    row = 3 * _sublane(128)
    for j in range(3):
        kept = kept + jnp.where(row + j < 16, square[8 * j : 8 * j + 8], 0.0)
        kept = kept + jnp.where(row + j >= 8, square[24 + 8 * j : 32 + 8 * j], 0.0)
    square = jnp.sum(jnp.sum(kept, axis=0, keepdims=True), axis=1, keepdims=True)
    entries = (C >> LEVELS) * ((S >> LEVELS) - (S >> (LEVELS + COARSE)))
    limit = jnp.sqrt(square * (1.0 / entries) + FLOOR)
    coarse = jnp.where(highs, _shrink(coarse, limit), coarse)
    mine = jnp.where(core == 0, coarse[0:24], coarse[24:48])
    mine = jnp.concatenate([mine, jnp.zeros((8, 512), F32)], axis=0)
    hi = mine.astype(BF16)
    lo = (mine - hi.astype(F32)).astype(BF16)
    for c in copies[1:6]:
        c.wait()
    for k in range(3):
        before, after = near_left[k], near_right[k]
        at = lane % 4
        for ref, own, roll in ((x5h, a5h, 0), (x5l, a5l, 64)):
            a = pltpu.roll(before, (roll + 127) % 128, 1)
            b = pltpu.roll(after, (roll + 1) % 128, 1)
            ref[k] = jnp.where(at == 1, own[k], jnp.where(at == 0, a, b))
    def nt(a, b):
        return lax.dot_general(a, b, (((1,), (1,)), ((), ())), preferred_element_type=F32)

    current = nt(hi, v[0]) + nt(lo, v[0]) + nt(hi, v[1])

    def level(l, get_current, low, high, n, y, t, nxt, step, needed):
        tl = jnp.broadcast_to(limits[l] * (1.0 / KS), (8, 128))
        th = jnp.broadcast_to(limits[l] * KS, (8, 128))
        is_low = needed(lane)

        def get_low(k):
            return jnp.where(is_low, get_current(k), _shrink(low[k], tl))

        def store(j, m, value):
            nxt[pl.ds(j, m)] = value

        put = _Backward(y, t, store, step)
        _chan_inverse(get_low, lambda k: _shrink(high[k], th), n, w, l, 128, put)

    def pick(r, k, c, n):
        return _table(table, (r, k), (c, n))

    level(
        5, lambda k: current[8 * k : 8 * k + 8], x5l, x5h, 3, y5, pick(896, 128, 0, 128), c4, 6, lambda i: i < 32
    )
    level(4, lambda k: c4[k], a4l, a4h, 6, y4, pick(768, 128, 128, 128), c3, 12, lambda i: i < 32)
    level(3, lambda k: c3[k], a3l, a3h, 12, y3, pick(768, 128, 0, 128), c2, 24, lambda i: i < 64)
    level(2, lambda k: c2[k], a2l, a2h, 24, y2, pick(640, 128, 0, 256), c1, 24, lambda i: i < 85)
    for c in copies[6:]:
        c.wait()
    tl = jnp.broadcast_to(limits[1] * (1.0 / KS), (8, 256))
    th = jnp.broadcast_to(limits[1] * KS, (8, 256))
    lane2 = lax.broadcasted_iota(jnp.int32, (8, 256), 1)
    is_low1 = (lane2 < 64) | ((lane2 >= 192) & (lane2 < 208))

    def get_low1(k):
        v1 = jnp.concatenate([a1l[k], r1l[k]], axis=1)
        return jnp.where(is_low1, c1[k], _shrink(v1, tl))

    def get_high1(k):
        return _shrink(jnp.concatenate([a1h[k], r1h[k]], axis=1), th)

    def store1(j, m, value):
        c0[pl.ds(j, m)] = value

    put1 = _Backward(y1, pick(384, 256, 0, 256), store1, 24)
    _chan_inverse(get_low1, get_high1, 48, w, 1, 256, put1)
    tl0 = jnp.broadcast_to(limits[0] * (1.0 / KS), (8, 128))
    th0 = jnp.broadcast_to(limits[0] * KS, (8, 384))
    rim_low = lane < 32

    def get_low0(k):
        now = c0[k]
        rim = jnp.where(rim_low, _tile(now, 1), _shrink(rlow0[k], tl0))
        return jnp.concatenate([_tile(now, 0), _shrink(dlow0[k], tl0), rim], axis=1)

    def get_high0(k):
        return _shrink(jnp.concatenate([dhigh0[k], dhigh1[k], rhigh0[k]], axis=1), th0)

    def store0(j, m, value):
        for i in range(m):
            fa[pl.ds(j + i, 8, stride=SEG), :] = value[i, :, 0:128]
            fb[pl.ds(j + i, 8, stride=SEG), :] = value[i, :, 128:256]

    put0 = _Backward(y0, pick(0, 384, 0, 256), store0, 24)
    _chan_inverse(get_low0, get_high0, 96, w, 0, 384, put0)
    at_own = pl.multiple_of(core * HALO, 8)
    last = [
        pltpu.make_async_copy(buf.at[pl.ds(at_own, OWN)], out.at[:, pl.ds(128 * i, 128)], sems.at[1 + i])
        for i, buf in enumerate((fa, fb))
    ]
    for c in last:
        c.start()
    for c in last:
        c.wait()


VM = pl.BlockSpec(memory_space=pltpu.VMEM)
SM = pl.BlockSpec(memory_space=pltpu.SMEM)
ANY = pl.BlockSpec(memory_space=pl.ANY)
HBM = pl.BlockSpec(memory_space=pltpu.HBM)


def _call(kernel, name, limit, args, specs, outs, out_specs, scratch):
    args = [
        pltpu.with_memory_space_constraint(x, pltpu.HBM) if spec is HBM else x for x, spec in zip(args, specs)
    ]
    outs = [jax.ShapeDtypeStruct(s, F32) if isinstance(s, tuple) else s for s in outs]
    return pl.pallas_call(
        kernel,
        out_shape=[pltpu.HBM(s.shape, s.dtype) if spec is HBM else s for s, spec in zip(outs, out_specs)],
        in_specs=specs,
        out_specs=out_specs,
        scratch_shapes=[pltpu.VMEM(s, F32) if isinstance(s, tuple) else s for s in scratch],
        compiler_params=pltpu.CompilerParams(vmem_limit_bytes=limit << 20),
        name=name,
    )(*args)


def _shift(v, by):
    return lax.ppermute(v, "tm", [(i, i + by) for i in range(NT) if 0 <= i + by < NT])


def shards(record, gauge_table, gauge_index):
    tables = _tables()
    core = lax.axis_index("chan")
    place = lax.axis_index("tm")
    variant = jnp.where(place == 0, 0, jnp.where(place == NT - 1, 2, 1))
    sc = jnp.stack([core, variant, place]).astype(jnp.int32)
    dma = pltpu.SemaphoreType.DMA
    (sent,) = _call(_half_kernel, "half", 2, (sc, record), [SM, HBM], [(HALO, 256)], [ANY], [dma((4,))])
    recv = lax.ppermute(sent, "chan", [(0, 1), (1, 0)])
    right, left, rim_in, low0, a1l, sums, w, rim_table, own_kept = _call(
        _own_kernel, "own", 20,
        (sc, record, recv, gauge_table, gauge_index, tables["own"], tables["rim"]),
        [SM, HBM, ANY, HBM, HBM, HBM, HBM],
        [(72, 8, 128), (72, 8, 128), (SEG, 8, 128), (96, 8, 128), (48, 8, 128), (2, 8, 128),
         (LEVELS, 3, 8, 128), jax.ShapeDtypeStruct((2, 640, 256), BF16), (384, 8, 128)],
        [VM] * 8 + [HBM],
        [(LEVELS, GTAB), pltpu.VMEM((LEVELS, NBLK), jnp.int32), pltpu.VMEM((2, 384, 256), BF16), (384, 8, 128),
         (8 * SEG, 128), (8 * SEG, 128), (SEG, 8, 256), (SEG, 8, 256), (96, 8, 128), dma((10,))],
    )
    from_left, from_right = _shift(right, 1), _shift(left, -1)
    rim_kept, message, payload = _call(
        _rim_kernel, "rim", 16, (sc, rim_in, from_left, from_right, low0, a1l, sums, rim_table, w),
        [SM] + [VM] * 8, [(378, 8, 128), (3, 8, 128), (256, 128)], [HBM] * 3,
        [(378, 8, 128), (3, 8, 128), (256, 128),
         (SEG, 8, 128), (SEG, 8, 128), (96, 8, 128), (48, 8, 256), (48, 8, 128), (24, 8, 128), (12, 8, 128),
         (6, 8, 256), (3, 8, 256), dma((6,))],
    )
    everyone = lax.all_to_all(payload, ("chan", "tm"), split_axis=0, concat_axis=0, tiled=True)
    near_left, near_right = _shift(message, 1), _shift(message, -1)
    (out,) = _call(
        _back_kernel, "back", 24,
        (sc, everyone, near_left, near_right, tables["w"], tables["v"], tables["back"], own_kept, rim_kept, w),
        [SM, VM] + [HBM] * 7 + [VM], [(OWN, 256)], [HBM],
        [
            (3, 8, 128), (3, 8, 128), pltpu.VMEM((2, 512, 512), BF16), pltpu.VMEM((2, 1024, 256), BF16),
            (384, 8, 128), (378, 8, 128),
            pltpu.VMEM((2, 128, 512), BF16), (2, 128, 128), (3, 8, 128), (3, 8, 128),
            (6, 8, 128), (12, 8, 128), (24, 8, 128), (48, 8, 128), (96, 8, 256), (SEG, 8, 384),
            (6, 8, 128), (12, 8, 128), (24, 8, 128), (48, 8, 256), (96, 8, 256),
            (8 * SEG, 128), (8 * SEG, 128), dma((11,)),
        ],
    )
    return out


def solution(mesh):
    return jax.shard_map(
        shards,
        mesh=mesh,
        in_specs=(P("chan", "tm"), P(), P()),
        out_specs=P("chan", "tm"),
        check_vma=False,
    )
```

time: 88.4 us -> 70 us (0.79)
  the two profiles are of different devices: /device:TPU:1 before, /device:TPU:6 now
where the time goes in v2:
time: 70 us; the launch traced here: 69.8 us
  starting transfers between devices  34.6 us (49%)
  Pallas kernels  17.9 us (26%)
  waiting for transfers between devices  16.5 us (24%)
    ppermute x4, starting transfers between devices, _shift(): lax.ppermute(v, 'tm', [(i, i + by) for i in range(NT) if 0 <= i + by < NT])  23.3 us
    pallas_call x4, Pallas kernels, _call(): pl.pallas_call(kernel, out_shape=[pltpu.HBM(s.shape, s.dtype) if spec is...  17.9 us
    ppermute x4, waiting for transfers between devices, _shift(): lax.ppermute(v, 'tm', [(i, i + by) for i in range(NT) if 0 <= i + by < NT])  14.6 us
    all_to_all x1, starting transfers between devices, shards(): lax.all_to_all(payload, ('chan', 'tm'), split_axis=0, concat_axis=0, tile...  11.3 us
    ppermute x1, waiting for transfers between devices, shards(): recv = lax.ppermute(sent, 'chan', [(0, 1), (1, 0)])  1.9 us
  transfers between devices with their start and end apart: 6, of which 4 were waited for; matrix products, arithmetic and copies ran while one was open for 0% of the time, Pallas kernels for 0%

profile of v2, /device:TPU:6, one launch (start us, length us, event | category | flops | bytes accessed | tf_op | source)
XLA Modules:
  0.0 69.8 jit_solution(9982388515390978715)
XLA Ops:
  0.0 0.1 pad_add_fusion.sc
  0.1 1.7 %half.1 = f32[512,256]{1,0:T(8,128)S(1)} custom-call(s32[3]{0:T(128)S(1)} %pad_add_fusion.sc, f32[1024,256]{1,0:T(8,128)} %x.3), custom_call_target="tpu_custom_call" | custom-call | tf_op jit(solution)/shard_map/half/pallas_call | solution.py:779
  1.8 0.1 collective-permute-start
  1.9 1.9 %collective-permute-done.recv = f32[512,256]{1,0:T(8,128)S(1)} collective-permute-done((f32[512,256]{1,0:T(8,128)S(1)}, f32[512,256]{1,0:T(8,128)S(1)}, u32[]{:S(2)}, u32[]{:S(2)}) %collective-permute-start) | collective-permute-done | bytes 524320 | tf_op jit(solution)/shard_map/ppermute | solution.py:802
  3.8 5.0 %own.1 = (f32[72,8,128]{2,1,0:T(8,128)S(1)}, f32[72,8,128]{2,1,0:T(8,128)S(1)}, f32[192,8,128]{2,1,0:T(8,128)S(1)}, f32[96,8,128]{2,1,0:T(8,128)S(1)}, f32[48,8,...) custom-call(s32[3]{0:T(128)S(1)} %pad_add_fusion.sc, ...), custom_call_target="tpu_custom_call" | custom-call | tf_op jit(solution)/shard_map/own/pallas_call | solution.py:779
  8.7 3.8 %collective-permute-start.1 = (f32[72,8,128]{2,1,0:T(8,128)S(1)}, f32[72,8,128]{2,1,0:T(8,128)S(1)}, u32[]{:S(2)}, u32[]{:S(2)}) collective-permute-start(f32[72,8,128]{2,1,0:T(8,128)S(1)} %get-tuple-element.18), channel_id=1, source_target_pairs={{0,2},{2,4},{4,6},{6,8},{8,10},{10,12},{12,14},{14,16},{16,18},{18... | collective-permute-start | bytes 884744 | tf_op jit(solution)/shard_map/ppermute | solution.py:791
  12.6 8.6 %collective-permute-start.2 = (f32[72,8,128]{2,1,0:T(8,128)S(1)}, f32[72,8,128]{2,1,0:T(8,128)S(1)}, u32[]{:S(2)}, u32[]{:S(2)}) collective-permute-start(f32[72,8,128]{2,1,0:T(8,128)S(1)} %get-tuple-element.19), channel_id=1, source_target_pairs={{2,0},{4,2},{6,4},{8,6},{10,8},{12,10},{14,12},{16,14},{18,16},{20... | collective-permute-start | bytes 884744 | tf_op jit(solution)/shard_map/ppermute | solution.py:791
  21.2 5.4 %collective-permute-done.1.from_left = f32[72,8,128]{2,1,0:T(8,128)S(1)} collective-permute-done((f32[72,8,128]{2,1,0:T(8,128)S(1)}, f32[72,8,128]{2,1,0:T(8,128)S(1)}, u32[]{:S(2)}, u32[]{:S(2)}) %collective-permute-start.1) | collective-permute-done | bytes 294944 | tf_op jit(solution)/shard_map/ppermute | solution.py:791
  26.5 1.2 %collective-permute-done.2.from_right = f32[72,8,128]{2,1,0:T(8,128)S(1)} collective-permute-done((f32[72,8,128]{2,1,0:T(8,128)S(1)}, f32[72,8,128]{2,1,0:T(8,128)S(1)}, u32[]{:S(2)}, u32[]{:S(2)}) %collective-permute-start.2) | collective-permute-done | bytes 294944 | tf_op jit(solution)/shard_map/ppermute | solution.py:791
  27.7 3.3 %rim.1 = (f32[378,8,128]{2,1,0:T(8,128)}, f32[3,8,128]{2,1,0:T(8,128)}, f32[256,128]{1,0:T(8,128)}) custom-call(s32[3]{0:T(128)S(1)} %pad_add_fusion.sc, f32[192,8,128]{2,1,0:T(8,128)S(1)} %get-tuple-element.17.rim_in, f32[72,8,128]{2,1,0:T(8,128)S(1)} %collective-permute-done.1.from_left, f32[72,8,128]{2,1,0:T(8,128)S(1)} %collective-permute-done.2.from_right, ...), custom_call_target="tpu_custom_call" | custom-call | tf_op jit(solution)/shard_map/rim/pallas_call | solution.py:779
  31.0 11.3 %all-to-all-start = ((f32[256,1,128]{2,1,0:T(1,128)}), f32[256,1,128]{2,1,0:T(1,128)S(1)}, u32[]{:S(2)}, u32[]{:S(2)}) async-start(f32[256,1,128]{2,1,0:T(1,128)} %bitcast.8), calls=%async_computation | async-start | bytes 262144 | tf_op jit(solution)/shard_map/all_to_all | solution.py:821
  42.3 9.0 %collective-permute-start.4 = (f32[3,8,128]{2,1,0:T(8,128)}, f32[3,8,128]{2,1,0:T(8,128)S(1)}, u32[]{:S(2)}, u32[]{:S(2)}) collective-permute-start(f32[3,8,128]{2,1,0:T(8,128)} %get-tuple-element.26), channel_id=1, source_target_pairs={{2,0},{4,2},{6,4},{8,6},{10,8},{12,10},{14,12},{16,14},{18,16},{20... | collective-permute-start | bytes 36872 | tf_op jit(solution)/shard_map/ppermute | solution.py:791
  51.2 1.9 %collective-permute-start.3 = (f32[3,8,128]{2,1,0:T(8,128)}, f32[3,8,128]{2,1,0:T(8,128)S(1)}, u32[]{:S(2)}, u32[]{:S(2)}) collective-permute-start(f32[3,8,128]{2,1,0:T(8,128)} %get-tuple-element.26), channel_id=1, source_target_pairs={{0,2},{2,4},{4,6},{6,8},{8,10},{10,12},{12,14},{14,16},{16,18},{18... | collective-permute-start | bytes 36872 | tf_op jit(solution)/shard_map/ppermute | solution.py:791
  53.2 0.0 collective-permute-done.4.near_right_all
  53.2 0.0 copy-start
  53.2 8.1 %collective-permute-done.3.near_left_all = f32[3,8,128]{2,1,0:T(8,128)S(1)} collective-permute-done((f32[3,8,128]{2,1,0:T(8,128)}, f32[3,8,128]{2,1,0:T(8,128)S(1)}, u32[]{:S(2)}, u32[]{:S(2)}) %collective-permute-start.3) | collective-permute-done | bytes 12320 | tf_op jit(solution)/shard_map/ppermute | solution.py:791
  61.3 0.0 copy-start.1
  61.3 0.0 all-to-all-done
  61.3 0.0 copy-done
  61.3 0.6 copy-done.1
  61.9 7.9 %back.1 = f32[1024,256]{1,0:T(8,128)} custom-call(s32[3]{0:T(128)S(1)} %pad_add_fusion.sc, f32[256,128]{1,0:T(8,128)S(1)} %bitcast.7, f32[3,8,128]{2,1,0:T(8,128)} %copy-done.1, f32[3,8,128]{2,1,0:T(8,128)} %copy-done, bf16[2,512,512]{2,1,0:T(8,128)(2,1)} %constant.28.clone.coarse_all, bf16[128,2,16,512]{3,2,1,0:T(8,128)(2,1)} %constant.29.clone.v_all, ...), custom_call_target="tpu_custom_call" | custom-call | tf_op jit(solution)/shard_map/back/pallas_call | solution.py:779
Async XLA Ops:
  1.8 2.0 %collective-permute-start = (f32[512,256]{1,0:T(8,128)S(1)}, f32[512,256]{1,0:T(8,128)S(1)}, u32[]{:S(2)}, u32[]{:S(2)}) collective-permute-start(f32[512,256]{1,0:T(8,128)S(1)} %half.1), channel_id=1, source_target_pairs={{0,1},{1,0},{2,3},{3,2},{4,5},{5,4},{6,7},{7,6},{8,9},{9,8},{10,11... | collective-permute-start | bytes 1572872 | tf_op jit(solution)/shard_map/ppermute | solution.py:802
  8.7 17.8 %collective-permute-start.1 = (f32[72,8,128]{2,1,0:T(8,128)S(1)}, f32[72,8,128]{2,1,0:T(8,128)S(1)}, u32[]{:S(2)}, u32[]{:S(2)}) collective-permute-start(f32[72,8,128]{2,1,0:T(8,128)S(1)} %get-tuple-element.18), channel_id=1, source_target_pairs={{0,2},{2,4},{4,6},{6,8},{8,10},{10,12},{12,14},{14,16},{16,18},{18... | collective-permute-start | bytes 884744 | tf_op jit(solution)/shard_map/ppermute | solution.py:791
  12.6 15.1 %collective-permute-start.2 = (f32[72,8,128]{2,1,0:T(8,128)S(1)}, f32[72,8,128]{2,1,0:T(8,128)S(1)}, u32[]{:S(2)}, u32[]{:S(2)}) collective-permute-start(f32[72,8,128]{2,1,0:T(8,128)S(1)} %get-tuple-element.19), channel_id=1, source_target_pairs={{2,0},{4,2},{6,4},{8,6},{10,8},{12,10},{14,12},{16,14},{18,16},{20... | collective-permute-start | bytes 884744 | tf_op jit(solution)/shard_map/ppermute | solution.py:791
  31.0 30.2 %all-to-all-start = ((f32[256,1,128]{2,1,0:T(1,128)}), f32[256,1,128]{2,1,0:T(1,128)S(1)}, u32[]{:S(2)}, u32[]{:S(2)}) async-start(f32[256,1,128]{2,1,0:T(1,128)} %bitcast.8), calls=%async_computation | async-start | bytes 262144 | tf_op jit(solution)/shard_map/all_to_all | solution.py:821
  42.3 10.9 %collective-permute-start.4 = (f32[3,8,128]{2,1,0:T(8,128)}, f32[3,8,128]{2,1,0:T(8,128)S(1)}, u32[]{:S(2)}, u32[]{:S(2)}) collective-permute-start(f32[3,8,128]{2,1,0:T(8,128)} %get-tuple-element.26), channel_id=1, source_target_pairs={{2,0},{4,2},{6,4},{8,6},{10,8},{12,10},{14,12},{16,14},{18,16},{20... | collective-permute-start | bytes 36872 | tf_op jit(solution)/shard_map/ppermute | solution.py:791
  51.2 10.0 %collective-permute-start.3 = (f32[3,8,128]{2,1,0:T(8,128)}, f32[3,8,128]{2,1,0:T(8,128)S(1)}, u32[]{:S(2)}, u32[]{:S(2)}) collective-permute-start(f32[3,8,128]{2,1,0:T(8,128)} %get-tuple-element.26), channel_id=1, source_target_pairs={{0,2},{2,4},{4,6},{6,8},{8,10},{10,12},{12,14},{14,16},{16,18},{18... | collective-permute-start | bytes 36872 | tf_op jit(solution)/shard_map/ppermute | solution.py:791
  53.2 8.1 %copy-start = (f32[3,8,128]{2,1,0:T(8,128)}, f32[3,8,128]{2,1,0:T(8,128)S(1)}, u32[]{:S(2)}) copy-start(f32[3,8,128]{2,1,0:T(8,128)S(1)} %collective-permute-done.4.near_right_all) | copy-start | bytes 36868
  61.3 0.6 copy-start.1

commit v3 on v2

--- a/solution.py
+++ b/solution.py
@@ -109,14 +109,14 @@
 IN2 = {
     **OWN_LOW1, **_run(67, 125, 67), **_run(-61, -3, 131), **{k: 128 + v for k, v in RIM_LOW1.items()}
 }
-LOW2 = _run(-28, 57, 0)
-HIGH2 = _run(-3, 36, 85)
-LOW3 = _run(-12, 27, 0)
+LOW2 = _run(-28, 61, 0)
+HIGH2 = _run(-3, 36, 89)
+LOW3 = _run(-12, 29, 0)
 HIGH3 = _run(-3, 20, 64)
-LOW4 = _run(-4, 12, 0)
+LOW4 = _run(-4, 13, 0)
 HIGH4 = _run(-3, 12, 32)
-LOW5 = {4 * (d - 1) + i: 4 * i + d for i in range(4) for d in range(3)}
-HIGH5 = {k: 32 + v for k, v in LOW5.items()}
+LOW5 = _run(-4, 8, 0)
+HIGH5 = _run(-4, 8, 16)
 
 
 def _part(places, first, last):
@@ -128,8 +128,8 @@
     return ((0, far), (-far, far), (-far, width))
 
 
-def _bundle(parts, rows):
-    out = np.zeros((rows, 256))
+def _bundle(parts, rows, cols):
+    out = np.zeros((rows, cols))
     for r, c, m in parts:
         out[r : r + m.shape[0], c : c + m.shape[1]] = m
     return _pair(out)
@@ -146,24 +146,27 @@
             (256, 0, fw(OWN_LOW0, OWN_LOW1, OWN_HIGH1, 128, 128, -far, far, KS)),
         ),
         384,
+        256,
     )
     rim, back = [], []
     for v in range(3):
         a, b = zip(*(_edges(256 >> l)[v] for l in range(LEVELS)))
-        t5 = fw(LOW4, _part(LOW5, 0, 4), _part(HIGH5, 0, 4), 128, 256, a[5], b[5], KS)
-        for i in range(128):
-            t5[:, 128 + i] = t5[:, LOW5[i % 4]]
+        t5 = fw(LOW4, _part(LOW5, 0, 5), _part(HIGH5, 0, 5), 128, 256, a[5], b[5], KS)
+        lows, highs = t5[:, 4:8].copy(), t5[:, 20:24].copy()
+        sixteen = np.concatenate([lows, highs[:, 1:], lows[:, 1:], highs[:, 1:], np.zeros((128, 3))], axis=1)
+        t5[:, 128:] = np.tile(sixteen, (1, 8))
         rim.append(
             _bundle(
                 (
                     (0, 0, fw(IN1, RIM_LOW1, RIM_HIGH1, 256, 128, a[1], b[1], KS)),
                     (0, 128, fw(IN2, LOW2, HIGH2, 256, 128, a[2], b[2], KS)),
-                    (256, 0, fw(RIM_IN0, RIM_LOW0, RIM_HIGH0, 128, 128, a[0], b[0], 1.0)),
-                    (256, 128, fw(LOW2, LOW3, HIGH3, 128, 128, a[3], b[3], KS)),
-                    (384, 0, t5),
-                    (512, 0, fw(LOW3, LOW4, HIGH4, 128, 128, a[4], b[4], KS)),
+                    (0, 256, fw(LOW2, LOW3, HIGH3, 128, 128, a[3], b[3], KS)),
+                    (128, 256, fw(LOW3, LOW4, HIGH4, 128, 128, a[4], b[4], KS)),
+                    (256, 0, t5),
+                    (384, 0, fw(RIM_IN0, RIM_LOW0, RIM_HIGH0, 128, 128, a[0], b[0], 1.0)),
                 ),
-                640,
+                512,
+                384,
             )
         )
         low0 = {**OWN_LOW0, **{k: 256 + v for k, v in RIM_LOW0.items() if -2 <= k < 130}}
@@ -181,6 +184,7 @@
                     (896, 0, inv(LOW5, HIGH5, _part(LOW4, -2, 12), 128, 128, a[5], b[5], 1.0 / KS)),
                 ),
                 1024,
+                256,
             )
         )
     out["rim"], out["back"] = np.stack(rim), np.stack(back)
@@ -192,19 +196,15 @@
         bands.append(high)
     coarse = np.concatenate([current] + bands[::-1])
     order = (np.arange(n) % NT) * 4 + np.arange(n) // NT
-    out["w"] = _pair((KS * coarse.T)[order])
     last = n >> COARSE
     current = np.eye(n)[:last]
     for step in range(COARSE):
         size = last << step
         current = _unlift(current, np.eye(n)[size : 2 * size])
-    rebuilt = np.zeros((n + 8, n))
-    rebuilt[4 : n + 4] = current / KS
-    rebuilt = _pair(rebuilt)
-    pieces = np.zeros((NT, 2, 16, n), ml_dtypes.bfloat16)
-    for k, lane in LOW5.items():
-        pieces[:, :, lane] = np.moveaxis(rebuilt[:, 4 + k : 4 + k + n : 4], 0, 1)
-    out["v"] = pieces
+    both = np.zeros((n + 640, n))
+    both[:n] = (KS * coarse.T)[order]
+    both[n + 4 : 2 * n + 4] = current / KS
+    out["coarse"] = _pair(both)
     return out
 
 
@@ -396,44 +396,27 @@
     ]
 
 
-def _half_kernel(sc, x, out, sems):
-    at = pl.multiple_of((1 - sc[0]) * HALO, 8)
+def _load_kernel(
+    sc, x_all, gauge_table_all, gauge_index_all, own_all, rim_all,
+    low, high, ends, own_table, rim_table, w,
+    x, gauge_table, gauge_index, sems,
+):
+    core = sc[0]
     copies = [
-        pltpu.make_async_copy(x.at[pl.ds(at + 128 * i, 128)], out.at[pl.ds(128 * i, 128)], sems.at[i])
-        for i in range(4)
+        pltpu.make_async_copy(src, dst, sems.at[i])
+        for i, (src, dst) in enumerate(
+            (
+                (gauge_index_all, gauge_index),
+                (gauge_table_all, gauge_table),
+                (own_all, own_table),
+                *((x_all.at[pl.ds(256 * i, 256)], x.at[pl.ds(256 * i, 256)]) for i in range(4)),
+                (rim_all.at[sc[1]], rim_table),
+            )
+        )
     ]
     for c in copies:
         c.start()
-    for c in copies:
-        c.wait()
-
-
-def _own_kernel(
-    sc, x, recv, gauge_table_all, gauge_index_all, table_all, rim_all,
-    right, left, rim_in, low0, a1l, sums, w, rim_table, kept,
-    gauge_table, gauge_index, table, details, xa, xb, xs, y0, y1, sems,
-):
-    core = sc[0]
-    gauges = [
-        pltpu.make_async_copy(gauge_index_all, gauge_index, sems.at[4]),
-        pltpu.make_async_copy(gauge_table_all, gauge_table, sems.at[5]),
-    ]
-    for c in gauges:
-        c.start()
-    at_own = pl.multiple_of(core * HALO, 8)
-    at_recv = pl.multiple_of((1 - core) * OWN, 8)
-    copies = []
-    for i, buf in enumerate((xa, xb)):
-        lanes = pl.ds(128 * i, 128)
-        copies.append(pltpu.make_async_copy(x.at[:, lanes], buf.at[pl.ds(at_own, OWN)], sems.at[2 * i]))
-        copies.append(pltpu.make_async_copy(recv.at[:, lanes], buf.at[pl.ds(at_recv, HALO)], sems.at[2 * i + 1]))
-    for c in copies:
-        c.start()
-    own_table = pltpu.make_async_copy(table_all, table, sems.at[6])
-    own_table.start()
-    next_table = pltpu.make_async_copy(rim_all.at[sc[1]], rim_table, sems.at[7])
-    next_table.start()
-    for c in gauges:
+    for c in copies[:2]:
         c.wait()
     index = gauge_index[...]
     table_rows = gauge_table[...]
@@ -446,26 +429,51 @@
         for q in range(3):
             hit = jnp.where(block == q, weights[l : l + 1], 0.0)
             w[l, q] = jnp.broadcast_to(jnp.sum(hit, axis=1, keepdims=True), (8, 128))
-    for c in copies:
-        c.wait()
+    copies[2].wait()
+    for i in range(4):
+        copies[3 + i].wait()
+        _first(x, own_table, low, high, ends, 0, range(256 * i, 256 * i + 256, 128))
+    copies[7].wait()
+
+
+def _first(x, table, low, high, ends, at, blocks):
+    lane = _lane(128)
+    for r in blocks:
+        v = x[pl.ds(r, 128), :]
+        y = _dot3(v, _table(table, (0, 256), (0, 256)))
+        rows = pl.ds(at + r, 128)
+        low[rows, :] = y[:, 0:128]
+        high[rows, :] = y[:, 128:256]
+        ends[rows, :] = jnp.where(lane < 32, v[:, 0:128], v[:, 128:256])
+
+
+def _own_kernel(
+    sc, recv, own_low, own_high, own_ends, table, w,
+    right, left, rim_in, low0, a1l, details, sums,
+    fl, fh, fe, y1,
+):
+    core = sc[0]
+    at_own = pl.multiple_of(core * HALO, 8)
+    at_recv = pl.multiple_of((1 - core) * OWN, 8)
+    for src, dst in ((own_low, fl), (own_high, fh), (own_ends, fe)):
+        for r in range(0, OWN, 128):
+            dst[pl.ds(at_own + r, 128), :] = src[pl.ds(r, 128), :]
+    theirs = recv.at[pl.ds(at_own, HALO)]
+    _first(theirs, table, fl, fh, fe, at_recv, range(0, HALO, 128))
     lane = _lane()
     group = lane // 32
     for i in range(48):
         to_right, to_left = None, None
         for g in range(4):
             j = 48 * g + i
-            a = xa[pl.ds(j, 8, stride=SEG), :]
-            b = xb[pl.ds(j, 8, stride=SEG), :]
-            xs[j, :, 0:128] = a
-            xs[j, :, 128:256] = b
-            rim_in[j] = jnp.where(lane < 32, a, b)
-            a = pltpu.roll(a, 32 * g, 1) if g else a
-            b = pltpu.roll(b, (32 * g + 32) % 128, 1) if g != 3 else b
+            v = fe[pl.ds(j, 8, stride=SEG), :]
+            rim_in[j] = v
+            a = pltpu.roll(v, 32 * g, 1) if g else v
+            b = pltpu.roll(v, (32 * g + 32) % 128, 1) if g != 3 else v
             to_left = a if to_left is None else jnp.where(group == g, a, to_left)
             to_right = b if to_right is None else jnp.where(group == g, b, to_right)
         right[i] = to_right
         left[i] = to_left
-    own_table.wait()
     rows = _own_rows(core)
     sq = _Squares()
 
@@ -480,11 +488,12 @@
         sq.add(("high", 0, q), _tile(v, 0))
         sq.add(("high", 1, q), _tile(v, 1))
 
-    get = _Forward(lambda j, n: xs[pl.ds(j, n)], _table(table, (0, 256), (0, 256)), y0, 24)
+    def get(j):
+        rows = pl.ds(j, 8, stride=SEG)
+        return jnp.concatenate([fl[rows, :], fh[rows, :]], axis=1)
+
     _chan_forward(get, 96, w, 0, 256, put_low, put_high)
     sums[0] = sq.total(rows, {("low", 1): None, ("high", 0): None, ("high", 1): None})
-    keep0 = pltpu.make_async_copy(details.at[pl.ds(0, 288)], kept.at[pl.ds(0, 288)], sems.at[8])
-    keep0.start()
     sq1 = _Squares()
 
     def put_low1(k, q, v):
@@ -502,16 +511,11 @@
 
     get = _Forward(lambda j, n: low0[pl.ds(j, n)], _table(table, (256, 128), (0, 128)), y1, 24)
     _chan_forward(get, 48, w, 1, 128, put_low1, put_high1)
-    keep1 = pltpu.make_async_copy(details.at[pl.ds(288, 96)], kept.at[pl.ds(288, 96)], sems.at[9])
-    keep1.start()
     for k in (24, 25):
         packed = jnp.where(lane < 64, a1l[k - 24], pltpu.roll(a1l[k], 64, 1))
         right[24 + k] = packed
         left[24 + k] = packed
     sums[1] = sq1.total(rows, {("low", 0): _ones(_mask(lane, OWN_HIGH1, 0, 64)), ("high", 0): None})
-    next_table.wait()
-    keep0.wait()
-    keep1.wait()
 
 
 def _bands(details):
@@ -522,21 +526,29 @@
     return out
 
 
+def _fetch_kernel(sc, after, back_all, coarse_all, back_table, coarse_table, sems):
+    del after
+    copies = []
+    for src, dst, parts in ((back_all.at[sc[1]], back_table, 4), (coarse_all, coarse_table, 4)):
+        n = dst.shape[1] // parts
+        for i in range(2):
+            for k in range(parts):
+                rows = pl.ds(n * k, n)
+                copies.append(pltpu.make_async_copy(src.at[i, rows], dst.at[i, rows], sems.at[len(copies)]))
+    for c in copies:
+        c.start()
+    for c in copies:
+        c.wait()
+
+
 def _rim_kernel(
-    sc, rim_in, from_left, from_right, low0, a1l, own_sums, table, w,
-    kept, message_out, payload_out,
-    details, message, payload, rim, y0, y1, x2, y2, y3, y4, y5, l5, sems,
+    sc, rim_in, from_left, from_right, low0, a1l, own_sums, table, w, after,
+    details, payload,
+    rim, y0, y1, x2, y2, y3, y4, y5, l5, h5, flat,
 ):
+    del after
     core = sc[0]
     rlow0, rhigh0, r1l, r1h, a2l, a2h, a3l, a3h, a4l, a4h, a5l, a5h = _bands(details)
-    copies = []
-
-    def keep(first, last):
-        rows = pl.ds(first, last - first)
-        c = pltpu.make_async_copy(details.at[rows], kept.at[rows], sems.at[len(copies)])
-        c.start()
-        copies.append(c)
-
     lane = _lane()
     for j in range(SEG):
         g, i = j // 48, j % 48
@@ -557,7 +569,7 @@
             sq.add(("low", 0, q), _tile(value, 0))
 
         def put_high(k, q, value):
-            high[k] = _tile(value, 0)
+            high[k] = value
             sq.add(("high", 0, q), _tile(value, 0))
 
         _chan_forward(_Forward(load, t, y, step), n, w, l, lanes, put_low, put_high)
@@ -569,14 +581,12 @@
     def pick(r, k, c, n):
         return _table(table, (r, k), (c, n))
 
-    level(0, lambda j, n: rim[pl.ds(j, n)], 96, pick(256, 128, 0, 128), y0, 24, 128, rlow0, rhigh0, RIM_LOW0, RIM_HIGH0, 128)
-    keep(0, 192)
+    level(0, lambda j, n: rim[pl.ds(j, n)], 96, pick(384, 128, 0, 128), y0, 24, 128, rlow0, rhigh0, RIM_LOW0, RIM_HIGH0, 128)
 
     def load1(j, n):
         return jnp.concatenate([low0[pl.ds(j, n)], rlow0[pl.ds(j, n)]], axis=2)
 
     level(1, load1, 48, pick(0, 256, 0, 128), y1, 24, 128, r1l, r1h, RIM_LOW1, RIM_HIGH1, 64)
-    keep(192, 288)
     for j in range(48):
         h, i = j // 24, 48 + j % 24
         b, a = from_left[i], from_right[i]
@@ -587,31 +597,26 @@
         x2[j, :, 0:128] = jnp.where(lane < 64, a1l[j], a)
         x2[j, :, 128:256] = jnp.where(lane < 64, b, r1l[j])
     level(2, lambda j, n: x2[pl.ds(j, n)], 24, pick(0, 256, 128, 128), y2, 24, 128, a2l, a2h, LOW2, HIGH2, 32)
-    level(3, lambda j, n: a2l[pl.ds(j, n)], 12, pick(256, 128, 128, 128), y3, 24, 128, a3l, a3h, LOW3, HIGH3, 16)
-    keep(288, 360)
-    level(4, lambda j, n: a3l[pl.ds(j, n)], 6, pick(512, 128, 0, 128), y4, 12, 128, a4l, a4h, LOW4, HIGH4, 8)
-    level(5, lambda j, n: a4l[pl.ds(j, n)], 3, pick(384, 128, 0, 256), y5, 6, 256, l5, a5h, LOW5, HIGH5, 4)
+    level(3, lambda j, n: a2l[pl.ds(j, n)], 12, pick(0, 128, 256, 128), y3, 24, 128, a3l, a3h, LOW3, HIGH3, 16)
+    level(4, lambda j, n: a3l[pl.ds(j, n)], 6, pick(128, 128, 256, 128), y4, 12, 128, a4l, a4h, LOW4, HIGH4, 8)
+    level(5, lambda j, n: a4l[pl.ds(j, n)], 3, pick(256, 128, 0, 256), y5, 6, 256, l5, h5, LOW5, HIGH5, 4)
     sub = _sublane(128)
-    line = jnp.zeros((8, 128), F32)
     for j in range(3):
-        a = l5[j, :, 0:128]
-        a5l[j] = a
-        message[j] = jnp.where(lane < 64, a5h[j], pltpu.roll(a, 64, 1))
-        line = line + jnp.where(lane // 4 == 8 * j + sub, l5[j, :, 128:256], 0.0)
-    keep(360, 378)
-    copies.append(pltpu.make_async_copy(message, message_out, sems.at[4]))
-    copies[-1].start()
+        a5l[j] = l5[j, :, 0:128]
+        a5h[j] = h5[j, :, 0:128]
+        flat[pl.ds(j, 8, stride=3), :] = jnp.where(lane % 16 < 7, l5[j, :, 128:256], h5[j, :, 128:256])
     sums = jnp.zeros((8, 128), F32)
     for l in range(LEVELS):
         sums = jnp.where(sub == l, jnp.sum(totals[l], axis=0, keepdims=True), sums)
-    sums = jnp.sum(sums, axis=1, keepdims=True)
-    line = line + jnp.where((lane == 96 + sub) & (sub < LEVELS), sums, 0.0)
-    line = jnp.sum(line, axis=0, keepdims=True)
-    payload[...] = jnp.broadcast_to(line, payload.shape)
-    copies.append(pltpu.make_async_copy(payload, payload_out, sems.at[5]))
-    copies[-1].start()
-    for c in copies:
-        c.wait()
+    sums = jnp.where((lane == 16 * sub + 13) & (sub < LEVELS), jnp.sum(sums, axis=1, keepdims=True), 0.0)
+    lines = []
+    for h in range(2):
+        mine = flat[pl.ds(pl.multiple_of(8 * core + 8 * h, 8), 8), :]
+        mine = jnp.where(lane // 16 == sub, mine, 0.0)
+        lines.append(jnp.sum(mine + sums if h == 0 else mine, axis=0, keepdims=True))
+    block = jnp.where(sub % 2 == 0, lines[0], lines[1])
+    for i in range(64):
+        payload[pl.ds(8 * i, 8), :] = block
 
 
 def _shrink(v, limit):
@@ -619,79 +624,68 @@
 
 
 def _back_kernel(
-    sc, g, near_left_all, near_right_all, coarse_all, v_all, back_all, own_kept, rim_kept, w,
+    sc, g, coarse_table, table, own_details, rim_details, w,
     out,
-    near_left, near_right, w_all, table, own_details, rim_details, v, gt, x5l, x5h, y5, y4, y3, y2, y1, y0, c4, c3, c2, c1, c0, fa, fb, sems,
+    gt, nears, cur, x5l, x5h, y5, y4, y3, y2, y1, y0, c4, c3, c2, c1, c0, fa, fb, sems,
 ):
-    core, variant = sc[0], sc[1]
+    core, place = sc[0], sc[2]
     rlow0, rhigh0, r1l, r1h, a2l, a2h, a3l, a3h, a4l, a4h, a5l, a5h = _bands(rim_details)
     dlow0, dhigh0, dhigh1 = (own_details.at[pl.ds(96 * i, 96)] for i in range(3))
     a1l, a1h = (own_details.at[pl.ds(288 + 48 * i, 48)] for i in range(2))
-    v[...] = jnp.zeros(v.shape, BF16)
-    small = pl.ds(288, 90)
-    large = pl.ds(0, 288)
-    copies = [
-        pltpu.make_async_copy(src, dst, sems.at[3 + i])
-        for i, (src, dst) in enumerate(
-            (
-                (coarse_all, w_all),
-                (v_all.at[sc[2]], v.at[:, pl.ds(0, 16), :]),
-                (near_left_all, near_left),
-                (near_right_all, near_right),
-                (rim_kept.at[small], rim_details.at[small]),
-                (back_all.at[variant], table),
-                (own_kept, own_details),
-                (rim_kept.at[large], rim_details.at[large]),
-            )
-        )
-    ]
-    for c in copies:
-        c.start()
     lane = _lane()
     lane1 = _lane(1)
-    total = jnp.sum(g[...], axis=0, keepdims=True)
+    sub = _sublane(128)
+    for h in range(2):
+        half = g[pl.ds(h, 256, stride=2), :]
+        if h == 0:
+            total = jnp.sum(half, axis=0, keepdims=True)
+        for c in range(2):
+            gt[c, h] = jnp.transpose(half[NT * c : NT * c + NT])
     limits = []
     for l in range(LEVELS):
         entries = 3 * (C >> (l + 1)) * (S >> (l + 1))
-        s = jnp.sum(jnp.where(lane1 == 96 + l, total, 0.0), axis=1, keepdims=True)
+        s = jnp.sum(jnp.where(lane1 == 16 * l + 13, total, 0.0), axis=1, keepdims=True)
         limits.append(jnp.sqrt(s * (1.0 / entries) + FLOOR))
-    gt[0] = jnp.transpose(g[0:128])
-    gt[1] = jnp.transpose(g[128:256])
     rows = [
-        jnp.concatenate([gt[c, pl.ds(m, 24, stride=4), :] for m in range(4)], axis=1) for c in range(2)
+        jnp.concatenate([gt[c, h, pl.ds(m, 8, stride=16), :] for m in range(4)], axis=1)
+        for c in range(2)
+        for h in range(2)
     ]
-    copies[0].wait()
-    coarse = _dot3(jnp.concatenate(rows, axis=0), lambda i: w_all[i])
-    position = lax.broadcasted_iota(jnp.int32, (48, 512), 1)
-    highs = position >= (S >> (LEVELS + COARSE))
-    square = jnp.where(highs, coarse * coarse, 0.0)
-    square = square[:, 0:128] + square[:, 128:256] + square[:, 256:384] + square[:, 384:512]
-    kept = jnp.zeros((8, 128), F32)
-    row = 3 * _sublane(128)
-    for j in range(3):
-        kept = kept + jnp.where(row + j < 16, square[8 * j : 8 * j + 8], 0.0)
-        kept = kept + jnp.where(row + j >= 8, square[24 + 8 * j : 32 + 8 * j], 0.0)
-    square = jnp.sum(jnp.sum(kept, axis=0, keepdims=True), axis=1, keepdims=True)
+    coarse = _dot3(jnp.concatenate(rows, axis=0), lambda i: coarse_table[i, 0:512, :])
+    highs = lax.broadcasted_iota(jnp.int32, (32, 512), 1) >= (S >> (LEVELS + COARSE))
+    square = jnp.sum(jnp.where(highs, coarse * coarse, 0.0), axis=0, keepdims=True)
+    square = jnp.sum(square, axis=1, keepdims=True)
     entries = (C >> LEVELS) * ((S >> LEVELS) - (S >> (LEVELS + COARSE)))
     limit = jnp.sqrt(square * (1.0 / entries) + FLOOR)
     coarse = jnp.where(highs, _shrink(coarse, limit), coarse)
-    mine = jnp.where(core == 0, coarse[0:24], coarse[24:48])
-    mine = jnp.concatenate([mine, jnp.zeros((8, 512), F32)], axis=0)
-    hi = mine.astype(BF16)
-    lo = (mine - hi.astype(F32)).astype(BF16)
-    for c in copies[1:6]:
-        c.wait()
+    hi = coarse.astype(BF16)
+    lo = (coarse - hi.astype(F32)).astype(BF16)
+    for side, other in enumerate((jnp.maximum(place - 1, 0), jnp.minimum(place + 1, NT - 1))):
+        for c in range(2):
+            for h in range(2):
+                line = jnp.broadcast_to(g[pl.ds(2 * (NT * c + other) + h, 1), :], (8, 128))
+                near = line
+                for k in range(1, 8):
+                    near = jnp.where(sub == k, pltpu.roll(line, 128 - 16 * k, 1), near)
+                nears[side, pl.ds(16 * c + 8 * h, 8), :] = near
     for k in range(3):
-        before, after = near_left[k], near_right[k]
-        at = lane % 4
-        for ref, own, roll in ((x5h, a5h, 0), (x5l, a5l, 64)):
-            a = pltpu.roll(before, (roll + 127) % 128, 1)
-            b = pltpu.roll(after, (roll + 1) % 128, 1)
-            ref[k] = jnp.where(at == 1, own[k], jnp.where(at == 0, a, b))
+        rows = pl.ds(8 * core + k, 8, stride=3)
+        before, after = nears[0, rows, :], nears[1, rows, :]
+        v = a5h[k]
+        for at, near, shift in ((1, before, 122), (9, after, 2), (17, before, 7), (25, after, 15)):
+            v = jnp.where((lane >= at) & (lane < at + 3), pltpu.roll(near, shift, 1), v)
+        x5h[k] = v
+        v = a5l[k]
+        for at, near, shift in ((17, before, 13), (25, after, 21)):
+            v = jnp.where((lane >= at) & (lane < at + 3), pltpu.roll(near, shift, 1), v)
+        x5l[k] = v
+
     def nt(a, b):
         return lax.dot_general(a, b, (((1,), (1,)), ((), ())), preferred_element_type=F32)
 
-    current = nt(hi, v[0]) + nt(lo, v[0]) + nt(hi, v[1])
+    rows = pl.ds(pl.multiple_of(512 + 16 * (place // 4), 16), 128)
+    current = nt(hi, coarse_table[0, rows, :]) + nt(lo, coarse_table[0, rows, :]) + nt(hi, coarse_table[1, rows, :])
+    cur[...] = pltpu.roll(current, (128 - 4 * (place % 4)) % 128, 1)
 
     def level(l, get_current, low, high, n, y, t, nxt, step, needed):
         tl = jnp.broadcast_to(limits[l] * (1.0 / KS), (8, 128))
@@ -711,13 +705,11 @@
         return _table(table, (r, k), (c, n))
 
     level(
-        5, lambda k: current[8 * k : 8 * k + 8], x5l, x5h, 3, y5, pick(896, 128, 0, 128), c4, 6, lambda i: i < 32
+        5, lambda k: cur[pl.ds(8 * core + k, 8, stride=3), :], x5l, x5h, 3, y5, pick(896, 128, 0, 128), c4, 6, lambda i: i < 12
     )
     level(4, lambda k: c4[k], a4l, a4h, 6, y4, pick(768, 128, 128, 128), c3, 12, lambda i: i < 32)
     level(3, lambda k: c3[k], a3l, a3h, 12, y3, pick(768, 128, 0, 128), c2, 24, lambda i: i < 64)
-    level(2, lambda k: c2[k], a2l, a2h, 24, y2, pick(640, 128, 0, 256), c1, 24, lambda i: i < 85)
-    for c in copies[6:]:
-        c.wait()
+    level(2, lambda k: c2[k], a2l, a2h, 24, y2, pick(640, 128, 0, 256), c1, 24, lambda i: i < 89)
     tl = jnp.broadcast_to(limits[1] * (1.0 / KS), (8, 256))
     th = jnp.broadcast_to(limits[1] * KS, (8, 256))
     lane2 = lax.broadcasted_iota(jnp.int32, (8, 256), 1)
@@ -756,7 +748,7 @@
     _chan_inverse(get_low0, get_high0, 96, w, 0, 384, put0)
     at_own = pl.multiple_of(core * HALO, 8)
     last = [
-        pltpu.make_async_copy(buf.at[pl.ds(at_own, OWN)], out.at[:, pl.ds(128 * i, 128)], sems.at[1 + i])
+        pltpu.make_async_copy(buf.at[pl.ds(at_own, OWN)], out.at[:, pl.ds(128 * i, 128)], sems.at[i])
         for i, buf in enumerate((fa, fb))
     ]
     for c in last:
@@ -798,39 +790,42 @@
     variant = jnp.where(place == 0, 0, jnp.where(place == NT - 1, 2, 1))
     sc = jnp.stack([core, variant, place]).astype(jnp.int32)
     dma = pltpu.SemaphoreType.DMA
-    (sent,) = _call(_half_kernel, "half", 2, (sc, record), [SM, HBM], [(HALO, 256)], [ANY], [dma((4,))])
-    recv = lax.ppermute(sent, "chan", [(0, 1), (1, 0)])
-    right, left, rim_in, low0, a1l, sums, w, rim_table, own_kept = _call(
-        _own_kernel, "own", 20,
-        (sc, record, recv, gauge_table, gauge_index, tables["own"], tables["rim"]),
-        [SM, HBM, ANY, HBM, HBM, HBM, HBM],
-        [(72, 8, 128), (72, 8, 128), (SEG, 8, 128), (96, 8, 128), (48, 8, 128), (2, 8, 128),
-         (LEVELS, 3, 8, 128), jax.ShapeDtypeStruct((2, 640, 256), BF16), (384, 8, 128)],
-        [VM] * 8 + [HBM],
-        [(LEVELS, GTAB), pltpu.VMEM((LEVELS, NBLK), jnp.int32), pltpu.VMEM((2, 384, 256), BF16), (384, 8, 128),
-         (8 * SEG, 128), (8 * SEG, 128), (SEG, 8, 256), (SEG, 8, 256), (96, 8, 128), dma((10,))],
+    recv = lax.ppermute(record, "chan", [(0, 1), (1, 0)])
+    low, high, ends, own_table, rim_table, w = _call(
+        _load_kernel, "load", 12, (sc, record, gauge_table, gauge_index, tables["own"], tables["rim"]),
+        [SM] + [HBM] * 5,
+        [(OWN, 128), (OWN, 128), (OWN, 128), jax.ShapeDtypeStruct((2, 384, 256), BF16),
+         jax.ShapeDtypeStruct((2, 512, 384), BF16), (LEVELS, 3, 8, 128)],
+        [VM] * 6,
+        [(OWN, 256), (LEVELS, GTAB), pltpu.VMEM((LEVELS, NBLK), jnp.int32), dma((8,))],
+    )
+    right, left, rim_in, low0, a1l, own_details, sums = _call(
+        _own_kernel, "own", 12, (sc, recv, low, high, ends, own_table, w), [SM] + [VM] * 6,
+        [(72, 8, 128), (72, 8, 128), (SEG, 8, 128), (96, 8, 128), (48, 8, 128), (384, 8, 128), (2, 8, 128)],
+        [VM] * 7,
+        [(8 * SEG, 128), (8 * SEG, 128), (8 * SEG, 128), (48 * 2, 8, 128)],
     )
     from_left, from_right = _shift(right, 1), _shift(left, -1)
-    rim_kept, message, payload = _call(
-        _rim_kernel, "rim", 16, (sc, rim_in, from_left, from_right, low0, a1l, sums, rim_table, w),
-        [SM] + [VM] * 8, [(378, 8, 128), (3, 8, 128), (256, 128)], [HBM] * 3,
-        [(378, 8, 128), (3, 8, 128), (256, 128),
-         (SEG, 8, 128), (SEG, 8, 128), (96, 8, 128), (48, 8, 256), (48, 8, 128), (24, 8, 128), (12, 8, 128),
-         (6, 8, 256), (3, 8, 256), dma((6,))],
+    back_table, coarse_table = _call(
+        _fetch_kernel, "fetch", 2, (sc, sums, tables["back"], tables["coarse"]), [SM, VM, HBM, HBM],
+        [jax.ShapeDtypeStruct((2, 1024, 256), BF16), jax.ShapeDtypeStruct((2, 1152, 512), BF16)], [VM] * 2,
+        [dma((16,))],
+    )
+    rim_details, payload = _call(
+        _rim_kernel, "rim", 16, (sc, rim_in, from_left, from_right, low0, a1l, sums, rim_table, w, back_table), [SM] + [VM] * 8 + [ANY],
+        [(378, 8, 128), (512, 128)], [VM] * 2,
+        [(SEG, 8, 128), (SEG, 8, 128), (96, 8, 128), (48, 8, 256), (48, 8, 128), (24, 8, 128), (12, 8, 128),
+         (6, 8, 256), (3, 8, 256), (3, 8, 256), (24, 128)],
     )
     everyone = lax.all_to_all(payload, ("chan", "tm"), split_axis=0, concat_axis=0, tiled=True)
-    near_left, near_right = _shift(message, 1), _shift(message, -1)
     (out,) = _call(
-        _back_kernel, "back", 24,
-        (sc, everyone, near_left, near_right, tables["w"], tables["v"], tables["back"], own_kept, rim_kept, w),
-        [SM, VM] + [HBM] * 7 + [VM], [(OWN, 256)], [HBM],
+        _back_kernel, "back", 24, (sc, everyone, coarse_table, back_table, own_details, rim_details, w),
+        [SM] + [VM] * 6, [(OWN, 256)], [HBM],
         [
-            (3, 8, 128), (3, 8, 128), pltpu.VMEM((2, 512, 512), BF16), pltpu.VMEM((2, 1024, 256), BF16),
-            (384, 8, 128), (378, 8, 128),
-            pltpu.VMEM((2, 128, 512), BF16), (2, 128, 128), (3, 8, 128), (3, 8, 128),
+            (2, 2, 128, 128), (2, 32, 128), (32, 128), (3, 8, 128), (3, 8, 128),
             (6, 8, 128), (12, 8, 128), (24, 8, 128), (48, 8, 128), (96, 8, 256), (SEG, 8, 384),
             (6, 8, 128), (12, 8, 128), (24, 8, 128), (48, 8, 256), (96, 8, 256),
-            (8 * SEG, 128), (8 * SEG, 128), dma((11,)),
+            (8 * SEG, 128), (8 * SEG, 128), dma((2,)),
         ],
     )
     return out

time: 70 us -> 62.1 us (0.89)
  the two profiles are of different devices: /device:TPU:6 before, /device:TPU:1 now
where the time goes in v3:
time: 62.1 us; the launch traced here: 61.9 us
  blocking collectives  31.4 us (51%)
  Pallas kernels  17.4 us (28%)
  waiting for transfers between devices  6.59 us (11%)
  starting transfers between devices  6.33 us (10%)
    all_to_all x1, blocking collectives, shards(): lax.all_to_all(payload, ('chan', 'tm'), split_axis=0, concat_axis=0, tile...  31.4 us
    pallas_call x5, Pallas kernels, _call(): pl.pallas_call(kernel, out_shape=[pltpu.HBM(s.shape, s.dtype) if spec is...  17.4 us
    ppermute x2, waiting for transfers between devices, _shift(): lax.ppermute(v, 'tm', [(i, i + by) for i in range(NT) if 0 <= i + by < NT])  6.59 us
    ppermute x1, starting transfers between devices, shards(): recv = lax.ppermute(record, 'chan', [(0, 1), (1, 0)])  3.24 us
    ppermute x2, starting transfers between devices, _shift(): lax.ppermute(v, 'tm', [(i, i + by) for i in range(NT) if 0 <= i + by < NT])  3.09 us
  transfers between devices with their start and end apart: 3, of which 2 were waited for; matrix products, arithmetic and copies ran while one was open for 0% of the time, Pallas kernels for 9%

profile of v3, /device:TPU:1, one launch (start us, length us, event | category | flops | bytes accessed | tf_op | source)
XLA Modules:
  0.0 61.9 jit_solution(14139869033537550514)
XLA Ops:
  0.0 3.2 %collective-permute-start = (f32[1024,256]{1,0:T(8,128)}, f32[1024,256]{1,0:T(8,128)S(1)}, u32[]{:S(2)}, u32[]{:S(2)}) collective-permute-start(f32[1024,256]{1,0:T(8,128)} %x_all.1), channel_id=1, source_target_pairs={{0,1},{1,0},{2,3},{3,2},{4,5},{5,4},{6,7},{7,6},{8,9},{9,8},{10,11... | collective-permute-start | bytes 3145736 | tf_op jit(solution)/shard_map/ppermute | solution.py:793
  3.2 0.1 pad_add_fusion.sc
  3.3 2.8 %load.1 = (f32[1024,128]{1,0:T(8,128)S(1)}, f32[1024,128]{1,0:T(8,128)S(1)}, f32[1024,128]{1,0:T(8,128)S(1)}, bf16[2,384,256]{2,1,0:T(8,128)(2,1)S(1)}, bf16[2,5...) custom-call(s32[3]{0:T(128)S(1)} %pad_add_fusion.sc, f32[1024,256]{1,0:T(8,128)} %x_all.1, f32[6,8]{1,0:T(8,128)} %gauge_table_all.1, ...), custom_call_target="tpu_custom_call" | custom-call | tf_op jit(solution)/shard_map/load/pallas_call | solution.py:771
  6.1 0.0 collective-permute-done.recv
  6.1 2.7 %own.1 = (f32[72,8,128]{2,1,0:T(8,128)S(1)}, f32[72,8,128]{2,1,0:T(8,128)S(1)}, f32[192,8,128]{2,1,0:T(8,128)S(1)}, f32[96,8,128]{2,1,0:T(8,128)S(1)}, f32[48,8,...) custom-call(s32[3]{0:T(128)S(1)} %pad_add_fusion.sc, ...), custom_call_target="tpu_custom_call" | custom-call | tf_op jit(solution)/shard_map/own/pallas_call | solution.py:771
  8.8 1.8 %collective-permute-start.1 = (f32[72,8,128]{2,1,0:T(8,128)S(1)}, f32[72,8,128]{2,1,0:T(8,128)S(1)}, u32[]{:S(2)}, u32[]{:S(2)}) collective-permute-start(f32[72,8,128]{2,1,0:T(8,128)S(1)} %get-tuple-element.28), channel_id=1, source_target_pairs={{0,2},{2,4},{4,6},{6,8},{8,10},{10,12},{12,14},{14,16},{16,18},{18... | collective-permute-start | bytes 884744 | tf_op jit(solution)/shard_map/ppermute | solution.py:783
  10.6 1.3 %collective-permute-start.2 = (f32[72,8,128]{2,1,0:T(8,128)S(1)}, f32[72,8,128]{2,1,0:T(8,128)S(1)}, u32[]{:S(2)}, u32[]{:S(2)}) collective-permute-start(f32[72,8,128]{2,1,0:T(8,128)S(1)} %get-tuple-element.29), channel_id=1, source_target_pairs={{2,0},{4,2},{6,4},{8,6},{10,8},{12,10},{14,12},{16,14},{18,16},{20... | collective-permute-start | bytes 884744 | tf_op jit(solution)/shard_map/ppermute | solution.py:783
  11.9 2.7 %fetch.1 = (bf16[2,1024,256]{2,1,0:T(8,128)(2,1)S(1)}, bf16[2,1152,512]{2,1,0:T(8,128)(2,1)S(1)}) custom-call(s32[3]{0:T(128)S(1)} %pad_add_fusion.sc, f32[2,8,128]{2,1,0:T(8,128)S(1)} %get-tuple-element.32.after.own_sums, bf16[3,2,1024,256]{3,2,1,0:T(8,128)(2,1)} %constant.26.clone.back_all, bf16[2,1152,512]{2,1,0:T(8,128)(2,1)} %constant.27.clone.coarse_all), custom_call_target="tpu_custom_call" | custom-call | tf_op jit(solution)/shard_map/fetch/pallas_call | solution.py:771
  14.6 2.4 %collective-permute-done.1.from_left = f32[72,8,128]{2,1,0:T(8,128)S(1)} collective-permute-done((f32[72,8,128]{2,1,0:T(8,128)S(1)}, f32[72,8,128]{2,1,0:T(8,128)S(1)}, u32[]{:S(2)}, u32[]{:S(2)}) %collective-permute-start.1) | collective-permute-done | bytes 294944 | tf_op jit(solution)/shard_map/ppermute | solution.py:783
  17.0 4.2 %collective-permute-done.2.from_right = f32[72,8,128]{2,1,0:T(8,128)S(1)} collective-permute-done((f32[72,8,128]{2,1,0:T(8,128)S(1)}, f32[72,8,128]{2,1,0:T(8,128)S(1)}, u32[]{:S(2)}, u32[]{:S(2)}) %collective-permute-start.2) | collective-permute-done | bytes 294944 | tf_op jit(solution)/shard_map/ppermute | solution.py:783
  21.2 2.6 %rim.1 = (f32[378,8,128]{2,1,0:T(8,128)S(1)}, f32[512,128]{1,0:T(8,128)S(1)}) custom-call(s32[3]{0:T(128)S(1)} %pad_add_fusion.sc, f32[192,8,128]{2,1,0:T(8,128)S(1)} %get-tuple-element.27.rim_in, f32[72,8,128]{2,1,0:T(8,128)S(1)} %collective-permute-done.1.from_left, f32[72,8,128]{2,1,0:T(8,128)S(1)} %collective-permute-done.2.from_right, ...), custom_call_target="tpu_custom_call" | custom-call | tf_op jit(solution)/shard_map/rim/pallas_call | solution.py:771
  23.8 31.4 %all_to_all.11 = f32[256,2,128]{2,1,0:T(2,128)S(1)} all-to-all(f32[256,2,128]{2,1,0:T(2,128)S(1)} %bitcast.6), channel_id=1, replica_groups=mesh['tm'=128,'chan'=2] {'chan','tm'}, dimensions={0} | all-to-all | bytes 524288 | tf_op jit(solution)/shard_map/all_to_all | solution.py:820
  55.2 6.7 %back.1 = f32[1024,256]{1,0:T(8,128)} custom-call(s32[3]{0:T(128)S(1)} %pad_add_fusion.sc, f32[512,128]{1,0:T(8,128)S(1)} %bitcast.5, bf16[2,1152,512]{2,1,0:T(8,128)(2,1)S(1)} %get-tuple-element.36.coarse_table, bf16[2,1024,256]{2,1,0:T(8,128)(2,1)S(1)} %get-tuple-element.34.after.table, f32[384,8,128]{2,1,0:T(8,128)S(1)} %get-tuple-element.37.own_details, ...), custom_call_target="tpu_custom_call" | custom-call | tf_op jit(solution)/shard_map/back/pallas_call | solution.py:771
Async XLA Ops:
  0.0 6.1 %collective-permute-start = (f32[1024,256]{1,0:T(8,128)}, f32[1024,256]{1,0:T(8,128)S(1)}, u32[]{:S(2)}, u32[]{:S(2)}) collective-permute-start(f32[1024,256]{1,0:T(8,128)} %x_all.1), channel_id=1, source_target_pairs={{0,1},{1,0},{2,3},{3,2},{4,5},{5,4},{6,7},{7,6},{8,9},{9,8},{10,11... | collective-permute-start | bytes 3145736 | tf_op jit(solution)/shard_map/ppermute | solution.py:793
  8.8 8.2 %collective-permute-start.1 = (f32[72,8,128]{2,1,0:T(8,128)S(1)}, f32[72,8,128]{2,1,0:T(8,128)S(1)}, u32[]{:S(2)}, u32[]{:S(2)}) collective-permute-start(f32[72,8,128]{2,1,0:T(8,128)S(1)} %get-tuple-element.28), channel_id=1, source_target_pairs={{0,2},{2,4},{4,6},{6,8},{8,10},{10,12},{12,14},{14,16},{16,18},{18... | collective-permute-start | bytes 884744 | tf_op jit(solution)/shard_map/ppermute | solution.py:783
  10.6 10.6 %collective-permute-start.2 = (f32[72,8,128]{2,1,0:T(8,128)S(1)}, f32[72,8,128]{2,1,0:T(8,128)S(1)}, u32[]{:S(2)}, u32[]{:S(2)}) collective-permute-start(f32[72,8,128]{2,1,0:T(8,128)S(1)} %get-tuple-element.29), channel_id=1, source_target_pairs={{2,0},{4,2},{6,4},{8,6},{10,8},{12,10},{14,12},{16,14},{18,16},{20... | collective-permute-start | bytes 884744 | tf_op jit(solution)/shard_map/ppermute | solution.py:783

commit v4 on v3

--- a/solution.py
+++ b/solution.py
@@ -99,8 +99,8 @@
 OWN_LOW0 = _run(2, 126, 2)
 OWN_HIGH0 = _run(2, 126, 130)
 RIM_LOW0 = {**_run(-10, 2, 0), **_run(126, 137, 12)}
-RIM_HIGH0 = {**_run(-2, 2, 32), **_run(126, 130, 36)}
-RIM_IN0 = {**_run(0, 32, 0), **_run(-32, 0, 32), **_run(256, 288, 64), **_run(224, 256, 96)}
+RIM_HIGH0 = {**_run(-2, 2, 23), **_run(126, 130, 27)}
+RIM_IN0 = {**_run(-32, 0, 0), **_run(0, 32, 128), **_run(224, 256, 256), **_run(256, 288, 384)}
 OWN_LOW1 = _run(3, 61, 3)
 OWN_HIGH1 = _run(2, 61, 66)
 RIM_LOW1 = {**_run(-3, 3, 64), **_run(61, 67, 70)}
@@ -155,6 +155,8 @@
         lows, highs = t5[:, 4:8].copy(), t5[:, 20:24].copy()
         sixteen = np.concatenate([lows, highs[:, 1:], lows[:, 1:], highs[:, 1:], np.zeros((128, 3))], axis=1)
         t5[:, 128:] = np.tile(sixteen, (1, 8))
+        one = fw(RIM_IN0, RIM_LOW0, RIM_HIGH0, 512, 128, a[0], b[0], 1.0)
+        rim0 = sum(np.roll(one, (32 * g, 32 * g), (0, 1)) for g in range(4))
         rim.append(
             _bundle(
                 (
@@ -163,9 +165,9 @@
                     (0, 256, fw(LOW2, LOW3, HIGH3, 128, 128, a[3], b[3], KS)),
                     (128, 256, fw(LOW3, LOW4, HIGH4, 128, 128, a[4], b[4], KS)),
                     (256, 0, t5),
-                    (384, 0, fw(RIM_IN0, RIM_LOW0, RIM_HIGH0, 128, 128, a[0], b[0], 1.0)),
+                    (384, 0, rim0),
                 ),
-                512,
+                896,
                 384,
             )
         )
@@ -173,17 +175,26 @@
         high0 = {**OWN_HIGH0, **{k: 256 + v for k, v in RIM_HIGH0.items()}}
         low1 = {**OWN_LOW1, **{k: 128 + v for k, v in RIM_LOW1.items()}}
         high1 = {**OWN_HIGH1, **{k: 128 + v for k, v in RIM_HIGH1.items()}}
+        full = inv(low0, high0, _run(0, 256, 0), 288, 256, a[0], b[0], 1.0)
+        ends = np.zeros((128, 128))
+        for i in range(32):
+            for c in range(-7, 8):
+                ends[i, c % 128] = full[256 + i, c % 256]
+        ends = sum(np.roll(ends, (32 * g, 32 * g), (0, 1)) for g in range(4))
+        s1 = inv(low1, high1, _part(IN1, -1, 130), 256, 256, a[1], b[1], 1.0 / KS)
+        s1[:, 128:] = np.tile(s1[:, 128:160], (1, 4))
         back.append(
             _bundle(
                 (
-                    (0, 0, inv(low0, high0, _run(0, 256, 0), 384, 256, a[0], b[0], 1.0)),
-                    (384, 0, inv(low1, high1, _part(IN1, -1, 130), 256, 256, a[1], b[1], 1.0 / KS)),
-                    (640, 0, inv(LOW2, HIGH2, _part(low1, -2, 67), 128, 256, a[2], b[2], 1.0 / KS)),
-                    (768, 0, inv(LOW3, HIGH3, _part(LOW2, -2, 36), 128, 128, a[3], b[3], 1.0 / KS)),
-                    (768, 128, inv(LOW4, HIGH4, _part(LOW3, -2, 20), 128, 128, a[4], b[4], 1.0 / KS)),
-                    (896, 0, inv(LOW5, HIGH5, _part(LOW4, -2, 12), 128, 128, a[5], b[5], 1.0 / KS)),
+                    (0, 0, full[:256]),
+                    (256, 0, s1),
+                    (512, 0, inv(LOW2, HIGH2, _part(low1, -2, 67), 128, 256, a[2], b[2], 1.0 / KS)),
+                    (640, 0, inv(LOW3, HIGH3, _part(LOW2, -2, 36), 128, 128, a[3], b[3], 1.0 / KS)),
+                    (640, 128, inv(LOW4, HIGH4, _part(LOW3, -2, 20), 128, 128, a[4], b[4], 1.0 / KS)),
+                    (768, 0, inv(LOW5, HIGH5, _part(LOW4, -2, 12), 128, 128, a[5], b[5], 1.0 / KS)),
+                    (768, 128, ends),
                 ),
-                1024,
+                896,
                 256,
             )
         )
@@ -229,7 +240,8 @@
     hi = x.astype(BF16)
     lo = (x - hi.astype(F32)).astype(BF16)
     d = functools.partial(jnp.dot, preferred_element_type=F32)
-    return d(hi, t(0)) + d(lo, t(0)) + d(hi, t(1))
+    both = d(jnp.concatenate([hi, lo], axis=0), t(0))
+    return both[: x.shape[0]] + both[x.shape[0] :] + d(hi, t(1))
 
 
 def _time(load, t, y, step, j):
@@ -280,6 +292,32 @@
     return v if lanes == 128 else jnp.concatenate([v] * (lanes // 128), axis=1)
 
 
+class _QuarterWrap:
+    def __init__(self):
+        self.sub, self.group = _sublane(128), _lane() // 32
+
+    def after(self, first, last):
+        moved = pltpu.roll(first, 96, 1)
+        moved = jnp.where(self.group == 3, pltpu.roll(moved, 7, 0), moved)
+        return jnp.where((self.group == 3) & (self.sub == 7), last, moved)
+
+    def before(self, last, first):
+        moved = pltpu.roll(last, 32, 1)
+        moved = jnp.where(self.group == 0, pltpu.roll(moved, 1, 0), moved)
+        return jnp.where((self.group == 0) & (self.sub == 0), first, moved)
+
+
+def _quarters(values):
+    group = _lane() // 32
+    out = []
+    for c in range(3):
+        v = values[0]
+        for g in range(1, 4):
+            v = jnp.where(group == g, values[(24 * g + 8 * c) // 32], v)
+        out.append(v)
+    return out
+
+
 class _Wrap:
     def __init__(self, lanes):
         sub = _sublane(lanes)
@@ -292,13 +330,13 @@
         return jnp.where(self.first, first, pltpu.roll(last, 1, 0))
 
 
-def _coefs(w_ref, level, lanes):
-    return [[_wide(c * w_ref[level, q], lanes) for q in range(3)] for c in (A1, B1, A2, B2)]
-
-
-def _chan_forward(get, n, w_ref, level, lanes, put_low, put_high):
-    wrap = _Wrap(lanes)
-    ca, cb, cc, cd = _coefs(w_ref, level, lanes)
+def _coefs(weights, lanes):
+    return [[_wide(c * v, lanes) for v in weights] for c in (A1, B1, A2, B2)]
+
+
+def _chan_forward(get, n, weights, lanes, put_low, put_high, wrap=None):
+    wrap = wrap or _Wrap(lanes)
+    ca, cb, cc, cd = _coefs(weights, lanes)
     per = n // 3
     first = get(0)
     e, o1, e1, o2 = {0: first}, {}, {}, {}
@@ -328,9 +366,9 @@
         low(k)
 
 
-def _chan_inverse(get_low, get_high, n, w_ref, level, lanes, put):
-    wrap = _Wrap(lanes)
-    ca, cb, cc, cd = _coefs(w_ref, level, lanes)
+def _chan_inverse(get_low, get_high, n, weights, lanes, put, wrap=None):
+    wrap = wrap or _Wrap(lanes)
+    ca, cb, cc, cd = _coefs(weights, lanes)
     per = n // 3
     o = {0: get_high(0)}
     o[-1] = wrap.before(get_high(n - 1), o[0])
@@ -387,6 +425,10 @@
 
 def _tile(v, i):
     return v[:, 128 * i : 128 * (i + 1)]
+
+
+def _blocks(w, level):
+    return [w[level, q] for q in range(3)]
 
 
 def _own_rows(core):
@@ -449,8 +491,8 @@
 
 def _own_kernel(
     sc, recv, own_low, own_high, own_ends, table, w,
-    right, left, rim_in, low0, a1l, details, sums,
-    fl, fh, fe, y1,
+    right, left, low0, a1l, fh, details, sums,
+    fl, fe, y1,
 ):
     core = sc[0]
     at_own = pl.multiple_of(core * HALO, 8)
@@ -467,7 +509,6 @@
         for g in range(4):
             j = 48 * g + i
             v = fe[pl.ds(j, 8, stride=SEG), :]
-            rim_in[j] = v
             a = pltpu.roll(v, 32 * g, 1) if g else v
             b = pltpu.roll(v, (32 * g + 32) % 128, 1) if g != 3 else v
             to_left = a if to_left is None else jnp.where(group == g, a, to_left)
@@ -478,27 +519,19 @@
     sq = _Squares()
 
     def put_low(k, q, v):
-        low0[k] = _tile(v, 0)
-        details[k] = _tile(v, 1)
-        sq.add(("low", 1, q), _tile(v, 1))
+        low0[k] = v
 
     def put_high(k, q, v):
-        details[96 + k] = _tile(v, 0)
-        details[192 + k] = _tile(v, 1)
-        sq.add(("high", 0, q), _tile(v, 0))
-        sq.add(("high", 1, q), _tile(v, 1))
-
-    def get(j):
-        rows = pl.ds(j, 8, stride=SEG)
-        return jnp.concatenate([fl[rows, :], fh[rows, :]], axis=1)
-
-    _chan_forward(get, 96, w, 0, 256, put_low, put_high)
-    sums[0] = sq.total(rows, {("low", 1): None, ("high", 0): None, ("high", 1): None})
+        details[k] = v
+        sq.add(("high", 0, q), v)
+
+    _chan_forward(lambda j: fl[pl.ds(j, 8, stride=SEG), :], 96, _blocks(w, 0), 128, put_low, put_high)
+    sums[0] = sq.total(rows, {("high", 0): None})
     sq1 = _Squares()
 
     def put_low1(k, q, v):
         a1l[k] = v
-        details[288 + k] = v
+        details[96 + k] = v
         sq1.add(("low", 0, q), v)
         if k >= 26:
             packed = jnp.where(lane < 64, a1l[k - 24], pltpu.roll(v, 64, 1))
@@ -506,11 +539,11 @@
             left[24 + k] = packed
 
     def put_high1(k, q, v):
-        details[336 + k] = v
+        details[144 + k] = v
         sq1.add(("high", 0, q), v)
 
     get = _Forward(lambda j, n: low0[pl.ds(j, n)], _table(table, (256, 128), (0, 128)), y1, 24)
-    _chan_forward(get, 48, w, 1, 128, put_low1, put_high1)
+    _chan_forward(get, 48, _blocks(w, 1), 128, put_low1, put_high1)
     for k in (24, 25):
         packed = jnp.where(lane < 64, a1l[k - 24], pltpu.roll(a1l[k], 64, 1))
         right[24 + k] = packed
@@ -520,14 +553,13 @@
 
 def _bands(details):
     out, at = [], 0
-    for n in (96, 48, 24, 12, 6, 3):
+    for n in (24, 48, 24, 12, 6, 3):
         out += [details.at[pl.ds(at, n)], details.at[pl.ds(at + n, n)]]
         at += 2 * n
     return out
 
 
-def _fetch_kernel(sc, after, back_all, coarse_all, back_table, coarse_table, sems):
-    del after
+def _aside_kernel(sc, fh, w, back_all, coarse_all, back_table, coarse_table, details, sums, sems):
     copies = []
     for src, dst, parts in ((back_all.at[sc[1]], back_table, 4), (coarse_all, coarse_table, 4)):
         n = dst.shape[1] // parts
@@ -537,31 +569,38 @@
                 copies.append(pltpu.make_async_copy(src.at[i, rows], dst.at[i, rows], sems.at[len(copies)]))
     for c in copies:
         c.start()
+    rows = _own_rows(sc[0])
+    sq = _Squares()
+
+    def put_low(k, q, v):
+        details[k] = v
+        sq.add(("low", 0, q), v)
+
+    def put_high(k, q, v):
+        details[96 + k] = v
+        sq.add(("high", 0, q), v)
+
+    _chan_forward(lambda j: fh[pl.ds(j, 8, stride=SEG), :], 96, _blocks(w, 0), 128, put_low, put_high)
+    sums[...] = sq.total(rows, {("low", 0): None, ("high", 0): None})
     for c in copies:
         c.wait()
 
 
 def _rim_kernel(
-    sc, rim_in, from_left, from_right, low0, a1l, own_sums, table, w, after,
+    sc, right, left, from_left, from_right, low0, a1l, own_sums, more_sums, table, w,
     details, payload,
     rim, y0, y1, x2, y2, y3, y4, y5, l5, h5, flat,
 ):
-    del after
     core = sc[0]
     rlow0, rhigh0, r1l, r1h, a2l, a2h, a3l, a3h, a4l, a4h, a5l, a5h = _bands(details)
     lane = _lane()
-    for j in range(SEG):
-        g, i = j // 48, j % 48
-        a = from_left[i]
-        b = from_right[i]
-        a = pltpu.roll(a, (32 - 32 * g) % 128, 1) if g != 1 else a
-        b = pltpu.roll(b, (64 - 32 * g) % 128, 1) if g != 2 else b
-        halo = jnp.where(lane < 64, a, b)
-        rim[j] = jnp.where((lane < 32) | (lane >= 96), rim_in[j], halo)
     rows = _own_rows(core)
     totals = []
 
     def level(l, load, n, t, y, step, lanes, low, high, own_low, own_high, pairs):
+        quarters = l == 0
+        weights = _blocks(w, l)
+        place = lane % 32 if quarters else lane
         sq = _Squares()
 
         def put_low(k, q, value):
@@ -572,19 +611,29 @@
             high[k] = value
             sq.add(("high", 0, q), _tile(value, 0))
 
-        _chan_forward(_Forward(load, t, y, step), n, w, l, lanes, put_low, put_high)
-        is_high = _mask(lane, own_high, 0, pairs)
-        is_low = _mask(lane, own_low, 0, pairs)
-        total = sq.total(rows, {("low", 0): _ones(is_high), ("high", 0): _ones(is_high | is_low)})
+        wrap = _QuarterWrap() if quarters else None
+        weights = _quarters(weights) if quarters else weights
+        _chan_forward(_Forward(load, t, y, step), n, weights, lanes, put_low, put_high, wrap)
+        is_high = _mask(place, own_high, 0, pairs)
+        is_low = _mask(place, own_low, 0, pairs)
+        total = sq.total(_quarters(rows) if quarters else rows, {("low", 0): _ones(is_high), ("high", 0): _ones(is_high | is_low)})
         totals.append(total + own_sums[l] if l < 2 else total)
 
     def pick(r, k, c, n):
         return _table(table, (r, k), (c, n))
 
-    level(0, lambda j, n: rim[pl.ds(j, n)], 96, pick(384, 128, 0, 128), y0, 24, 128, rlow0, rhigh0, RIM_LOW0, RIM_HIGH0, 128)
+    def load0(j, n):
+        at = pl.ds(j, n)
+        return jnp.concatenate([from_left[at], left[at], right[at], from_right[at]], axis=2)
+
+    level(0, load0, 24, pick(384, 512, 0, 128), y0, 24, 128, rlow0, rhigh0, RIM_LOW0, RIM_HIGH0, 128)
+    totals[0] = totals[0] + more_sums[...]
+    for g in range(4):
+        for i in range(24):
+            rim[24 * g + i] = pltpu.roll(rlow0[i], 128 - 32 * g, 1) if g else rlow0[i]
 
     def load1(j, n):
-        return jnp.concatenate([low0[pl.ds(j, n)], rlow0[pl.ds(j, n)]], axis=2)
+        return jnp.concatenate([low0[pl.ds(j, n)], rim[pl.ds(j, n)]], axis=2)
 
     level(1, load1, 48, pick(0, 256, 0, 128), y1, 24, 128, r1l, r1h, RIM_LOW1, RIM_HIGH1, 64)
     for j in range(48):
@@ -615,7 +664,7 @@
         mine = jnp.where(lane // 16 == sub, mine, 0.0)
         lines.append(jnp.sum(mine + sums if h == 0 else mine, axis=0, keepdims=True))
     block = jnp.where(sub % 2 == 0, lines[0], lines[1])
-    for i in range(64):
+    for i in range(32):
         payload[pl.ds(8 * i, 8), :] = block
 
 
@@ -624,23 +673,23 @@
 
 
 def _back_kernel(
-    sc, g, coarse_table, table, own_details, rim_details, w,
+    sc, mine, theirs, coarse_table, table, own_details, more_details, rim_details, w,
     out,
-    gt, nears, cur, x5l, x5h, y5, y4, y3, y2, y1, y0, c4, c3, c2, c1, c0, fa, fb, sems,
+    gt, nears, cur, x5l, x5h, y5, y4, y3, y2, y1, c4, c3, c2, c1, c0, f0, f1, f2, yr, stage, sems,
 ):
     core, place = sc[0], sc[2]
     rlow0, rhigh0, r1l, r1h, a2l, a2h, a3l, a3h, a4l, a4h, a5l, a5h = _bands(rim_details)
-    dlow0, dhigh0, dhigh1 = (own_details.at[pl.ds(96 * i, 96)] for i in range(3))
-    a1l, a1h = (own_details.at[pl.ds(288 + 48 * i, 48)] for i in range(2))
+    dhigh0, dlow0, dhigh1 = own_details.at[pl.ds(0, 96)], more_details.at[pl.ds(0, 96)], more_details.at[pl.ds(96, 96)]
+    a1l, a1h = (own_details.at[pl.ds(96 + 48 * i, 48)] for i in range(2))
     lane = _lane()
     lane1 = _lane(1)
     sub = _sublane(128)
     for h in range(2):
-        half = g[pl.ds(h, 256, stride=2), :]
+        halves = [g[pl.ds(h, NT, stride=2), :] for g in (mine, theirs)]
         if h == 0:
-            total = jnp.sum(half, axis=0, keepdims=True)
+            total = jnp.sum(halves[0] + halves[1], axis=0, keepdims=True)
         for c in range(2):
-            gt[c, h] = jnp.transpose(half[NT * c : NT * c + NT])
+            gt[c, h] = jnp.transpose(jnp.where(core == c, halves[0], halves[1]))
     limits = []
     for l in range(LEVELS):
         entries = 3 * (C >> (l + 1)) * (S >> (l + 1))
@@ -663,7 +712,8 @@
     for side, other in enumerate((jnp.maximum(place - 1, 0), jnp.minimum(place + 1, NT - 1))):
         for c in range(2):
             for h in range(2):
-                line = jnp.broadcast_to(g[pl.ds(2 * (NT * c + other) + h, 1), :], (8, 128))
+                row = pl.ds(2 * other + h, 1)
+                line = jnp.broadcast_to(jnp.where(core == c, mine[row, :], theirs[row, :]), (8, 128))
                 near = line
                 for k in range(1, 8):
                     near = jnp.where(sub == k, pltpu.roll(line, 128 - 16 * k, 1), near)
@@ -699,17 +749,17 @@
             nxt[pl.ds(j, m)] = value
 
         put = _Backward(y, t, store, step)
-        _chan_inverse(get_low, lambda k: _shrink(high[k], th), n, w, l, 128, put)
+        _chan_inverse(get_low, lambda k: _shrink(high[k], th), n, _blocks(w, l), 128, put)
 
     def pick(r, k, c, n):
         return _table(table, (r, k), (c, n))
 
     level(
-        5, lambda k: cur[pl.ds(8 * core + k, 8, stride=3), :], x5l, x5h, 3, y5, pick(896, 128, 0, 128), c4, 6, lambda i: i < 12
+        5, lambda k: cur[pl.ds(8 * core + k, 8, stride=3), :], x5l, x5h, 3, y5, pick(768, 128, 0, 128), c4, 6, lambda i: i < 12
     )
-    level(4, lambda k: c4[k], a4l, a4h, 6, y4, pick(768, 128, 128, 128), c3, 12, lambda i: i < 32)
-    level(3, lambda k: c3[k], a3l, a3h, 12, y3, pick(768, 128, 0, 128), c2, 24, lambda i: i < 64)
-    level(2, lambda k: c2[k], a2l, a2h, 24, y2, pick(640, 128, 0, 256), c1, 24, lambda i: i < 89)
+    level(4, lambda k: c4[k], a4l, a4h, 6, y4, pick(640, 128, 128, 128), c3, 12, lambda i: i < 32)
+    level(3, lambda k: c3[k], a3l, a3h, 12, y3, pick(640, 128, 0, 128), c2, 24, lambda i: i < 64)
+    level(2, lambda k: c2[k], a2l, a2h, 24, y2, pick(512, 128, 0, 256), c1, 24, lambda i: i < 89)
     tl = jnp.broadcast_to(limits[1] * (1.0 / KS), (8, 256))
     th = jnp.broadcast_to(limits[1] * KS, (8, 256))
     lane2 = lax.broadcasted_iota(jnp.int32, (8, 256), 1)
@@ -725,35 +775,55 @@
     def store1(j, m, value):
         c0[pl.ds(j, m)] = value
 
-    put1 = _Backward(y1, pick(384, 256, 0, 256), store1, 24)
-    _chan_inverse(get_low1, get_high1, 48, w, 1, 256, put1)
+    put1 = _Backward(y1, pick(256, 256, 0, 256), store1, 24)
+    _chan_inverse(get_low1, get_high1, 48, _blocks(w, 1), 256, put1)
     tl0 = jnp.broadcast_to(limits[0] * (1.0 / KS), (8, 128))
-    th0 = jnp.broadcast_to(limits[0] * KS, (8, 384))
-    rim_low = lane < 32
+    th0 = jnp.broadcast_to(limits[0] * KS, (8, 256))
+    group = lane // 32
+    rim_low = lane % 32 < 23
+
+    def get_low_rim(k):
+        now = c0[k, :, 128:256]
+        for q in range(1, 4):
+            now = jnp.where(group == q, c0[24 * q + k, :, 128:256], now)
+        return jnp.where(rim_low, now, _shrink(rlow0[k], tl0))
+
+    def store_rim(j, m, value):
+        for i in range(m):
+            for q in range(4):
+                v = pltpu.roll(value[i], 128 - 32 * q, 1) if q else value[i]
+                f2[pl.ds(48 * q + j + i, 8, stride=SEG), :] = v
+
+    put_rim = _Backward(yr, pick(768, 128, 128, 128), store_rim, 24)
+    _chan_inverse(
+        get_low_rim, lambda k: _shrink(rhigh0[k], th0[:, 0:128]), 24, _quarters(_blocks(w, 0)), 128, put_rim, _QuarterWrap()
+    )
 
     def get_low0(k):
-        now = c0[k]
-        rim = jnp.where(rim_low, _tile(now, 1), _shrink(rlow0[k], tl0))
-        return jnp.concatenate([_tile(now, 0), _shrink(dlow0[k], tl0), rim], axis=1)
+        return jnp.concatenate([c0[k, :, 0:128], _shrink(dlow0[k], tl0)], axis=1)
 
     def get_high0(k):
-        return _shrink(jnp.concatenate([dhigh0[k], dhigh1[k], rhigh0[k]], axis=1), th0)
-
-    def store0(j, m, value):
-        for i in range(m):
-            fa[pl.ds(j + i, 8, stride=SEG), :] = value[i, :, 0:128]
-            fb[pl.ds(j + i, 8, stride=SEG), :] = value[i, :, 128:256]
-
-    put0 = _Backward(y0, pick(0, 384, 0, 256), store0, 24)
-    _chan_inverse(get_low0, get_high0, 96, w, 0, 384, put0)
+        return _shrink(jnp.concatenate([dhigh0[k], dhigh1[k]], axis=1), th0)
+
+    def put0(j, value):
+        for i, buf in enumerate((f0, f1)):
+            buf[pl.ds(j, 8, stride=SEG), :] = _tile(value, i)
+
+    _chan_inverse(get_low0, get_high0, 96, _blocks(w, 0), 256, put0)
     at_own = pl.multiple_of(core * HALO, 8)
-    last = [
-        pltpu.make_async_copy(buf.at[pl.ds(at_own, OWN)], out.at[:, pl.ds(128 * i, 128)], sems.at[i])
-        for i, buf in enumerate((fa, fb))
-    ]
-    for c in last:
-        c.start()
-    for c in last:
+    t = pick(0, 256, 0, 256)
+    wide = _lane(128)
+    copies = []
+    for r in range(0, OWN, 128):
+        rows = pl.ds(at_own + r, 128)
+        done = pl.ds(r, 128)
+        ends = f2[rows, :]
+        v = _dot3(jnp.concatenate([f0[rows, :], f1[rows, :]], axis=1), t)
+        stage[done, 0:128] = _tile(v, 0) + jnp.where(wide < 8, ends, 0.0)
+        stage[done, 128:256] = _tile(v, 1) + jnp.where(wide >= 121, ends, 0.0)
+        copies.append(pltpu.make_async_copy(stage.at[done], out.at[done], sems.at[r // 128]))
+        copies[-1].start()
+    for c in copies:
         c.wait()
 
 
@@ -795,37 +865,40 @@
         _load_kernel, "load", 12, (sc, record, gauge_table, gauge_index, tables["own"], tables["rim"]),
         [SM] + [HBM] * 5,
         [(OWN, 128), (OWN, 128), (OWN, 128), jax.ShapeDtypeStruct((2, 384, 256), BF16),
-         jax.ShapeDtypeStruct((2, 512, 384), BF16), (LEVELS, 3, 8, 128)],
+         jax.ShapeDtypeStruct((2, 896, 384), BF16), (LEVELS, 3, 8, 128)],
         [VM] * 6,
         [(OWN, 256), (LEVELS, GTAB), pltpu.VMEM((LEVELS, NBLK), jnp.int32), dma((8,))],
     )
-    right, left, rim_in, low0, a1l, own_details, sums = _call(
+    right, left, low0, a1l, fh, own_details, sums = _call(
         _own_kernel, "own", 12, (sc, recv, low, high, ends, own_table, w), [SM] + [VM] * 6,
-        [(72, 8, 128), (72, 8, 128), (SEG, 8, 128), (96, 8, 128), (48, 8, 128), (384, 8, 128), (2, 8, 128)],
+        [(72, 8, 128), (72, 8, 128), (96, 8, 128), (48, 8, 128), (8 * SEG, 128), (192, 8, 128), (2, 8, 128)],
         [VM] * 7,
-        [(8 * SEG, 128), (8 * SEG, 128), (8 * SEG, 128), (48 * 2, 8, 128)],
+        [(8 * SEG, 128), (8 * SEG, 128), (96, 8, 128)],
     )
     from_left, from_right = _shift(right, 1), _shift(left, -1)
-    back_table, coarse_table = _call(
-        _fetch_kernel, "fetch", 2, (sc, sums, tables["back"], tables["coarse"]), [SM, VM, HBM, HBM],
-        [jax.ShapeDtypeStruct((2, 1024, 256), BF16), jax.ShapeDtypeStruct((2, 1152, 512), BF16)], [VM] * 2,
+    back_table, coarse_table, more_details, more_sums = _call(
+        _aside_kernel, "aside", 6, (sc, fh, w, tables["back"], tables["coarse"]), [SM, VM, VM, HBM, HBM],
+        [jax.ShapeDtypeStruct((2, 896, 256), BF16), jax.ShapeDtypeStruct((2, 1152, 512), BF16), (192, 8, 128), (8, 128)],
+        [VM] * 4,
         [dma((16,))],
     )
     rim_details, payload = _call(
-        _rim_kernel, "rim", 16, (sc, rim_in, from_left, from_right, low0, a1l, sums, rim_table, w, back_table), [SM] + [VM] * 8 + [ANY],
-        [(378, 8, 128), (512, 128)], [VM] * 2,
-        [(SEG, 8, 128), (SEG, 8, 128), (96, 8, 128), (48, 8, 256), (48, 8, 128), (24, 8, 128), (12, 8, 128),
+        _rim_kernel, "rim", 16,
+        (sc, right, left, from_left, from_right, low0, a1l, sums, more_sums, rim_table, w), [SM] + [VM] * 10,
+        [(234, 8, 128), (256, 128)], [VM] * 2,
+        [(96, 8, 128), (48, 8, 128), (96, 8, 128), (48, 8, 256), (48, 8, 128), (24, 8, 128), (12, 8, 128),
          (6, 8, 256), (3, 8, 256), (3, 8, 256), (24, 128)],
     )
-    everyone = lax.all_to_all(payload, ("chan", "tm"), split_axis=0, concat_axis=0, tiled=True)
+    mine = lax.all_to_all(payload, "tm", split_axis=0, concat_axis=0, tiled=True)
+    theirs = lax.ppermute(mine, "chan", [(0, 1), (1, 0)])
     (out,) = _call(
-        _back_kernel, "back", 24, (sc, everyone, coarse_table, back_table, own_details, rim_details, w),
-        [SM] + [VM] * 6, [(OWN, 256)], [HBM],
+        _back_kernel, "back", 24, (sc, mine, theirs, coarse_table, back_table, own_details, more_details, rim_details, w),
+        [SM] + [VM] * 8, [(OWN, 256)], [HBM],
         [
             (2, 2, 128, 128), (2, 32, 128), (32, 128), (3, 8, 128), (3, 8, 128),
-            (6, 8, 128), (12, 8, 128), (24, 8, 128), (48, 8, 128), (96, 8, 256), (SEG, 8, 384),
+            (6, 8, 128), (12, 8, 128), (24, 8, 128), (48, 8, 128), (96, 8, 256),
             (6, 8, 128), (12, 8, 128), (24, 8, 128), (48, 8, 256), (96, 8, 256),
-            (8 * SEG, 128), (8 * SEG, 128), dma((2,)),
+            (8 * SEG, 128), (8 * SEG, 128), (8 * SEG, 128), (48, 8, 128), (OWN, 256), dma((8,)),
         ],
     )
     return out

time: 62.1 us -> 59.9 us (0.965)
  blocking collectives: 31.4 us -> 27.7 us
  starting transfers between devices: 6.33 us -> 8.27 us
  Pallas kernels: 17.4 us -> 15.9 us
  waiting for transfers between devices: 6.59 us -> 7.59 us
    all_to_all x1, blocking collectives: 31.4 us -> 27.7 us  [shards(): lax.all_to_all(payload, 'tm', split_axis=0, concat_axis=0, tiled=True)]
    ppermute x0 -> x1, starting transfers between devices: none -> 1.92 us  [shards(): theirs = lax.ppermute(mine, 'chan', [(0, 1), (1, 0)])]
    pallas_call x5, Pallas kernels: 17.4 us -> 15.9 us  [_call(): pl.pallas_call(kernel, out_shape=[pltpu.HBM(s.shape, s.dtype) if spec is...]
    ppermute x0 -> x1, waiting for transfers between devices: none -> 0.99 us  [shards(): theirs = lax.ppermute(mine, 'chan', [(0, 1), (1, 0)])]
  transfers between devices with their start and end apart: 3 -> 4, of which waited for: 2 -> 3; matrix products, arithmetic and copies ran while one was open for 0% -> 0% of each run, Pallas kernels for 9% -> 9%
where the time goes in v4:
time: 59.9 us; the launch traced here: 59.7 us
  blocking collectives  27.7 us (46%)
  Pallas kernels  15.9 us (27%)
  starting transfers between devices  8.27 us (14%)
  waiting for transfers between devices  7.59 us (13%)
    all_to_all x1, blocking collectives, shards(): lax.all_to_all(payload, 'tm', split_axis=0, concat_axis=0, tiled=True)  27.7 us
    pallas_call x5, Pallas kernels, _call(): pl.pallas_call(kernel, out_shape=[pltpu.HBM(s.shape, s.dtype) if spec is...  15.9 us
    ppermute x2, waiting for transfers between devices, _shift(): lax.ppermute(v, 'tm', [(i, i + by) for i in range(NT) if 0 <= i + by < NT])  6.6 us
    ppermute x1, starting transfers between devices, shards(): recv = lax.ppermute(record, 'chan', [(0, 1), (1, 0)])  3.24 us
    ppermute x2, starting transfers between devices, _shift(): lax.ppermute(v, 'tm', [(i, i + by) for i in range(NT) if 0 <= i + by < NT])  3.12 us
    ppermute x1, starting transfers between devices, shards(): theirs = lax.ppermute(mine, 'chan', [(0, 1), (1, 0)])  1.92 us
  transfers between devices with their start and end apart: 4, of which 3 were waited for; matrix products, arithmetic and copies ran while one was open for 0% of the time, Pallas kernels for 9%

profile of v4, /device:TPU:1, one launch (start us, length us, event | category | flops | bytes accessed | tf_op | source)
XLA Modules:
  0.0 59.7 jit_solution(3482437150751428616)
XLA Ops:
  0.0 3.2 %collective-permute-start = (f32[1024,256]{1,0:T(8,128)}, f32[1024,256]{1,0:T(8,128)S(1)}, u32[]{:S(2)}, u32[]{:S(2)}) collective-permute-start(f32[1024,256]{1,0:T(8,128)} %x_all.1), channel_id=1, source_target_pairs={{0,1},{1,0},{2,3},{3,2},{4,5},{5,4},{6,7},{7,6},{8,9},{9,8},{10,11... | collective-permute-start | bytes 3145736 | tf_op jit(solution)/shard_map/ppermute | solution.py:863
  3.2 0.1 pad_add_fusion.sc
  3.3 2.8 %load.1 = (f32[1024,128]{1,0:T(8,128)S(1)}, f32[1024,128]{1,0:T(8,128)S(1)}, f32[1024,128]{1,0:T(8,128)S(1)}, bf16[2,384,256]{2,1,0:T(8,128)(2,1)S(1)}, bf16[2,8...) custom-call(s32[3]{0:T(128)S(1)} %pad_add_fusion.sc, f32[1024,256]{1,0:T(8,128)} %x_all.1, f32[6,8]{1,0:T(8,128)} %gauge_table_all.1, ...), custom_call_target="tpu_custom_call" | custom-call | tf_op jit(solution)/shard_map/load/pallas_call | solution.py:841
  6.1 0.0 collective-permute-done.recv
  6.1 2.1 %own.1 = (f32[72,8,128]{2,1,0:T(8,128)S(1)}, f32[72,8,128]{2,1,0:T(8,128)S(1)}, f32[96,8,128]{2,1,0:T(8,128)S(1)}, f32[48,8,128]{2,1,0:T(8,128)S(1)}, f32[1536,1...) custom-call(s32[3]{0:T(128)S(1)} %pad_add_fusion.sc, ...), custom_call_target="tpu_custom_call" | custom-call | tf_op jit(solution)/shard_map/own/pallas_call | solution.py:841
  8.2 1.8 %collective-permute-start.1 = (f32[72,8,128]{2,1,0:T(8,128)S(1)}, f32[72,8,128]{2,1,0:T(8,128)S(1)}, u32[]{:S(2)}, u32[]{:S(2)}) collective-permute-start(f32[72,8,128]{2,1,0:T(8,128)S(1)} %get-tuple-element.29.right), channel_id=1, source_target_pairs={{0,2},{2,4},{4,6},{6,8},{8,10},{10,12},{12,14},{14,16},{16,18},{18... | collective-permute-start | bytes 884744 | tf_op jit(solution)/shard_map/ppermute | solution.py:853
  10.1 1.3 %collective-permute-start.2 = (f32[72,8,128]{2,1,0:T(8,128)S(1)}, f32[72,8,128]{2,1,0:T(8,128)S(1)}, u32[]{:S(2)}, u32[]{:S(2)}) collective-permute-start(f32[72,8,128]{2,1,0:T(8,128)S(1)} %get-tuple-element.30.left), channel_id=1, source_target_pairs={{2,0},{4,2},{6,4},{8,6},{10,8},{12,10},{14,12},{16,14},{18,16},{20... | collective-permute-start | bytes 884744 | tf_op jit(solution)/shard_map/ppermute | solution.py:853
  11.4 2.7 %aside.1 = (bf16[2,896,256]{2,1,0:T(8,128)(2,1)S(1)}, bf16[2,1152,512]{2,1,0:T(8,128)(2,1)S(1)}, f32[192,8,128]{2,1,0:T(8,128)S(1)}, f32[8,128]{1,0:T(8,128)S(1)}) custom-call(s32[3]{0:T(128)S(1)} %pad_add_fusion.sc, f32[1536,128]{1,0:T(8,128)S(1)} %get-tuple-element.34.fh, f32[6,3,8,128]{3,2,1,0:T(8,128)S(1)} %get-tuple-element.28.w, ...), custom_call_target="tpu_custom_call" | custom-call | tf_op jit(solution)/shard_map/aside/pallas_call | solution.py:841
  14.0 2.4 %collective-permute-done.1.from_left = f32[72,8,128]{2,1,0:T(8,128)S(1)} collective-permute-done((f32[72,8,128]{2,1,0:T(8,128)S(1)}, f32[72,8,128]{2,1,0:T(8,128)S(1)}, u32[]{:S(2)}, u32[]{:S(2)}) %collective-permute-start.1) | collective-permute-done | bytes 294944 | tf_op jit(solution)/shard_map/ppermute | solution.py:853
  16.5 4.2 %collective-permute-done.2.from_right = f32[72,8,128]{2,1,0:T(8,128)S(1)} collective-permute-done((f32[72,8,128]{2,1,0:T(8,128)S(1)}, f32[72,8,128]{2,1,0:T(8,128)S(1)}, u32[]{:S(2)}, u32[]{:S(2)}) %collective-permute-start.2) | collective-permute-done | bytes 294944 | tf_op jit(solution)/shard_map/ppermute | solution.py:853
  20.6 2.7 %rim.1 = (f32[234,8,128]{2,1,0:T(8,128)S(1)}, f32[256,128]{1,0:T(8,128)S(1)}) custom-call(s32[3]{0:T(128)S(1)} %pad_add_fusion.sc, f32[72,8,128]{2,1,0:T(8,128)S(1)} %get-tuple-element.29.right, f32[72,8,128]{2,1,0:T(8,128)S(1)} %get-tuple-element.30.left, f32[72,8,128]{2,1,0:T(8,128)S(1)} %collective-permute-done.1.from_left, ...), custom_call_target="tpu_custom_call" | custom-call | tf_op jit(solution)/shard_map/rim/pallas_call | solution.py:841
  23.4 27.7 %all_to_all.11 = f32[128,2,128]{2,1,0:T(2,128)S(1)} all-to-all(f32[128,2,128]{2,1,0:T(2,128)S(1)} %bitcast.7), channel_id=1, replica_groups=mesh['tm'=128,'chan'=2] {'tm'}, dimensions={0} | all-to-all | bytes 262144 | tf_op jit(solution)/shard_map/all_to_all | solution.py:892
  51.1 1.9 %collective-permute-start.3 = (f32[256,128]{1,0:T(8,128)S(1)}, f32[256,128]{1,0:T(8,128)S(1)}, u32[]{:S(2)}, u32[]{:S(2)}) collective-permute-start(f32[256,128]{1,0:T(8,128)S(1)} %bitcast.5), channel_id=1, source_target_pairs={{0,1},{1,0},{2,3},{3,2},{4,5},{5,4},{6,7},{7,6},{8,9},{9,8},{10,11... | collective-permute-start | bytes 393224 | tf_op jit(solution)/shard_map/ppermute | solution.py:893
  53.0 1.0 %collective-permute-done.3.theirs = f32[256,128]{1,0:T(8,128)S(1)} collective-permute-done((f32[256,128]{1,0:T(8,128)S(1)}, f32[256,128]{1,0:T(8,128)S(1)}, u32[]{:S(2)}, u32[]{:S(2)}) %collective-permute-start.3) | collective-permute-done | bytes 131104 | tf_op jit(solution)/shard_map/ppermute | solution.py:893
  54.0 5.7 %back.1 = f32[1024,256]{1,0:T(8,128)} custom-call(s32[3]{0:T(128)S(1)} %pad_add_fusion.sc, f32[256,128]{1,0:T(8,128)S(1)} %bitcast.6, f32[256,128]{1,0:T(8,128)S(1)} %collective-permute-done.3.theirs, bf16[2,1152,512]{2,1,0:T(8,128)(2,1)S(1)} %get-tuple-element.38.coarse_table, bf16[2,896,256]{2,1,0:T(8,128)(2,1)S(1)} %get-tuple-element.39.table, ...), custom_call_target="tpu_custom_call" | custom-call | tf_op jit(solution)/shard_map/back/pallas_call | solution.py:841
Async XLA Ops:
  0.0 6.1 %collective-permute-start = (f32[1024,256]{1,0:T(8,128)}, f32[1024,256]{1,0:T(8,128)S(1)}, u32[]{:S(2)}, u32[]{:S(2)}) collective-permute-start(f32[1024,256]{1,0:T(8,128)} %x_all.1), channel_id=1, source_target_pairs={{0,1},{1,0},{2,3},{3,2},{4,5},{5,4},{6,7},{7,6},{8,9},{9,8},{10,11... | collective-permute-start | bytes 3145736 | tf_op jit(solution)/shard_map/ppermute | solution.py:863
  8.2 8.2 %collective-permute-start.1 = (f32[72,8,128]{2,1,0:T(8,128)S(1)}, f32[72,8,128]{2,1,0:T(8,128)S(1)}, u32[]{:S(2)}, u32[]{:S(2)}) collective-permute-start(f32[72,8,128]{2,1,0:T(8,128)S(1)} %get-tuple-element.29.right), channel_id=1, source_target_pairs={{0,2},{2,4},{4,6},{6,8},{8,10},{10,12},{12,14},{14,16},{16,18},{18... | collective-permute-start | bytes 884744 | tf_op jit(solution)/shard_map/ppermute | solution.py:853
  10.1 10.6 %collective-permute-start.2 = (f32[72,8,128]{2,1,0:T(8,128)S(1)}, f32[72,8,128]{2,1,0:T(8,128)S(1)}, u32[]{:S(2)}, u32[]{:S(2)}) collective-permute-start(f32[72,8,128]{2,1,0:T(8,128)S(1)} %get-tuple-element.30.left), channel_id=1, source_target_pairs={{2,0},{4,2},{6,4},{8,6},{10,8},{12,10},{14,12},{16,14},{18,16},{20... | collective-permute-start | bytes 884744 | tf_op jit(solution)/shard_map/ppermute | solution.py:853
  51.1 2.9 %collective-permute-start.3 = (f32[256,128]{1,0:T(8,128)S(1)}, f32[256,128]{1,0:T(8,128)S(1)}, u32[]{:S(2)}, u32[]{:S(2)}) collective-permute-start(f32[256,128]{1,0:T(8,128)S(1)} %bitcast.5), channel_id=1, source_target_pairs={{0,1},{1,0},{2,3},{3,2},{4,5},{5,4},{6,7},{7,6},{8,9},{9,8},{10,11... | collective-permute-start | bytes 393224 | tf_op jit(solution)/shard_map/ppermute | solution.py:893

commit v5 on v4

--- a/solution.py
+++ b/solution.py
@@ -850,7 +850,7 @@
 
 
 def _shift(v, by):
-    return lax.ppermute(v, "tm", [(i, i + by) for i in range(NT) if 0 <= i + by < NT])
+    return lax.ppermute(v, "tm", [(i, (i + by) % NT) for i in range(NT)])
 
 
 def shards(record, gauge_table, gauge_index):

time: 59.9 us -> 57.1 us (0.953)
  blocking collectives: 27.7 us -> 21.5 us
  starting transfers between devices: 8.27 us -> 13.8 us
  waiting for transfers between devices: 7.59 us -> 5.63 us
    all_to_all x1, blocking collectives: 27.7 us -> 21.5 us  [shards(): lax.all_to_all(payload, 'tm', split_axis=0, concat_axis=0, tiled=True)]
    ppermute x2, starting transfers between devices: 3.12 us -> 8.64 us  [_shift(): return lax.ppermute(v, 'tm', [(i, (i + by) % NT) for i in range(NT)])]
    ppermute x2, waiting for transfers between devices: 6.6 us -> 4.64 us  [_shift(): return lax.ppermute(v, 'tm', [(i, (i + by) % NT) for i in range(NT)])]
  transfers between devices with their start and end apart: 4 -> 4, of which waited for: 3 -> 2; matrix products, arithmetic and copies ran while one was open for 0% -> 0% of each run, Pallas kernels for 9% -> 10%
where the time goes in v5:
time: 57.1 us; the launch traced here: 57 us
  blocking collectives  21.5 us (38%)
  Pallas kernels  15.9 us (28%)
  starting transfers between devices  13.8 us (24%)
  waiting for transfers between devices  5.63 us (10%)
    all_to_all x1, blocking collectives, shards(): lax.all_to_all(payload, 'tm', split_axis=0, concat_axis=0, tiled=True)  21.5 us
    pallas_call x5, Pallas kernels, _call(): pl.pallas_call(kernel, out_shape=[pltpu.HBM(s.shape, s.dtype) if spec is...  15.9 us
    ppermute x2, starting transfers between devices, _shift(): return lax.ppermute(v, 'tm', [(i, (i + by) % NT) for i in range(NT)])  8.64 us
    ppermute x2, waiting for transfers between devices, _shift(): return lax.ppermute(v, 'tm', [(i, (i + by) % NT) for i in range(NT)])  4.64 us
    ppermute x1, starting transfers between devices, shards(): recv = lax.ppermute(record, 'chan', [(0, 1), (1, 0)])  3.24 us
    ppermute x1, starting transfers between devices, shards(): theirs = lax.ppermute(mine, 'chan', [(0, 1), (1, 0)])  1.91 us
  transfers between devices with their start and end apart: 4, of which 2 were waited for; matrix products, arithmetic and copies ran while one was open for 0% of the time, Pallas kernels for 10%

profile of v5, /device:TPU:1, one launch (start us, length us, event | category | flops | bytes accessed | tf_op | source)
XLA Modules:
  0.0 57.0 jit_solution(8642205104502476048)
XLA Ops:
  0.0 3.2 %collective-permute-start = (f32[1024,256]{1,0:T(8,128)}, f32[1024,256]{1,0:T(8,128)S(1)}, u32[]{:S(2)}, u32[]{:S(2)}) collective-permute-start(f32[1024,256]{1,0:T(8,128)} %x_all.1), channel_id=1, source_target_pairs={{0,1},{1,0},{2,3},{3,2},{4,5},{5,4},{6,7},{7,6},{8,9},{9,8},{10,11... | collective-permute-start | bytes 3145736 | tf_op jit(solution)/shard_map/ppermute | solution.py:863
  3.2 0.1 pad_add_fusion.sc
  3.3 2.8 %load.1 = (f32[1024,128]{1,0:T(8,128)S(1)}, f32[1024,128]{1,0:T(8,128)S(1)}, f32[1024,128]{1,0:T(8,128)S(1)}, bf16[2,384,256]{2,1,0:T(8,128)(2,1)S(1)}, bf16[2,8...) custom-call(s32[3]{0:T(128)S(1)} %pad_add_fusion.sc, f32[1024,256]{1,0:T(8,128)} %x_all.1, f32[6,8]{1,0:T(8,128)} %gauge_table_all.1, ...), custom_call_target="tpu_custom_call" | custom-call | tf_op jit(solution)/shard_map/load/pallas_call | solution.py:841
  6.1 0.0 collective-permute-done.recv
  6.1 2.1 %own.1 = (f32[72,8,128]{2,1,0:T(8,128)S(1)}, f32[72,8,128]{2,1,0:T(8,128)S(1)}, f32[96,8,128]{2,1,0:T(8,128)S(1)}, f32[48,8,128]{2,1,0:T(8,128)S(1)}, f32[1536,1...) custom-call(s32[3]{0:T(128)S(1)} %pad_add_fusion.sc, ...), custom_call_target="tpu_custom_call" | custom-call | tf_op jit(solution)/shard_map/own/pallas_call | solution.py:841
  8.2 0.1 collective-permute-start.1
  8.3 8.6 %collective-permute-start.2 = (f32[72,8,128]{2,1,0:T(8,128)S(1)}, f32[72,8,128]{2,1,0:T(8,128)S(1)}, u32[]{:S(2)}, u32[]{:S(2)}) collective-permute-start(f32[72,8,128]{2,1,0:T(8,128)S(1)} %get-tuple-element.30.left), channel_id=1, source_target_pairs={{0,254},{2,0},{4,2},{6,4},{8,6},{10,8},{12,10},{14,12},{16,14},{18... | collective-permute-start | bytes 884744 | tf_op jit(solution)/shard_map/ppermute | solution.py:853
  16.9 2.7 %aside.1 = (bf16[2,896,256]{2,1,0:T(8,128)(2,1)S(1)}, bf16[2,1152,512]{2,1,0:T(8,128)(2,1)S(1)}, f32[192,8,128]{2,1,0:T(8,128)S(1)}, f32[8,128]{1,0:T(8,128)S(1)}) custom-call(s32[3]{0:T(128)S(1)} %pad_add_fusion.sc, f32[1536,128]{1,0:T(8,128)S(1)} %get-tuple-element.34.fh, f32[6,3,8,128]{3,2,1,0:T(8,128)S(1)} %get-tuple-element.28.w, ...), custom_call_target="tpu_custom_call" | custom-call | tf_op jit(solution)/shard_map/aside/pallas_call | solution.py:841
  19.6 4.6 %collective-permute-done.1.from_left = f32[72,8,128]{2,1,0:T(8,128)S(1)} collective-permute-done((f32[72,8,128]{2,1,0:T(8,128)S(1)}, f32[72,8,128]{2,1,0:T(8,128)S(1)}, u32[]{:S(2)}, u32[]{:S(2)}) %collective-permute-start.1) | collective-permute-done | bytes 294944 | tf_op jit(solution)/shard_map/ppermute | solution.py:853
  24.2 0.0 collective-permute-done.2.from_right
  24.2 2.7 %rim.1 = (f32[234,8,128]{2,1,0:T(8,128)S(1)}, f32[256,128]{1,0:T(8,128)S(1)}) custom-call(s32[3]{0:T(128)S(1)} %pad_add_fusion.sc, f32[72,8,128]{2,1,0:T(8,128)S(1)} %get-tuple-element.29.right, f32[72,8,128]{2,1,0:T(8,128)S(1)} %get-tuple-element.30.left, f32[72,8,128]{2,1,0:T(8,128)S(1)} %collective-permute-done.1.from_left, ...), custom_call_target="tpu_custom_call" | custom-call | tf_op jit(solution)/shard_map/rim/pallas_call | solution.py:841
  26.9 21.5 %all_to_all.11 = f32[128,2,128]{2,1,0:T(2,128)S(1)} all-to-all(f32[128,2,128]{2,1,0:T(2,128)S(1)} %bitcast.7), channel_id=1, replica_groups=mesh['tm'=128,'chan'=2] {'tm'}, dimensions={0} | all-to-all | bytes 262144 | tf_op jit(solution)/shard_map/all_to_all | solution.py:892
  48.4 1.9 %collective-permute-start.3 = (f32[256,128]{1,0:T(8,128)S(1)}, f32[256,128]{1,0:T(8,128)S(1)}, u32[]{:S(2)}, u32[]{:S(2)}) collective-permute-start(f32[256,128]{1,0:T(8,128)S(1)} %bitcast.5), channel_id=1, source_target_pairs={{0,1},{1,0},{2,3},{3,2},{4,5},{5,4},{6,7},{7,6},{8,9},{9,8},{10,11... | collective-permute-start | bytes 393224 | tf_op jit(solution)/shard_map/ppermute | solution.py:893
  50.3 1.0 %collective-permute-done.3.theirs = f32[256,128]{1,0:T(8,128)S(1)} collective-permute-done((f32[256,128]{1,0:T(8,128)S(1)}, f32[256,128]{1,0:T(8,128)S(1)}, u32[]{:S(2)}, u32[]{:S(2)}) %collective-permute-start.3) | collective-permute-done | bytes 131104 | tf_op jit(solution)/shard_map/ppermute | solution.py:893
  51.3 5.7 %back.1 = f32[1024,256]{1,0:T(8,128)} custom-call(s32[3]{0:T(128)S(1)} %pad_add_fusion.sc, f32[256,128]{1,0:T(8,128)S(1)} %bitcast.6, f32[256,128]{1,0:T(8,128)S(1)} %collective-permute-done.3.theirs, bf16[2,1152,512]{2,1,0:T(8,128)(2,1)S(1)} %get-tuple-element.38.coarse_table, bf16[2,896,256]{2,1,0:T(8,128)(2,1)S(1)} %get-tuple-element.39.table, ...), custom_call_target="tpu_custom_call" | custom-call | tf_op jit(solution)/shard_map/back/pallas_call | solution.py:841
Async XLA Ops:
  0.0 6.1 %collective-permute-start = (f32[1024,256]{1,0:T(8,128)}, f32[1024,256]{1,0:T(8,128)S(1)}, u32[]{:S(2)}, u32[]{:S(2)}) collective-permute-start(f32[1024,256]{1,0:T(8,128)} %x_all.1), channel_id=1, source_target_pairs={{0,1},{1,0},{2,3},{3,2},{4,5},{5,4},{6,7},{7,6},{8,9},{9,8},{10,11... | collective-permute-start | bytes 3145736 | tf_op jit(solution)/shard_map/ppermute | solution.py:863
  8.2 15.9 %collective-permute-start.1 = (f32[72,8,128]{2,1,0:T(8,128)S(1)}, f32[72,8,128]{2,1,0:T(8,128)S(1)}, u32[]{:S(2)}, u32[]{:S(2)}) collective-permute-start(f32[72,8,128]{2,1,0:T(8,128)S(1)} %get-tuple-element.29.right), channel_id=1, source_target_pairs={{0,2},{2,4},{4,6},{6,8},{8,10},{10,12},{12,14},{14,16},{16,18},{18... | collective-permute-start | bytes 884744 | tf_op jit(solution)/shard_map/ppermute | solution.py:853
  8.3 15.9 %collective-permute-start.2 = (f32[72,8,128]{2,1,0:T(8,128)S(1)}, f32[72,8,128]{2,1,0:T(8,128)S(1)}, u32[]{:S(2)}, u32[]{:S(2)}) collective-permute-start(f32[72,8,128]{2,1,0:T(8,128)S(1)} %get-tuple-element.30.left), channel_id=1, source_target_pairs={{0,254},{2,0},{4,2},{6,4},{8,6},{10,8},{12,10},{14,12},{16,14},{18... | collective-permute-start | bytes 884744 | tf_op jit(solution)/shard_map/ppermute | solution.py:853
  48.4 2.9 %collective-permute-start.3 = (f32[256,128]{1,0:T(8,128)S(1)}, f32[256,128]{1,0:T(8,128)S(1)}, u32[]{:S(2)}, u32[]{:S(2)}) collective-permute-start(f32[256,128]{1,0:T(8,128)S(1)} %bitcast.5), channel_id=1, source_target_pairs={{0,1},{1,0},{2,3},{3,2},{4,5},{5,4},{6,7},{7,6},{8,9},{9,8},{10,11... | collective-permute-start | bytes 393224 | tf_op jit(solution)/shard_map/ppermute | solution.py:893

commit v6 on v5

--- a/solution.py
+++ b/solution.py
@@ -98,14 +98,14 @@
 
 OWN_LOW0 = _run(2, 126, 2)
 OWN_HIGH0 = _run(2, 126, 130)
-RIM_LOW0 = {**_run(-10, 2, 0), **_run(126, 137, 12)}
-RIM_HIGH0 = {**_run(-2, 2, 23), **_run(126, 130, 27)}
-RIM_IN0 = {**_run(-32, 0, 0), **_run(0, 32, 128), **_run(224, 256, 256), **_run(256, 288, 384)}
+RIM_LOW0 = {**_run(-2, 2, 0), **_run(126, 130, 4)}
+RIM_HIGH0 = {**_run(-2, 2, 8), **_run(126, 130, 12)}
+RIM_IN0 = {**_run(-8, 0, 0), **_run(0, 8, 128), **_run(248, 256, 256), **_run(256, 264, 384)}
 OWN_LOW1 = _run(3, 61, 3)
 OWN_HIGH1 = _run(2, 61, 66)
 RIM_LOW1 = {**_run(-3, 3, 64), **_run(61, 67, 70)}
 RIM_HIGH1 = {**_run(-3, 2, 80), **_run(61, 67, 85)}
-IN1 = {**OWN_LOW0, **{k: 128 + v for k, v in RIM_LOW0.items()}}
+IN1 = {**OWN_LOW0, **{k: 128 + v for k, v in RIM_LOW0.items()}, **_run(-10, -2, 160), **_run(130, 138, 168)}
 IN2 = {
     **OWN_LOW1, **_run(67, 125, 67), **_run(-61, -3, 131), **{k: 128 + v for k, v in RIM_LOW1.items()}
 }
@@ -156,7 +156,7 @@
         sixteen = np.concatenate([lows, highs[:, 1:], lows[:, 1:], highs[:, 1:], np.zeros((128, 3))], axis=1)
         t5[:, 128:] = np.tile(sixteen, (1, 8))
         one = fw(RIM_IN0, RIM_LOW0, RIM_HIGH0, 512, 128, a[0], b[0], 1.0)
-        rim0 = sum(np.roll(one, (32 * g, 32 * g), (0, 1)) for g in range(4))
+        rim0 = [sum(np.roll(one, (8 * (4 * g + h), 32 * g), (0, 1)) for g in range(4)) for h in range(4)]
         rim.append(
             _bundle(
                 (
@@ -165,10 +165,10 @@
                     (0, 256, fw(LOW2, LOW3, HIGH3, 128, 128, a[3], b[3], KS)),
                     (128, 256, fw(LOW3, LOW4, HIGH4, 128, 128, a[4], b[4], KS)),
                     (256, 0, t5),
-                    (384, 0, rim0),
+                    (384, 0, np.concatenate(rim0, axis=1)),
                 ),
                 896,
-                384,
+                512,
             )
         )
         low0 = {**OWN_LOW0, **{k: 256 + v for k, v in RIM_LOW0.items() if -2 <= k < 130}}
@@ -439,8 +439,8 @@
 
 
 def _load_kernel(
-    sc, x_all, gauge_table_all, gauge_index_all, own_all, rim_all,
-    low, high, ends, own_table, rim_table, w,
+    sc, x_all, gauge_table_all, gauge_index_all, own_all,
+    low, high, ends, own_table, w,
     x, gauge_table, gauge_index, sems,
 ):
     core = sc[0]
@@ -452,7 +452,6 @@
                 (gauge_table_all, gauge_table),
                 (own_all, own_table),
                 *((x_all.at[pl.ds(256 * i, 256)], x.at[pl.ds(256 * i, 256)]) for i in range(4)),
-                (rim_all.at[sc[1]], rim_table),
             )
         )
     ]
@@ -475,7 +474,6 @@
     for i in range(4):
         copies[3 + i].wait()
         _first(x, own_table, low, high, ends, 0, range(256 * i, 256 * i + 256, 128))
-    copies[7].wait()
 
 
 def _first(x, table, low, high, ends, at, blocks):
@@ -503,14 +501,13 @@
     theirs = recv.at[pl.ds(at_own, HALO)]
     _first(theirs, table, fl, fh, fe, at_recv, range(0, HALO, 128))
     lane = _lane()
-    group = lane // 32
-    for i in range(48):
+    group = lane // 8
+    for i in range(12):
         to_right, to_left = None, None
-        for g in range(4):
-            j = 48 * g + i
-            v = fe[pl.ds(j, 8, stride=SEG), :]
-            a = pltpu.roll(v, 32 * g, 1) if g else v
-            b = pltpu.roll(v, (32 * g + 32) % 128, 1) if g != 3 else v
+        for g in range(16):
+            v = fe[pl.ds(12 * g + i, 8, stride=SEG), :]
+            a = pltpu.roll(v, 8 * g, 1) if g else v
+            b = pltpu.roll(v, (8 * g + 8) % 128, 1) if g != 15 else v
             to_left = a if to_left is None else jnp.where(group == g, a, to_left)
             to_right = b if to_right is None else jnp.where(group == g, b, to_right)
         right[i] = to_right
@@ -527,6 +524,16 @@
 
     _chan_forward(lambda j: fl[pl.ds(j, 8, stride=SEG), :], 96, _blocks(w, 0), 128, put_low, put_high)
     sums[0] = sq.total(rows, {("high", 0): None})
+    for i in range(6):
+        to_right, to_left = None, None
+        for g in range(16):
+            v = low0[6 * g + i]
+            a = pltpu.roll(v, (8 * g - 118) % 128, 1)
+            b = pltpu.roll(v, (8 * g + 6) % 128, 1)
+            to_right = a if to_right is None else jnp.where(group == g, a, to_right)
+            to_left = b if to_left is None else jnp.where(group == (g + 1) % 16, b, to_left)
+        right[12 + i] = to_right
+        left[12 + i] = to_left
     sq1 = _Squares()
 
     def put_low1(k, q, v):
@@ -535,8 +542,8 @@
         sq1.add(("low", 0, q), v)
         if k >= 26:
             packed = jnp.where(lane < 64, a1l[k - 24], pltpu.roll(v, 64, 1))
-            right[24 + k] = packed
-            left[24 + k] = packed
+            right[k - 6] = packed
+            left[k - 6] = packed
 
     def put_high1(k, q, v):
         details[144 + k] = v
@@ -546,8 +553,8 @@
     _chan_forward(get, 48, _blocks(w, 1), 128, put_low1, put_high1)
     for k in (24, 25):
         packed = jnp.where(lane < 64, a1l[k - 24], pltpu.roll(a1l[k], 64, 1))
-        right[24 + k] = packed
-        left[24 + k] = packed
+        right[k - 6] = packed
+        left[k - 6] = packed
     sums[1] = sq1.total(rows, {("low", 0): _ones(_mask(lane, OWN_HIGH1, 0, 64)), ("high", 0): None})
 
 
@@ -559,14 +566,22 @@
     return out
 
 
-def _aside_kernel(sc, fh, w, back_all, coarse_all, back_table, coarse_table, details, sums, sems):
+def _aside_kernel(
+    sc, fh, w, rim_all, back_all, coarse_all, rim_table, back_table, coarse_table, details, sums, sems
+):
     copies = []
-    for src, dst, parts in ((back_all.at[sc[1]], back_table, 4), (coarse_all, coarse_table, 4)):
-        n = dst.shape[1] // parts
-        for i in range(2):
-            for k in range(parts):
-                rows = pl.ds(n * k, n)
-                copies.append(pltpu.make_async_copy(src.at[i, rows], dst.at[i, rows], sems.at[len(copies)]))
+    mine = pl.multiple_of(512 + 16 * (sc[2] // 4), 16)
+    for i in range(2):
+        for src, dst, start, n in (
+            (rim_all.at[sc[1], i], rim_table.at[i], 0, 448),
+            (rim_all.at[sc[1], i], rim_table.at[i], 448, 448),
+            (back_all.at[sc[1], i], back_table.at[i], 0, 896),
+            (coarse_all.at[i], coarse_table.at[i], 0, 512),
+        ):
+            rows = pl.ds(start, n)
+            copies.append(pltpu.make_async_copy(src.at[rows], dst.at[rows], sems.at[len(copies)]))
+        src, dst = coarse_all.at[i, pl.ds(mine, 128)], coarse_table.at[i, pl.ds(512, 128)]
+        copies.append(pltpu.make_async_copy(src, dst, sems.at[len(copies)]))
     for c in copies:
         c.start()
     rows = _own_rows(sc[0])
@@ -613,7 +628,8 @@
 
         wrap = _QuarterWrap() if quarters else None
         weights = _quarters(weights) if quarters else weights
-        _chan_forward(_Forward(load, t, y, step), n, weights, lanes, put_low, put_high, wrap)
+        get = y.__getitem__ if quarters else _Forward(load, t, y, step)
+        _chan_forward(get, n, weights, lanes, put_low, put_high, wrap)
         is_high = _mask(place, own_high, 0, pairs)
         is_low = _mask(place, own_low, 0, pairs)
         total = sq.total(_quarters(rows) if quarters else rows, {("low", 0): _ones(is_high), ("high", 0): _ones(is_high | is_low)})
@@ -622,22 +638,27 @@
     def pick(r, k, c, n):
         return _table(table, (r, k), (c, n))
 
-    def load0(j, n):
-        at = pl.ds(j, n)
-        return jnp.concatenate([from_left[at], left[at], right[at], from_right[at]], axis=2)
-
-    level(0, load0, 24, pick(384, 512, 0, 128), y0, 24, 128, rlow0, rhigh0, RIM_LOW0, RIM_HIGH0, 128)
+    raw = pl.ds(0, 12)
+    raw = jnp.concatenate([from_left[raw], left[raw], right[raw], from_right[raw]], axis=2)
+    raw = _dot3(raw.reshape(96, 512), pick(384, 512, 0, 512))
+    for h in range(4):
+        y0[pl.ds(12 * h, 12)] = _tile(raw, h).reshape(12, 8, 128)
+    level(0, None, 24, None, y0, 24, 128, rlow0, rhigh0, RIM_LOW0, RIM_HIGH0, 128)
     totals[0] = totals[0] + more_sums[...]
-    for g in range(4):
-        for i in range(24):
-            rim[24 * g + i] = pltpu.roll(rlow0[i], 128 - 32 * g, 1) if g else rlow0[i]
+    for j in range(96):
+        g, i = j // 24, j % 24
+        mine = pltpu.roll(rlow0[i], 128 - 32 * g, 1) if g else rlow0[i]
+        g, i = j // 6, 12 + j % 6
+        theirs = jnp.where(lane // 8 == g, from_left[i], from_right[i])
+        theirs = pltpu.roll(theirs, (32 - 8 * g) % 128, 1) if g != 4 else theirs
+        rim[j] = jnp.where(lane < 32, mine, theirs)
 
     def load1(j, n):
         return jnp.concatenate([low0[pl.ds(j, n)], rim[pl.ds(j, n)]], axis=2)
 
     level(1, load1, 48, pick(0, 256, 0, 128), y1, 24, 128, r1l, r1h, RIM_LOW1, RIM_HIGH1, 64)
     for j in range(48):
-        h, i = j // 24, 48 + j % 24
+        h, i = j // 24, 18 + j % 24
         b, a = from_left[i], from_right[i]
         if h == 0:
             a = pltpu.roll(a, 64, 1)
@@ -733,7 +754,7 @@
     def nt(a, b):
         return lax.dot_general(a, b, (((1,), (1,)), ((), ())), preferred_element_type=F32)
 
-    rows = pl.ds(pl.multiple_of(512 + 16 * (place // 4), 16), 128)
+    rows = pl.ds(512, 128)
     current = nt(hi, coarse_table[0, rows, :]) + nt(lo, coarse_table[0, rows, :]) + nt(hi, coarse_table[1, rows, :])
     cur[...] = pltpu.roll(current, (128 - 4 * (place % 4)) % 128, 1)
 
@@ -780,7 +801,7 @@
     tl0 = jnp.broadcast_to(limits[0] * (1.0 / KS), (8, 128))
     th0 = jnp.broadcast_to(limits[0] * KS, (8, 256))
     group = lane // 32
-    rim_low = lane % 32 < 23
+    rim_low = lane % 32 < 8
 
     def get_low_rim(k):
         now = c0[k, :, 128:256]
@@ -861,26 +882,27 @@
     sc = jnp.stack([core, variant, place]).astype(jnp.int32)
     dma = pltpu.SemaphoreType.DMA
     recv = lax.ppermute(record, "chan", [(0, 1), (1, 0)])
-    low, high, ends, own_table, rim_table, w = _call(
-        _load_kernel, "load", 12, (sc, record, gauge_table, gauge_index, tables["own"], tables["rim"]),
-        [SM] + [HBM] * 5,
-        [(OWN, 128), (OWN, 128), (OWN, 128), jax.ShapeDtypeStruct((2, 384, 256), BF16),
-         jax.ShapeDtypeStruct((2, 896, 384), BF16), (LEVELS, 3, 8, 128)],
-        [VM] * 6,
-        [(OWN, 256), (LEVELS, GTAB), pltpu.VMEM((LEVELS, NBLK), jnp.int32), dma((8,))],
+    low, high, ends, own_table, w = _call(
+        _load_kernel, "load", 12, (sc, record, gauge_table, gauge_index, tables["own"]),
+        [SM] + [HBM] * 4,
+        [(OWN, 128), (OWN, 128), (OWN, 128), jax.ShapeDtypeStruct((2, 384, 256), BF16), (LEVELS, 3, 8, 128)],
+        [VM] * 5,
+        [(OWN, 256), (LEVELS, GTAB), pltpu.VMEM((LEVELS, NBLK), jnp.int32), dma((7,))],
     )
     right, left, low0, a1l, fh, own_details, sums = _call(
         _own_kernel, "own", 12, (sc, recv, low, high, ends, own_table, w), [SM] + [VM] * 6,
-        [(72, 8, 128), (72, 8, 128), (96, 8, 128), (48, 8, 128), (8 * SEG, 128), (192, 8, 128), (2, 8, 128)],
+        [(42, 8, 128), (42, 8, 128), (96, 8, 128), (48, 8, 128), (8 * SEG, 128), (192, 8, 128), (2, 8, 128)],
         [VM] * 7,
         [(8 * SEG, 128), (8 * SEG, 128), (96, 8, 128)],
     )
     from_left, from_right = _shift(right, 1), _shift(left, -1)
-    back_table, coarse_table, more_details, more_sums = _call(
-        _aside_kernel, "aside", 6, (sc, fh, w, tables["back"], tables["coarse"]), [SM, VM, VM, HBM, HBM],
-        [jax.ShapeDtypeStruct((2, 896, 256), BF16), jax.ShapeDtypeStruct((2, 1152, 512), BF16), (192, 8, 128), (8, 128)],
-        [VM] * 4,
-        [dma((16,))],
+    rim_table, back_table, coarse_table, more_details, more_sums = _call(
+        _aside_kernel, "aside", 6, (sc, fh, w, tables["rim"], tables["back"], tables["coarse"]),
+        [SM, VM, VM, HBM, HBM, HBM],
+        [jax.ShapeDtypeStruct((2, 896, 512), BF16), jax.ShapeDtypeStruct((2, 896, 256), BF16),
+         jax.ShapeDtypeStruct((2, 640, 512), BF16), (192, 8, 128), (8, 128)],
+        [VM] * 5,
+        [dma((10,))],
     )
     rim_details, payload = _call(
         _rim_kernel, "rim", 16,

time: 57.1 us -> 54.4 us (0.953)
  waiting for transfers between devices: 5.63 us -> 2.92 us
    ppermute x2, waiting for transfers between devices: 4.64 us -> 1.94 us  [_shift(): return lax.ppermute(v, 'tm', [(i, (i + by) % NT) for i in range(NT)])]
where the time goes in v6:
time: 54.4 us; the launch traced here: 54.3 us
  blocking collectives  21.5 us (40%)
  Pallas kernels  15.9 us (29%)
  starting transfers between devices  13.8 us (25%)
  waiting for transfers between devices  2.92 us (5%)
    all_to_all x1, blocking collectives, shards(): lax.all_to_all(payload, 'tm', split_axis=0, concat_axis=0, tiled=True)  21.5 us
    pallas_call x5, Pallas kernels, _call(): pl.pallas_call(kernel, out_shape=[pltpu.HBM(s.shape, s.dtype) if spec is...  15.9 us
    ppermute x2, starting transfers between devices, _shift(): return lax.ppermute(v, 'tm', [(i, (i + by) % NT) for i in range(NT)])  8.64 us
    ppermute x1, starting transfers between devices, shards(): recv = lax.ppermute(record, 'chan', [(0, 1), (1, 0)])  3.24 us
    ppermute x2, waiting for transfers between devices, _shift(): return lax.ppermute(v, 'tm', [(i, (i + by) % NT) for i in range(NT)])  1.94 us
    ppermute x1, starting transfers between devices, shards(): theirs = lax.ppermute(mine, 'chan', [(0, 1), (1, 0)])  1.91 us
  transfers between devices with their start and end apart: 4, of which 2 were waited for; matrix products, arithmetic and copies ran while one was open for 0% of the time, Pallas kernels for 10%

profile of v6, /device:TPU:1, one launch (start us, length us, event | category | flops | bytes accessed | tf_op | source)
XLA Modules:
  0.0 54.3 jit_solution(4867368105329348550)
XLA Ops:
  0.0 3.2 %collective-permute-start = (f32[1024,256]{1,0:T(8,128)}, f32[1024,256]{1,0:T(8,128)S(1)}, u32[]{:S(2)}, u32[]{:S(2)}) collective-permute-start(f32[1024,256]{1,0:T(8,128)} %x_all.1), channel_id=1, source_target_pairs={{0,1},{1,0},{2,3},{3,2},{4,5},{5,4},{6,7},{7,6},{8,9},{9,8},{10,11... | collective-permute-start | bytes 3145736 | tf_op jit(solution)/shard_map/ppermute | solution.py:884
  3.2 0.1 pad_add_fusion.sc
  3.3 2.8 %load.1 = (f32[1024,128]{1,0:T(8,128)S(1)}, f32[1024,128]{1,0:T(8,128)S(1)}, f32[1024,128]{1,0:T(8,128)S(1)}, bf16[2,384,256]{2,1,0:T(8,128)(2,1)S(1)}, f32[6,3,8,128]{3,2,1,0:T(8,128)S(1)}) custom-call(s32[3]{0:T(128)S(1)} %pad_add_fusion.sc, f32[1024,256]{1,0:T(8,128)} %x_all.1, f32[6,8]{1,0:T(8,128)} %gauge_table_all.1, s32[6,32]{1,0:T(8,128)} %gauge_index_all.1, ...), custom_call_target="tpu_custom_call" | custom-call | tf_op jit(solution)/shard_map/load/pallas_call | solution.py:862
  6.1 0.0 collective-permute-done.recv
  6.1 2.1 %own.1 = (f32[42,8,128]{2,1,0:T(8,128)S(1)}, f32[42,8,128]{2,1,0:T(8,128)S(1)}, f32[96,8,128]{2,1,0:T(8,128)S(1)}, f32[48,8,128]{2,1,0:T(8,128)S(1)}, f32[1536,1...) custom-call(s32[3]{0:T(128)S(1)} %pad_add_fusion.sc, ...), custom_call_target="tpu_custom_call" | custom-call | tf_op jit(solution)/shard_map/own/pallas_call | solution.py:862
  8.3 0.1 collective-permute-start.1
  8.4 8.6 %collective-permute-start.2 = (f32[42,8,128]{2,1,0:T(8,128)S(1)}, f32[42,8,128]{2,1,0:T(8,128)S(1)}, u32[]{:S(2)}, u32[]{:S(2)}) collective-permute-start(f32[42,8,128]{2,1,0:T(8,128)S(1)} %get-tuple-element.30.left), channel_id=1, source_target_pairs={{0,254},{2,0},{4,2},{6,4},{8,6},{10,8},{12,10},{14,12},{16,14},{18... | collective-permute-start | bytes 516104 | tf_op jit(solution)/shard_map/ppermute | solution.py:874
  16.9 2.7 %aside.1 = (bf16[2,896,512]{2,1,0:T(8,128)(2,1)S(1)}, bf16[2,896,256]{2,1,0:T(8,128)(2,1)S(1)}, bf16[2,640,512]{2,1,0:T(8,128)(2,1)S(1)}, f32[192,8,128]{2,1,0:T(8,128)S(1)}, f32[8,128]{1,0:T(8,128)S(1)}) custom-call(s32[3]{0:T(128)S(1)} %pad_add_fusion.sc, f32[1536,128]{1,0:T(8,128)S(1)} %get-tuple-element.34.fh, f32[6,3,8,128]{3,2,1,0:T(8,128)S(1)} %get-tuple-element.28.w, ...), custom_call_target="tpu_custom_call" | custom-call | tf_op jit(solution)/shard_map/aside/pallas_call | solution.py:862
  19.6 1.9 %collective-permute-done.1.from_left = f32[42,8,128]{2,1,0:T(8,128)S(1)} collective-permute-done((f32[42,8,128]{2,1,0:T(8,128)S(1)}, f32[42,8,128]{2,1,0:T(8,128)S(1)}, u32[]{:S(2)}, u32[]{:S(2)}) %collective-permute-start.1) | collective-permute-done | bytes 172064 | tf_op jit(solution)/shard_map/ppermute | solution.py:874
  21.6 0.0 collective-permute-done.2.from_right
  21.6 2.6 %rim.1 = (f32[234,8,128]{2,1,0:T(8,128)S(1)}, f32[256,128]{1,0:T(8,128)S(1)}) custom-call(s32[3]{0:T(128)S(1)} %pad_add_fusion.sc, f32[42,8,128]{2,1,0:T(8,128)S(1)} %get-tuple-element.29.right, f32[42,8,128]{2,1,0:T(8,128)S(1)} %get-tuple-element.30.left, f32[42,8,128]{2,1,0:T(8,128)S(1)} %collective-permute-done.1.from_left, ...), custom_call_target="tpu_custom_call" | custom-call | tf_op jit(solution)/shard_map/rim/pallas_call | solution.py:862
  24.2 21.5 %all_to_all.11 = f32[128,2,128]{2,1,0:T(2,128)S(1)} all-to-all(f32[128,2,128]{2,1,0:T(2,128)S(1)} %bitcast.7), channel_id=1, replica_groups=mesh['tm'=128,'chan'=2] {'tm'}, dimensions={0} | all-to-all | bytes 262144 | tf_op jit(solution)/shard_map/all_to_all | solution.py:914
  45.7 1.9 %collective-permute-start.3 = (f32[256,128]{1,0:T(8,128)S(1)}, f32[256,128]{1,0:T(8,128)S(1)}, u32[]{:S(2)}, u32[]{:S(2)}) collective-permute-start(f32[256,128]{1,0:T(8,128)S(1)} %bitcast.5), channel_id=1, source_target_pairs={{0,1},{1,0},{2,3},{3,2},{4,5},{5,4},{6,7},{7,6},{8,9},{9,8},{10,11... | collective-permute-start | bytes 393224 | tf_op jit(solution)/shard_map/ppermute | solution.py:915
  47.6 1.0 %collective-permute-done.3.theirs = f32[256,128]{1,0:T(8,128)S(1)} collective-permute-done((f32[256,128]{1,0:T(8,128)S(1)}, f32[256,128]{1,0:T(8,128)S(1)}, u32[]{:S(2)}, u32[]{:S(2)}) %collective-permute-start.3) | collective-permute-done | bytes 131104 | tf_op jit(solution)/shard_map/ppermute | solution.py:915
  48.6 5.6 %back.1 = f32[1024,256]{1,0:T(8,128)} custom-call(s32[3]{0:T(128)S(1)} %pad_add_fusion.sc, f32[256,128]{1,0:T(8,128)S(1)} %bitcast.6, f32[256,128]{1,0:T(8,128)S(1)} %collective-permute-done.3.theirs, bf16[2,640,512]{2,1,0:T(8,128)(2,1)S(1)} %get-tuple-element.38.coarse_table, bf16[2,896,256]{2,1,0:T(8,128)(2,1)S(1)} %get-tuple-element.39.table, ...), custom_call_target="tpu_custom_call" | custom-call | tf_op jit(solution)/shard_map/back/pallas_call | solution.py:862
Async XLA Ops:
  0.0 6.1 %collective-permute-start = (f32[1024,256]{1,0:T(8,128)}, f32[1024,256]{1,0:T(8,128)S(1)}, u32[]{:S(2)}, u32[]{:S(2)}) collective-permute-start(f32[1024,256]{1,0:T(8,128)} %x_all.1), channel_id=1, source_target_pairs={{0,1},{1,0},{2,3},{3,2},{4,5},{5,4},{6,7},{7,6},{8,9},{9,8},{10,11... | collective-permute-start | bytes 3145736 | tf_op jit(solution)/shard_map/ppermute | solution.py:884
  8.3 13.3 %collective-permute-start.1 = (f32[42,8,128]{2,1,0:T(8,128)S(1)}, f32[42,8,128]{2,1,0:T(8,128)S(1)}, u32[]{:S(2)}, u32[]{:S(2)}) collective-permute-start(f32[42,8,128]{2,1,0:T(8,128)S(1)} %get-tuple-element.29.right), channel_id=1, source_target_pairs={{0,2},{2,4},{4,6},{6,8},{8,10},{10,12},{12,14},{14,16},{16,18},{18... | collective-permute-start | bytes 516104 | tf_op jit(solution)/shard_map/ppermute | solution.py:874
  8.4 13.2 %collective-permute-start.2 = (f32[42,8,128]{2,1,0:T(8,128)S(1)}, f32[42,8,128]{2,1,0:T(8,128)S(1)}, u32[]{:S(2)}, u32[]{:S(2)}) collective-permute-start(f32[42,8,128]{2,1,0:T(8,128)S(1)} %get-tuple-element.30.left), channel_id=1, source_target_pairs={{0,254},{2,0},{4,2},{6,4},{8,6},{10,8},{12,10},{14,12},{16,14},{18... | collective-permute-start | bytes 516104 | tf_op jit(solution)/shard_map/ppermute | solution.py:874
  45.7 2.9 %collective-permute-start.3 = (f32[256,128]{1,0:T(8,128)S(1)}, f32[256,128]{1,0:T(8,128)S(1)}, u32[]{:S(2)}, u32[]{:S(2)}) collective-permute-start(f32[256,128]{1,0:T(8,128)S(1)} %bitcast.5), channel_id=1, source_target_pairs={{0,1},{1,0},{2,3},{3,2},{4,5},{5,4},{6,7},{7,6},{8,9},{9,8},{10,11... | collective-permute-start | bytes 393224 | tf_op jit(solution)/shard_map/ppermute | solution.py:915

commit v7 on v6

--- a/solution.py
+++ b/solution.py
@@ -696,7 +696,7 @@
 def _back_kernel(
     sc, mine, theirs, coarse_table, table, own_details, more_details, rim_details, w,
     out,
-    gt, nears, cur, x5l, x5h, y5, y4, y3, y2, y1, c4, c3, c2, c1, c0, f0, f1, f2, yr, stage, sems,
+    both, gt, nears, cur, x5l, x5h, y5, y4, y3, y2, y1, c4, c3, c2, c1, c0, f0, f1, f2, yr, stage, sems,
 ):
     core, place = sc[0], sc[2]
     rlow0, rhigh0, r1l, r1h, a2l, a2h, a3l, a3h, a4l, a4h, a5l, a5h = _bands(rim_details)
@@ -705,12 +705,14 @@
     lane = _lane()
     lane1 = _lane(1)
     sub = _sublane(128)
+    both[0, 0:256, :] = mine[...]
+    both[1, 0:256, :] = theirs[...]
     for h in range(2):
-        halves = [g[pl.ds(h, NT, stride=2), :] for g in (mine, theirs)]
+        halves = [both[g, pl.ds(h, NT, stride=2), :] for g in range(2)]
         if h == 0:
             total = jnp.sum(halves[0] + halves[1], axis=0, keepdims=True)
         for c in range(2):
-            gt[c, h] = jnp.transpose(jnp.where(core == c, halves[0], halves[1]))
+            gt[c, h, 0:128, :] = jnp.transpose(jnp.where(core == c, halves[0], halves[1]))
     limits = []
     for l in range(LEVELS):
         entries = 3 * (C >> (l + 1)) * (S >> (l + 1))
@@ -756,7 +758,7 @@
 
     rows = pl.ds(512, 128)
     current = nt(hi, coarse_table[0, rows, :]) + nt(lo, coarse_table[0, rows, :]) + nt(hi, coarse_table[1, rows, :])
-    cur[...] = pltpu.roll(current, (128 - 4 * (place % 4)) % 128, 1)
+    cur[0:32, :] = pltpu.roll(current, (128 - 4 * (place % 4)) % 128, 1)
 
     def level(l, get_current, low, high, n, y, t, nxt, step, needed):
         tl = jnp.broadcast_to(limits[l] * (1.0 / KS), (8, 128))
@@ -850,8 +852,8 @@
 
 VM = pl.BlockSpec(memory_space=pltpu.VMEM)
 SM = pl.BlockSpec(memory_space=pltpu.SMEM)
-ANY = pl.BlockSpec(memory_space=pl.ANY)
 HBM = pl.BlockSpec(memory_space=pltpu.HBM)
+ROWS = (9 * SEG, 128)
 
 
 def _call(kernel, name, limit, args, specs, outs, out_specs, scratch):
@@ -891,9 +893,9 @@
     )
     right, left, low0, a1l, fh, own_details, sums = _call(
         _own_kernel, "own", 12, (sc, recv, low, high, ends, own_table, w), [SM] + [VM] * 6,
-        [(42, 8, 128), (42, 8, 128), (96, 8, 128), (48, 8, 128), (8 * SEG, 128), (192, 8, 128), (2, 8, 128)],
+        [(42, 8, 128), (42, 8, 128), (96, 8, 128), (48, 8, 128), ROWS, (192, 8, 128), (2, 8, 128)],
         [VM] * 7,
-        [(8 * SEG, 128), (8 * SEG, 128), (96, 8, 128)],
+        [ROWS, ROWS, (96, 8, 128)],
     )
     from_left, from_right = _shift(right, 1), _shift(left, -1)
     rim_table, back_table, coarse_table, more_details, more_sums = _call(
@@ -909,7 +911,7 @@
         (sc, right, left, from_left, from_right, low0, a1l, sums, more_sums, rim_table, w), [SM] + [VM] * 10,
         [(234, 8, 128), (256, 128)], [VM] * 2,
         [(96, 8, 128), (48, 8, 128), (96, 8, 128), (48, 8, 256), (48, 8, 128), (24, 8, 128), (12, 8, 128),
-         (6, 8, 256), (3, 8, 256), (3, 8, 256), (24, 128)],
+         (6, 8, 256), (3, 8, 256), (3, 8, 256), (32, 128)],
     )
     mine = lax.all_to_all(payload, "tm", split_axis=0, concat_axis=0, tiled=True)
     theirs = lax.ppermute(mine, "chan", [(0, 1), (1, 0)])
@@ -917,10 +919,10 @@
         _back_kernel, "back", 24, (sc, mine, theirs, coarse_table, back_table, own_details, more_details, rim_details, w),
         [SM] + [VM] * 8, [(OWN, 256)], [HBM],
         [
-            (2, 2, 128, 128), (2, 32, 128), (32, 128), (3, 8, 128), (3, 8, 128),
+            (2, 264, 128), (2, 2, 144, 128), (2, 40, 128), (40, 128), (3, 8, 128), (3, 8, 128),
             (6, 8, 128), (12, 8, 128), (24, 8, 128), (48, 8, 128), (96, 8, 256),
             (6, 8, 128), (12, 8, 128), (24, 8, 128), (48, 8, 256), (96, 8, 256),
-            (8 * SEG, 128), (8 * SEG, 128), (8 * SEG, 128), (48, 8, 128), (OWN, 256), dma((8,)),
+            ROWS, ROWS, ROWS, (48, 8, 128), (OWN, 256), dma((8,)),
         ],
     )
     return out

time: 54.4 us -> 54.5 us (level)
  no operation moved by 1% of the time
where the time goes in v7:
time: 54.5 us; the launch traced here: 54.4 us
  blocking collectives  21.5 us (39%)
  Pallas kernels  16 us (29%)
  starting transfers between devices  13.8 us (25%)
  waiting for transfers between devices  2.92 us (5%)
    all_to_all x1, blocking collectives, shards(): lax.all_to_all(payload, 'tm', split_axis=0, concat_axis=0, tiled=True)  21.5 us
    pallas_call x5, Pallas kernels, _call(): pl.pallas_call(kernel, out_shape=[pltpu.HBM(s.shape, s.dtype) if spec is...  16 us
    ppermute x2, starting transfers between devices, _shift(): return lax.ppermute(v, 'tm', [(i, (i + by) % NT) for i in range(NT)])  8.65 us
    ppermute x1, starting transfers between devices, shards(): recv = lax.ppermute(record, 'chan', [(0, 1), (1, 0)])  3.24 us
    ppermute x2, waiting for transfers between devices, _shift(): return lax.ppermute(v, 'tm', [(i, (i + by) % NT) for i in range(NT)])  1.94 us
    ppermute x1, starting transfers between devices, shards(): theirs = lax.ppermute(mine, 'chan', [(0, 1), (1, 0)])  1.92 us
  transfers between devices with their start and end apart: 4, of which 2 were waited for; matrix products, arithmetic and copies ran while one was open for 0% of the time, Pallas kernels for 10%

profile of v7, /device:TPU:1, one launch (start us, length us, event | category | flops | bytes accessed | tf_op | source)
XLA Modules:
  0.0 54.4 jit_solution(6089088214164660478)
XLA Ops:
  0.0 3.2 %collective-permute-start = (f32[1024,256]{1,0:T(8,128)}, f32[1024,256]{1,0:T(8,128)S(1)}, u32[]{:S(2)}, u32[]{:S(2)}) collective-permute-start(f32[1024,256]{1,0:T(8,128)} %x_all.1), channel_id=1, source_target_pairs={{0,1},{1,0},{2,3},{3,2},{4,5},{5,4},{6,7},{7,6},{8,9},{9,8},{10,11... | collective-permute-start | bytes 3145736 | tf_op jit(solution)/shard_map/ppermute | solution.py:886
  3.2 0.1 pad_add_fusion.sc
  3.3 2.8 %load.1 = (f32[1024,128]{1,0:T(8,128)S(1)}, f32[1024,128]{1,0:T(8,128)S(1)}, f32[1024,128]{1,0:T(8,128)S(1)}, bf16[2,384,256]{2,1,0:T(8,128)(2,1)S(1)}, f32[6,3,8,128]{3,2,1,0:T(8,128)S(1)}) custom-call(s32[3]{0:T(128)S(1)} %pad_add_fusion.sc, f32[1024,256]{1,0:T(8,128)} %x_all.1, f32[6,8]{1,0:T(8,128)} %gauge_table_all.1, s32[6,32]{1,0:T(8,128)} %gauge_index_all.1, ...), custom_call_target="tpu_custom_call" | custom-call | tf_op jit(solution)/shard_map/load/pallas_call | solution.py:864
  6.1 0.0 collective-permute-done.recv
  6.1 2.1 %own.1 = (f32[42,8,128]{2,1,0:T(8,128)S(1)}, f32[42,8,128]{2,1,0:T(8,128)S(1)}, f32[96,8,128]{2,1,0:T(8,128)S(1)}, f32[48,8,128]{2,1,0:T(8,128)S(1)}, f32[1728,1...) custom-call(s32[3]{0:T(128)S(1)} %pad_add_fusion.sc, ...), custom_call_target="tpu_custom_call" | custom-call | tf_op jit(solution)/shard_map/own/pallas_call | solution.py:864
  8.3 0.1 collective-permute-start.1
  8.4 8.6 %collective-permute-start.2 = (f32[42,8,128]{2,1,0:T(8,128)S(1)}, f32[42,8,128]{2,1,0:T(8,128)S(1)}, u32[]{:S(2)}, u32[]{:S(2)}) collective-permute-start(f32[42,8,128]{2,1,0:T(8,128)S(1)} %get-tuple-element.30.left), channel_id=1, source_target_pairs={{0,254},{2,0},{4,2},{6,4},{8,6},{10,8},{12,10},{14,12},{16,14},{18... | collective-permute-start | bytes 516104 | tf_op jit(solution)/shard_map/ppermute | solution.py:876
  16.9 2.7 %aside.1 = (bf16[2,896,512]{2,1,0:T(8,128)(2,1)S(1)}, bf16[2,896,256]{2,1,0:T(8,128)(2,1)S(1)}, bf16[2,640,512]{2,1,0:T(8,128)(2,1)S(1)}, f32[192,8,128]{2,1,0:T(8,128)S(1)}, f32[8,128]{1,0:T(8,128)S(1)}) custom-call(s32[3]{0:T(128)S(1)} %pad_add_fusion.sc, f32[1728,128]{1,0:T(8,128)S(1)} %get-tuple-element.34.fh, f32[6,3,8,128]{3,2,1,0:T(8,128)S(1)} %get-tuple-element.28.w, ...), custom_call_target="tpu_custom_call" | custom-call | tf_op jit(solution)/shard_map/aside/pallas_call | solution.py:864
  19.7 1.9 %collective-permute-done.1.from_left = f32[42,8,128]{2,1,0:T(8,128)S(1)} collective-permute-done((f32[42,8,128]{2,1,0:T(8,128)S(1)}, f32[42,8,128]{2,1,0:T(8,128)S(1)}, u32[]{:S(2)}, u32[]{:S(2)}) %collective-permute-start.1) | collective-permute-done | bytes 172064 | tf_op jit(solution)/shard_map/ppermute | solution.py:876
  21.6 0.0 collective-permute-done.2.from_right
  21.6 2.7 %rim.1 = (f32[234,8,128]{2,1,0:T(8,128)S(1)}, f32[256,128]{1,0:T(8,128)S(1)}) custom-call(s32[3]{0:T(128)S(1)} %pad_add_fusion.sc, f32[42,8,128]{2,1,0:T(8,128)S(1)} %get-tuple-element.29.right, f32[42,8,128]{2,1,0:T(8,128)S(1)} %get-tuple-element.30.left, f32[42,8,128]{2,1,0:T(8,128)S(1)} %collective-permute-done.1.from_left, ...), custom_call_target="tpu_custom_call" | custom-call | tf_op jit(solution)/shard_map/rim/pallas_call | solution.py:864
  24.3 21.5 %all_to_all.11 = f32[128,2,128]{2,1,0:T(2,128)S(1)} all-to-all(f32[128,2,128]{2,1,0:T(2,128)S(1)} %bitcast.7), channel_id=1, replica_groups=mesh['tm'=128,'chan'=2] {'tm'}, dimensions={0} | all-to-all | bytes 262144 | tf_op jit(solution)/shard_map/all_to_all | solution.py:916
  45.8 1.9 %collective-permute-start.3 = (f32[256,128]{1,0:T(8,128)S(1)}, f32[256,128]{1,0:T(8,128)S(1)}, u32[]{:S(2)}, u32[]{:S(2)}) collective-permute-start(f32[256,128]{1,0:T(8,128)S(1)} %bitcast.5), channel_id=1, source_target_pairs={{0,1},{1,0},{2,3},{3,2},{4,5},{5,4},{6,7},{7,6},{8,9},{9,8},{10,11... | collective-permute-start | bytes 393224 | tf_op jit(solution)/shard_map/ppermute | solution.py:917
  47.7 1.0 %collective-permute-done.3.theirs = f32[256,128]{1,0:T(8,128)S(1)} collective-permute-done((f32[256,128]{1,0:T(8,128)S(1)}, f32[256,128]{1,0:T(8,128)S(1)}, u32[]{:S(2)}, u32[]{:S(2)}) %collective-permute-start.3) | collective-permute-done | bytes 131104 | tf_op jit(solution)/shard_map/ppermute | solution.py:917
  48.7 5.7 %back.1 = f32[1024,256]{1,0:T(8,128)} custom-call(s32[3]{0:T(128)S(1)} %pad_add_fusion.sc, f32[256,128]{1,0:T(8,128)S(1)} %bitcast.6, f32[256,128]{1,0:T(8,128)S(1)} %collective-permute-done.3.theirs, bf16[2,640,512]{2,1,0:T(8,128)(2,1)S(1)} %get-tuple-element.38.coarse_table, bf16[2,896,256]{2,1,0:T(8,128)(2,1)S(1)} %get-tuple-element.39.table, ...), custom_call_target="tpu_custom_call" | custom-call | tf_op jit(solution)/shard_map/back/pallas_call | solution.py:864
Async XLA Ops:
  0.0 6.1 %collective-permute-start = (f32[1024,256]{1,0:T(8,128)}, f32[1024,256]{1,0:T(8,128)S(1)}, u32[]{:S(2)}, u32[]{:S(2)}) collective-permute-start(f32[1024,256]{1,0:T(8,128)} %x_all.1), channel_id=1, source_target_pairs={{0,1},{1,0},{2,3},{3,2},{4,5},{5,4},{6,7},{7,6},{8,9},{9,8},{10,11... | collective-permute-start | bytes 3145736 | tf_op jit(solution)/shard_map/ppermute | solution.py:886
  8.3 13.3 %collective-permute-start.1 = (f32[42,8,128]{2,1,0:T(8,128)S(1)}, f32[42,8,128]{2,1,0:T(8,128)S(1)}, u32[]{:S(2)}, u32[]{:S(2)}) collective-permute-start(f32[42,8,128]{2,1,0:T(8,128)S(1)} %get-tuple-element.29.right), channel_id=1, source_target_pairs={{0,2},{2,4},{4,6},{6,8},{8,10},{10,12},{12,14},{14,16},{16,18},{18... | collective-permute-start | bytes 516104 | tf_op jit(solution)/shard_map/ppermute | solution.py:876
  8.4 13.2 %collective-permute-start.2 = (f32[42,8,128]{2,1,0:T(8,128)S(1)}, f32[42,8,128]{2,1,0:T(8,128)S(1)}, u32[]{:S(2)}, u32[]{:S(2)}) collective-permute-start(f32[42,8,128]{2,1,0:T(8,128)S(1)} %get-tuple-element.30.left), channel_id=1, source_target_pairs={{0,254},{2,0},{4,2},{6,4},{8,6},{10,8},{12,10},{14,12},{16,14},{18... | collective-permute-start | bytes 516104 | tf_op jit(solution)/shard_map/ppermute | solution.py:876
  45.8 2.9 %collective-permute-start.3 = (f32[256,128]{1,0:T(8,128)S(1)}, f32[256,128]{1,0:T(8,128)S(1)}, u32[]{:S(2)}, u32[]{:S(2)}) collective-permute-start(f32[256,128]{1,0:T(8,128)S(1)} %bitcast.5), channel_id=1, source_target_pairs={{0,1},{1,0},{2,3},{3,2},{4,5},{5,4},{6,7},{7,6},{8,9},{9,8},{10,11... | collective-permute-start | bytes 393224 | tf_op jit(solution)/shard_map/ppermute | solution.py:917

commit v8 on v7

--- a/solution.py
+++ b/solution.py
@@ -471,9 +471,9 @@
             hit = jnp.where(block == q, weights[l : l + 1], 0.0)
             w[l, q] = jnp.broadcast_to(jnp.sum(hit, axis=1, keepdims=True), (8, 128))
     copies[2].wait()
-    for i in range(4):
-        copies[3 + i].wait()
-        _first(x, own_table, low, high, ends, 0, range(256 * i, 256 * i + 256, 128))
+    for c in copies[3:]:
+        c.wait()
+    _first(x, own_table, low, high, ends, 0, range(0, OWN, 128))
 
 
 def _first(x, table, low, high, ends, at, blocks):

time: 54.5 us -> 54.3 us (level)
  no operation moved by 1% of the time
where the time goes in v8:
time: 54.3 us; the launch traced here: 54.1 us
  blocking collectives  21.4 us (39%)
  Pallas kernels  15.8 us (29%)
  starting transfers between devices  14 us (26%)
  waiting for transfers between devices  2.81 us (5%)
    all_to_all x1, blocking collectives, shards(): lax.all_to_all(payload, 'tm', split_axis=0, concat_axis=0, tiled=True)  21.4 us
    pallas_call x5, Pallas kernels, _call(): pl.pallas_call(kernel, out_shape=[pltpu.HBM(s.shape, s.dtype) if spec is...  15.8 us
    ppermute x2, starting transfers between devices, _shift(): return lax.ppermute(v, 'tm', [(i, (i + by) % NT) for i in range(NT)])  8.65 us
    ppermute x1, starting transfers between devices, shards(): recv = lax.ppermute(record, 'chan', [(0, 1), (1, 0)])  3.24 us
    ppermute x1, starting transfers between devices, shards(): theirs = lax.ppermute(mine, 'chan', [(0, 1), (1, 0)])  2.15 us
    ppermute x2, waiting for transfers between devices, _shift(): return lax.ppermute(v, 'tm', [(i, (i + by) % NT) for i in range(NT)])  1.82 us
  transfers between devices with their start and end apart: 4, of which 2 were waited for; matrix products, arithmetic and copies ran while one was open for 0% of the time, Pallas kernels for 10%

profile of v8, /device:TPU:1, one launch (start us, length us, event | category | flops | bytes accessed | tf_op | source)
XLA Modules:
  0.0 54.1 jit_solution(7480107492192690848)
XLA Ops:
  0.0 3.2 %collective-permute-start = (f32[1024,256]{1,0:T(8,128)}, f32[1024,256]{1,0:T(8,128)S(1)}, u32[]{:S(2)}, u32[]{:S(2)}) collective-permute-start(f32[1024,256]{1,0:T(8,128)} %x_all.1), channel_id=1, source_target_pairs={{0,1},{1,0},{2,3},{3,2},{4,5},{5,4},{6,7},{7,6},{8,9},{9,8},{10,11... | collective-permute-start | bytes 3145736 | tf_op jit(solution)/shard_map/ppermute | solution.py:886
  3.2 0.1 pad_add_fusion.sc
  3.3 2.5 %load.1 = (f32[1024,128]{1,0:T(8,128)S(1)}, f32[1024,128]{1,0:T(8,128)S(1)}, f32[1024,128]{1,0:T(8,128)S(1)}, bf16[2,384,256]{2,1,0:T(8,128)(2,1)S(1)}, f32[6,3,8,128]{3,2,1,0:T(8,128)S(1)}) custom-call(s32[3]{0:T(128)S(1)} %pad_add_fusion.sc, f32[1024,256]{1,0:T(8,128)} %x_all.1, f32[6,8]{1,0:T(8,128)} %gauge_table_all.1, s32[6,32]{1,0:T(8,128)} %gauge_index_all.1, ...), custom_call_target="tpu_custom_call" | custom-call | tf_op jit(solution)/shard_map/load/pallas_call | solution.py:864
  5.9 0.0 collective-permute-done.recv
  5.9 2.1 %own.1 = (f32[42,8,128]{2,1,0:T(8,128)S(1)}, f32[42,8,128]{2,1,0:T(8,128)S(1)}, f32[96,8,128]{2,1,0:T(8,128)S(1)}, f32[48,8,128]{2,1,0:T(8,128)S(1)}, f32[1728,1...) custom-call(s32[3]{0:T(128)S(1)} %pad_add_fusion.sc, ...), custom_call_target="tpu_custom_call" | custom-call | tf_op jit(solution)/shard_map/own/pallas_call | solution.py:864
  8.0 0.1 collective-permute-start.1
  8.1 8.6 %collective-permute-start.2 = (f32[42,8,128]{2,1,0:T(8,128)S(1)}, f32[42,8,128]{2,1,0:T(8,128)S(1)}, u32[]{:S(2)}, u32[]{:S(2)}) collective-permute-start(f32[42,8,128]{2,1,0:T(8,128)S(1)} %get-tuple-element.30.left), channel_id=1, source_target_pairs={{0,254},{2,0},{4,2},{6,4},{8,6},{10,8},{12,10},{14,12},{16,14},{18... | collective-permute-start | bytes 516104 | tf_op jit(solution)/shard_map/ppermute | solution.py:876
  16.7 2.7 %aside.1 = (bf16[2,896,512]{2,1,0:T(8,128)(2,1)S(1)}, bf16[2,896,256]{2,1,0:T(8,128)(2,1)S(1)}, bf16[2,640,512]{2,1,0:T(8,128)(2,1)S(1)}, f32[192,8,128]{2,1,0:T(8,128)S(1)}, f32[8,128]{1,0:T(8,128)S(1)}) custom-call(s32[3]{0:T(128)S(1)} %pad_add_fusion.sc, f32[1728,128]{1,0:T(8,128)S(1)} %get-tuple-element.34.fh, f32[6,3,8,128]{3,2,1,0:T(8,128)S(1)} %get-tuple-element.28.w, ...), custom_call_target="tpu_custom_call" | custom-call | tf_op jit(solution)/shard_map/aside/pallas_call | solution.py:864
  19.4 1.8 %collective-permute-done.1.from_left = f32[42,8,128]{2,1,0:T(8,128)S(1)} collective-permute-done((f32[42,8,128]{2,1,0:T(8,128)S(1)}, f32[42,8,128]{2,1,0:T(8,128)S(1)}, u32[]{:S(2)}, u32[]{:S(2)}) %collective-permute-start.1) | collective-permute-done | bytes 172064 | tf_op jit(solution)/shard_map/ppermute | solution.py:876
  21.2 0.0 collective-permute-done.2.from_right
  21.2 2.7 %rim.1 = (f32[234,8,128]{2,1,0:T(8,128)S(1)}, f32[256,128]{1,0:T(8,128)S(1)}) custom-call(s32[3]{0:T(128)S(1)} %pad_add_fusion.sc, f32[42,8,128]{2,1,0:T(8,128)S(1)} %get-tuple-element.29.right, f32[42,8,128]{2,1,0:T(8,128)S(1)} %get-tuple-element.30.left, f32[42,8,128]{2,1,0:T(8,128)S(1)} %collective-permute-done.1.from_left, ...), custom_call_target="tpu_custom_call" | custom-call | tf_op jit(solution)/shard_map/rim/pallas_call | solution.py:864
  23.9 21.4 %all_to_all.11 = f32[128,2,128]{2,1,0:T(2,128)S(1)} all-to-all(f32[128,2,128]{2,1,0:T(2,128)S(1)} %bitcast.7), channel_id=1, replica_groups=mesh['tm'=128,'chan'=2] {'tm'}, dimensions={0} | all-to-all | bytes 262144 | tf_op jit(solution)/shard_map/all_to_all | solution.py:916
  45.3 2.1 %collective-permute-start.3 = (f32[256,128]{1,0:T(8,128)S(1)}, f32[256,128]{1,0:T(8,128)S(1)}, u32[]{:S(2)}, u32[]{:S(2)}) collective-permute-start(f32[256,128]{1,0:T(8,128)S(1)} %bitcast.5), channel_id=1, source_target_pairs={{0,1},{1,0},{2,3},{3,2},{4,5},{5,4},{6,7},{7,6},{8,9},{9,8},{10,11... | collective-permute-start | bytes 393224 | tf_op jit(solution)/shard_map/ppermute | solution.py:917
  47.5 1.0 %collective-permute-done.3.theirs = f32[256,128]{1,0:T(8,128)S(1)} collective-permute-done((f32[256,128]{1,0:T(8,128)S(1)}, f32[256,128]{1,0:T(8,128)S(1)}, u32[]{:S(2)}, u32[]{:S(2)}) %collective-permute-start.3) | collective-permute-done | bytes 131104 | tf_op jit(solution)/shard_map/ppermute | solution.py:917
  48.4 5.7 %back.1 = f32[1024,256]{1,0:T(8,128)} custom-call(s32[3]{0:T(128)S(1)} %pad_add_fusion.sc, f32[256,128]{1,0:T(8,128)S(1)} %bitcast.6, f32[256,128]{1,0:T(8,128)S(1)} %collective-permute-done.3.theirs, bf16[2,640,512]{2,1,0:T(8,128)(2,1)S(1)} %get-tuple-element.38.coarse_table, bf16[2,896,256]{2,1,0:T(8,128)(2,1)S(1)} %get-tuple-element.39.table, ...), custom_call_target="tpu_custom_call" | custom-call | tf_op jit(solution)/shard_map/back/pallas_call | solution.py:864
Async XLA Ops:
  0.0 5.9 %collective-permute-start = (f32[1024,256]{1,0:T(8,128)}, f32[1024,256]{1,0:T(8,128)S(1)}, u32[]{:S(2)}, u32[]{:S(2)}) collective-permute-start(f32[1024,256]{1,0:T(8,128)} %x_all.1), channel_id=1, source_target_pairs={{0,1},{1,0},{2,3},{3,2},{4,5},{5,4},{6,7},{7,6},{8,9},{9,8},{10,11... | collective-permute-start | bytes 3145736 | tf_op jit(solution)/shard_map/ppermute | solution.py:886
  8.0 13.2 %collective-permute-start.1 = (f32[42,8,128]{2,1,0:T(8,128)S(1)}, f32[42,8,128]{2,1,0:T(8,128)S(1)}, u32[]{:S(2)}, u32[]{:S(2)}) collective-permute-start(f32[42,8,128]{2,1,0:T(8,128)S(1)} %get-tuple-element.29.right), channel_id=1, source_target_pairs={{0,2},{2,4},{4,6},{6,8},{8,10},{10,12},{12,14},{14,16},{16,18},{18... | collective-permute-start | bytes 516104 | tf_op jit(solution)/shard_map/ppermute | solution.py:876
  8.1 13.1 %collective-permute-start.2 = (f32[42,8,128]{2,1,0:T(8,128)S(1)}, f32[42,8,128]{2,1,0:T(8,128)S(1)}, u32[]{:S(2)}, u32[]{:S(2)}) collective-permute-start(f32[42,8,128]{2,1,0:T(8,128)S(1)} %get-tuple-element.30.left), channel_id=1, source_target_pairs={{0,254},{2,0},{4,2},{6,4},{8,6},{10,8},{12,10},{14,12},{16,14},{18... | collective-permute-start | bytes 516104 | tf_op jit(solution)/shard_map/ppermute | solution.py:876
  45.3 3.1 %collective-permute-start.3 = (f32[256,128]{1,0:T(8,128)S(1)}, f32[256,128]{1,0:T(8,128)S(1)}, u32[]{:S(2)}, u32[]{:S(2)}) collective-permute-start(f32[256,128]{1,0:T(8,128)S(1)} %bitcast.5), channel_id=1, source_target_pairs={{0,1},{1,0},{2,3},{3,2},{4,5},{5,4},{6,7},{7,6},{8,9},{9,8},{10,11... | collective-permute-start | bytes 393224 | tf_op jit(solution)/shard_map/ppermute | solution.py:917

commit v9 on v8

--- a/solution.py
+++ b/solution.py
@@ -100,7 +100,7 @@
 OWN_HIGH0 = _run(2, 126, 130)
 RIM_LOW0 = {**_run(-2, 2, 0), **_run(126, 130, 4)}
 RIM_HIGH0 = {**_run(-2, 2, 8), **_run(126, 130, 12)}
-RIM_IN0 = {**_run(-8, 0, 0), **_run(0, 8, 128), **_run(248, 256, 256), **_run(256, 264, 384)}
+RIM_IN0 = {**_run(-8, 0, 120), **_run(0, 8, 128), **_run(248, 256, 376), **_run(256, 264, 384)}
 OWN_LOW1 = _run(3, 61, 3)
 OWN_HIGH1 = _run(2, 61, 66)
 RIM_LOW1 = {**_run(-3, 3, 64), **_run(61, 67, 70)}
@@ -156,7 +156,8 @@
         sixteen = np.concatenate([lows, highs[:, 1:], lows[:, 1:], highs[:, 1:], np.zeros((128, 3))], axis=1)
         t5[:, 128:] = np.tile(sixteen, (1, 8))
         one = fw(RIM_IN0, RIM_LOW0, RIM_HIGH0, 512, 128, a[0], b[0], 1.0)
-        rim0 = [sum(np.roll(one, (8 * (4 * g + h), 32 * g), (0, 1)) for g in range(4)) for h in range(4)]
+        one = one.reshape(4, 128, 128)
+        rim0 = [sum(np.roll(one, (8 * (4 * g + h), 32 * g), (1, 2)) for g in range(4)).reshape(512, 128) for h in range(4)]
         rim.append(
             _bundle(
                 (
@@ -506,10 +507,9 @@
         to_right, to_left = None, None
         for g in range(16):
             v = fe[pl.ds(12 * g + i, 8, stride=SEG), :]
-            a = pltpu.roll(v, 8 * g, 1) if g else v
-            b = pltpu.roll(v, (8 * g + 8) % 128, 1) if g != 15 else v
-            to_left = a if to_left is None else jnp.where(group == g, a, to_left)
-            to_right = b if to_right is None else jnp.where(group == g, b, to_right)
+            v = pltpu.roll(v, 8 * g, 1) if g else v
+            to_left = v if to_left is None else jnp.where(group == g, v, to_left)
+            to_right = v if to_right is None else jnp.where(group == (g + 15) % 16, v, to_right)
         right[i] = to_right
         left[i] = to_left
     rows = _own_rows(core)

time: 54.3 us -> 54.3 us (level)
  no operation moved by 1% of the time
where the time goes in v9:
time: 54.3 us; the launch traced here: 54.2 us
  blocking collectives  21.4 us (39%)
  Pallas kernels  15.8 us (29%)
  starting transfers between devices  14 us (26%)
  waiting for transfers between devices  2.8 us (5%)
    all_to_all x1, blocking collectives, shards(): lax.all_to_all(payload, 'tm', split_axis=0, concat_axis=0, tiled=True)  21.4 us
    pallas_call x5, Pallas kernels, _call(): pl.pallas_call(kernel, out_shape=[pltpu.HBM(s.shape, s.dtype) if spec is...  15.8 us
    ppermute x2, starting transfers between devices, _shift(): return lax.ppermute(v, 'tm', [(i, (i + by) % NT) for i in range(NT)])  8.65 us
    ppermute x1, starting transfers between devices, shards(): recv = lax.ppermute(record, 'chan', [(0, 1), (1, 0)])  3.24 us
    ppermute x1, starting transfers between devices, shards(): theirs = lax.ppermute(mine, 'chan', [(0, 1), (1, 0)])  2.15 us
    ppermute x2, waiting for transfers between devices, _shift(): return lax.ppermute(v, 'tm', [(i, (i + by) % NT) for i in range(NT)])  1.81 us
  transfers between devices with their start and end apart: 4, of which 2 were waited for; matrix products, arithmetic and copies ran while one was open for 0% of the time, Pallas kernels for 10%

profile of v9, /device:TPU:1, one launch (start us, length us, event | category | flops | bytes accessed | tf_op | source)
XLA Modules:
  0.0 54.2 jit_solution(9804018053185748004)
XLA Ops:
  0.0 3.2 %collective-permute-start = (f32[1024,256]{1,0:T(8,128)}, f32[1024,256]{1,0:T(8,128)S(1)}, u32[]{:S(2)}, u32[]{:S(2)}) collective-permute-start(f32[1024,256]{1,0:T(8,128)} %x_all.1), channel_id=1, source_target_pairs={{0,1},{1,0},{2,3},{3,2},{4,5},{5,4},{6,7},{7,6},{8,9},{9,8},{10,11... | collective-permute-start | bytes 3145736 | tf_op jit(solution)/shard_map/ppermute | solution.py:886
  3.2 0.1 pad_add_fusion.sc
  3.3 2.5 %load.1 = (f32[1024,128]{1,0:T(8,128)S(1)}, f32[1024,128]{1,0:T(8,128)S(1)}, f32[1024,128]{1,0:T(8,128)S(1)}, bf16[2,384,256]{2,1,0:T(8,128)(2,1)S(1)}, f32[6,3,8,128]{3,2,1,0:T(8,128)S(1)}) custom-call(s32[3]{0:T(128)S(1)} %pad_add_fusion.sc, f32[1024,256]{1,0:T(8,128)} %x_all.1, f32[6,8]{1,0:T(8,128)} %gauge_table_all.1, s32[6,32]{1,0:T(8,128)} %gauge_index_all.1, ...), custom_call_target="tpu_custom_call" | custom-call | tf_op jit(solution)/shard_map/load/pallas_call | solution.py:864
  5.9 0.0 collective-permute-done.recv
  5.9 2.2 %own.1 = (f32[42,8,128]{2,1,0:T(8,128)S(1)}, f32[42,8,128]{2,1,0:T(8,128)S(1)}, f32[96,8,128]{2,1,0:T(8,128)S(1)}, f32[48,8,128]{2,1,0:T(8,128)S(1)}, f32[1728,1...) custom-call(s32[3]{0:T(128)S(1)} %pad_add_fusion.sc, ...), custom_call_target="tpu_custom_call" | custom-call | tf_op jit(solution)/shard_map/own/pallas_call | solution.py:864
  8.1 0.1 collective-permute-start.1
  8.2 8.6 %collective-permute-start.2 = (f32[42,8,128]{2,1,0:T(8,128)S(1)}, f32[42,8,128]{2,1,0:T(8,128)S(1)}, u32[]{:S(2)}, u32[]{:S(2)}) collective-permute-start(f32[42,8,128]{2,1,0:T(8,128)S(1)} %get-tuple-element.30.left), channel_id=1, source_target_pairs={{0,254},{2,0},{4,2},{6,4},{8,6},{10,8},{12,10},{14,12},{16,14},{18... | collective-permute-start | bytes 516104 | tf_op jit(solution)/shard_map/ppermute | solution.py:876
  16.7 2.7 %aside.1 = (bf16[2,896,512]{2,1,0:T(8,128)(2,1)S(1)}, bf16[2,896,256]{2,1,0:T(8,128)(2,1)S(1)}, bf16[2,640,512]{2,1,0:T(8,128)(2,1)S(1)}, f32[192,8,128]{2,1,0:T(8,128)S(1)}, f32[8,128]{1,0:T(8,128)S(1)}) custom-call(s32[3]{0:T(128)S(1)} %pad_add_fusion.sc, f32[1728,128]{1,0:T(8,128)S(1)} %get-tuple-element.34.fh, f32[6,3,8,128]{3,2,1,0:T(8,128)S(1)} %get-tuple-element.28.w, ...), custom_call_target="tpu_custom_call" | custom-call | tf_op jit(solution)/shard_map/aside/pallas_call | solution.py:864
  19.5 1.8 %collective-permute-done.1.from_left = f32[42,8,128]{2,1,0:T(8,128)S(1)} collective-permute-done((f32[42,8,128]{2,1,0:T(8,128)S(1)}, f32[42,8,128]{2,1,0:T(8,128)S(1)}, u32[]{:S(2)}, u32[]{:S(2)}) %collective-permute-start.1) | collective-permute-done | bytes 172064 | tf_op jit(solution)/shard_map/ppermute | solution.py:876
  21.3 0.0 collective-permute-done.2.from_right
  21.3 2.7 %rim.1 = (f32[234,8,128]{2,1,0:T(8,128)S(1)}, f32[256,128]{1,0:T(8,128)S(1)}) custom-call(s32[3]{0:T(128)S(1)} %pad_add_fusion.sc, f32[42,8,128]{2,1,0:T(8,128)S(1)} %get-tuple-element.29.right, f32[42,8,128]{2,1,0:T(8,128)S(1)} %get-tuple-element.30.left, f32[42,8,128]{2,1,0:T(8,128)S(1)} %collective-permute-done.1.from_left, ...), custom_call_target="tpu_custom_call" | custom-call | tf_op jit(solution)/shard_map/rim/pallas_call | solution.py:864
  24.0 21.4 %all_to_all.11 = f32[128,2,128]{2,1,0:T(2,128)S(1)} all-to-all(f32[128,2,128]{2,1,0:T(2,128)S(1)} %bitcast.7), channel_id=1, replica_groups=mesh['tm'=128,'chan'=2] {'tm'}, dimensions={0} | all-to-all | bytes 262144 | tf_op jit(solution)/shard_map/all_to_all | solution.py:916
  45.4 2.2 %collective-permute-start.3 = (f32[256,128]{1,0:T(8,128)S(1)}, f32[256,128]{1,0:T(8,128)S(1)}, u32[]{:S(2)}, u32[]{:S(2)}) collective-permute-start(f32[256,128]{1,0:T(8,128)S(1)} %bitcast.5), channel_id=1, source_target_pairs={{0,1},{1,0},{2,3},{3,2},{4,5},{5,4},{6,7},{7,6},{8,9},{9,8},{10,11... | collective-permute-start | bytes 393224 | tf_op jit(solution)/shard_map/ppermute | solution.py:917
  47.5 1.0 %collective-permute-done.3.theirs = f32[256,128]{1,0:T(8,128)S(1)} collective-permute-done((f32[256,128]{1,0:T(8,128)S(1)}, f32[256,128]{1,0:T(8,128)S(1)}, u32[]{:S(2)}, u32[]{:S(2)}) %collective-permute-start.3) | collective-permute-done | bytes 131104 | tf_op jit(solution)/shard_map/ppermute | solution.py:917
  48.5 5.7 %back.1 = f32[1024,256]{1,0:T(8,128)} custom-call(s32[3]{0:T(128)S(1)} %pad_add_fusion.sc, f32[256,128]{1,0:T(8,128)S(1)} %bitcast.6, f32[256,128]{1,0:T(8,128)S(1)} %collective-permute-done.3.theirs, bf16[2,640,512]{2,1,0:T(8,128)(2,1)S(1)} %get-tuple-element.38.coarse_table, bf16[2,896,256]{2,1,0:T(8,128)(2,1)S(1)} %get-tuple-element.39.table, ...), custom_call_target="tpu_custom_call" | custom-call | tf_op jit(solution)/shard_map/back/pallas_call | solution.py:864
Async XLA Ops:
  0.0 5.9 %collective-permute-start = (f32[1024,256]{1,0:T(8,128)}, f32[1024,256]{1,0:T(8,128)S(1)}, u32[]{:S(2)}, u32[]{:S(2)}) collective-permute-start(f32[1024,256]{1,0:T(8,128)} %x_all.1), channel_id=1, source_target_pairs={{0,1},{1,0},{2,3},{3,2},{4,5},{5,4},{6,7},{7,6},{8,9},{9,8},{10,11... | collective-permute-start | bytes 3145736 | tf_op jit(solution)/shard_map/ppermute | solution.py:886
  8.1 13.2 %collective-permute-start.1 = (f32[42,8,128]{2,1,0:T(8,128)S(1)}, f32[42,8,128]{2,1,0:T(8,128)S(1)}, u32[]{:S(2)}, u32[]{:S(2)}) collective-permute-start(f32[42,8,128]{2,1,0:T(8,128)S(1)} %get-tuple-element.29.right), channel_id=1, source_target_pairs={{0,2},{2,4},{4,6},{6,8},{8,10},{10,12},{12,14},{14,16},{16,18},{18... | collective-permute-start | bytes 516104 | tf_op jit(solution)/shard_map/ppermute | solution.py:876
  8.2 13.1 %collective-permute-start.2 = (f32[42,8,128]{2,1,0:T(8,128)S(1)}, f32[42,8,128]{2,1,0:T(8,128)S(1)}, u32[]{:S(2)}, u32[]{:S(2)}) collective-permute-start(f32[42,8,128]{2,1,0:T(8,128)S(1)} %get-tuple-element.30.left), channel_id=1, source_target_pairs={{0,254},{2,0},{4,2},{6,4},{8,6},{10,8},{12,10},{14,12},{16,14},{18... | collective-permute-start | bytes 516104 | tf_op jit(solution)/shard_map/ppermute | solution.py:876
  45.4 3.1 %collective-permute-start.3 = (f32[256,128]{1,0:T(8,128)S(1)}, f32[256,128]{1,0:T(8,128)S(1)}, u32[]{:S(2)}, u32[]{:S(2)}) collective-permute-start(f32[256,128]{1,0:T(8,128)S(1)} %bitcast.5), channel_id=1, source_target_pairs={{0,1},{1,0},{2,3},{3,2},{4,5},{5,4},{6,7},{7,6},{8,9},{9,8},{10,11... | collective-permute-start | bytes 393224 | tf_op jit(solution)/shard_map/ppermute | solution.py:917
